TPU v7x, 32 devices: a whole 2x2x4 slice. The times are simulated.
32 devices in a mesh: grp: 2 (over y), row: 4 (over z), feat: 4 (over x, core).
Axes of the slice: x: 2, y: 2, z: 4, core: 2. Of those that a mesh axis runs over, the one named last changes fastest.
Arguments:
- queries: float32 [512, 8192], P('row', 'feat'), may hold values from -0.0625 to 0.0625
- train_rows: float32 [832, 8192], P(('grp', 'row'), 'feat'), parts along dimension 0, may hold values from -6 to 6
- inv_gram: float32 [16, 512, 512], P('feat')
Outputs:
- scores: float32 [512, 832], P('row', ('grp', 'feat')), parts along dimension 1
There are 2 independent parts, one for each index of `grp`. A program takes and returns all parts, laid end to end along the dimension named above; an argument that names none is the same for every part. Nothing has to cross between parts.
All inputs are finite; a program needn't handle non-finite values.
Results may differ from a plain program's by a relative error of at most 0.000082.
Values sent between devices are 32-bit elements; how exact they have to be, the bound alone decides.
No kernel may reach another device: no remote copies, remote signals or barrier semaphores. Data moves between devices by JAX's collectives and lax.ppermute only.
A program may use at most 64 MiB of HBM per device.

v0:
```python
import jax
import jax.numpy as jnp
from jax import lax
from jax.sharding import PartitionSpec as P


def shifted(array, axis, by):
    devices = lax.axis_size(axis)
    return lax.ppermute(array, axis, [(i, (i + by) % devices) for i in range(devices)])


def block_scores(left, right):
    return jnp.dot(
        left, right.T, precision=lax.Precision.HIGHEST, preferred_element_type=jnp.float32
    )


def place(buffer, values, source):
    return lax.dynamic_update_slice(
        buffer, values[:, None, :], (jnp.int32(0), source, jnp.int32(0))
    )


def rotate(moving, compute, buffer):
    nring = lax.axis_size("row")
    myself = lax.axis_index("row")
    buffer = compute(buffer, moving, myself)
    half = nring // 2

    def step_both(turn, carry):
        ahead, behind, acc = carry
        ahead = shifted(ahead, "row", 1)
        behind = shifted(behind, "row", -1)
        acc = compute(acc, ahead, (myself - turn) % nring)
        acc = compute(acc, behind, (myself + turn) % nring)
        return (ahead, behind, acc)

    ahead, behind, buffer = lax.fori_loop(1, half, step_both, (moving, moving, buffer))
    ahead = shifted(ahead, "row", 1)
    buffer = compute(buffer, ahead, (myself - half) % nring)
    return buffer


def shards(queries, train_rows, inv_gram):
    qrows, fshard = queries.shape
    nblocks, modsize = (inv_gram.shape[0], inv_gram.shape[1])
    trows = train_rows.shape[0]
    blocks = queries.reshape(qrows, nblocks, modsize)
    conditioned = jnp.einsum("qbi,bij->qbj", blocks, inv_gram, precision=lax.Precision.HIGHEST)
    conditioned = conditioned.reshape(qrows, fshard)
    nring = lax.axis_size("row")
    buffer = jnp.zeros((qrows, nring, trows), jnp.float32)

    def by_train(acc, block, source):
        return place(acc, block_scores(conditioned, block), source)

    buffer = rotate(train_rows, by_train, buffer)
    partial_scores = buffer.reshape(qrows, nring * trows)
    return lax.psum_scatter(partial_scores, "feat", scatter_dimension=1, tiled=True)


def solution(mesh):
    return jax.shard_map(
        shards,
        mesh=mesh,
        in_specs=(P("row", "feat"), P(("grp", "row"), "feat"), P("feat", None, None)),
        out_specs=P("row", ("grp", "feat")),
        check_vma=False,
    )
```

profile of v0, /device:TPU:0, one launch (start us, length us, event | category | flops | bytes accessed | tf_op | source)
XLA Modules:
  0.0 96.5 jit_solution(3766652897814166657)
XLA Ops:
  6.5 0.0 copy-start
  6.5 0.0 reduce-scatter.4.cloned.1.call-start
  6.5 3.0 %collective-permute-start = (f32[104,2048]{1,0:T(8,128)}, f32[104,2048]{1,0:T(8,128)S(1)}, u32[]{:S(2)}, u32[]{:S(2)}) collective-permute-start(f32[104,2048]{1,0:T(8,128)} %param.4), channel_id=1, source_target_pairs={{0,4},{4,8},{8,12},{12,0},{1,5},{5,9},{9,13},{13,1},{2,6},{6,10},{... | collective-permute-start | bytes 2555912 | tf_op jit(solution)/shard_map/while/body/eval_jaxpr/ppermute | solution.py:9
  9.6 2.0 %collective-permute-start.1 = (f32[104,2048]{1,0:T(8,128)}, f32[104,2048]{1,0:T(8,128)}, u32[]{:S(2)}, u32[]{:S(2)}) collective-permute-start(f32[104,2048]{1,0:T(8,128)} %param.4), channel_id=1, source_target_pairs={{0,12},{4,0},{8,4},{12,8},{1,13},{5,1},{9,5},{13,9},{2,14},{6,2},{... | collective-permute-start | bytes 2555912 | tf_op jit(solution)/shard_map/while/body/eval_jaxpr/ppermute | solution.py:9
  11.6 20.1 %collective-permute-done = f32[104,2048]{1,0:T(8,128)S(1)} collective-permute-done((f32[104,2048]{1,0:T(8,128)}, f32[104,2048]{1,0:T(8,128)S(1)}, u32[]{:S(2)}, u32[]{:S(2)}) %collective-permute-start) | collective-permute-done | bytes 852000 | tf_op jit(solution)/shard_map/while/body/eval_jaxpr/ppermute | solution.py:9
  31.7 0.0 collective-permute-start.2
  31.7 8.8 %fusion.4 = f32[4,512,128]{2,1,0:T(8,128)S(1)} fusion(f32[4,512,512]{2,1,0:T(8,128)} %param.5, f32[16,4,8,512]{3,2,1,0:T(8,128)} %bitcast.38), kind=kOutput, calls=%fused_computation.8 | convolution fusion | flops 1610612736 | bytes 6291456 | tf_op jit(solution)/shard_map/qbi,bij->qbj/dot_general | solution.py:49
  40.6 0.0 copy-done
  40.6 1.1 %fusion.3 = f32[128,4,104]{0,2,1:T(8,128)S(1)} fusion(f32[128,4,104]{0,2,1:T(8,128)S(1)} %broadcast_in_dim.17, s32[]{:T(128)S(6)} %select_n.32, f32[128,2048]{0,1:T(8,128)S(1)} %bitcast.34, f32[104,2048]{1,0:T(8,128)S(1)} %copy-done), kind=kOutput, calls=%fused_computation.7 | convolution fusion | flops 327155712 | bytes 1953796 | tf_op jit(solution)/shard_map/dot_general | solution.py:13
  41.7 1.1 %fusion.2 = f32[128,4,104]{0,2,1:T(8,128)S(1)} fusion(f32[128,4,104]{0,2,1:T(8,128)S(1)} %fusion.3, s32[]{:T(128)S(6)} %select_n.34, f32[128,2048]{0,1:T(8,128)S(1)} %bitcast.35, f32[104,2048]{1,0:T(8,128)S(1)} %collective-permute-done), kind=kOutput, calls=%fused_computation.5 | convolution fusion | flops 327155712 | bytes 1953796 | tf_op jit(solution)/shard_map/while/body/eval_jaxpr/dot_general | solution.py:13
  42.7 6.0 %collective-permute-done.1 = f32[104,2048]{1,0:T(8,128)} collective-permute-done((f32[104,2048]{1,0:T(8,128)}, f32[104,2048]{1,0:T(8,128)}, u32[]{:S(2)}, u32[]{:S(2)}) %collective-permute-start.1) | collective-permute-done | bytes 852000 | tf_op jit(solution)/shard_map/while/body/eval_jaxpr/ppermute | solution.py:9
  48.7 2.2 %fusion.1 = f32[128,4,104]{0,2,1:T(8,128)S(1)} fusion(f32[128,4,104]{0,2,1:T(8,128)S(1)} %fusion.2, s32[]{:T(128)S(6)} %select_n.36, f32[128,2048]{0,1:T(8,128)S(1)} %bitcast.36, f32[104,2048]{1,0:T(8,128)} %collective-permute-done.1), kind=kOutput, calls=%fused_computation.3 | convolution fusion | flops 327155712 | bytes 1953796 | tf_op jit(solution)/shard_map/while/body/eval_jaxpr/dot_general | solution.py:13
  50.9 16.6 %collective-permute-done.2 = f32[104,2048]{1,0:T(8,128)} collective-permute-done((f32[104,2048]{1,0:T(8,128)S(1)}, f32[104,2048]{1,0:T(8,128)}, u32[]{:S(2)}, u32[]{:S(2)}) %collective-permute-start.2) | collective-permute-done | bytes 852000 | tf_op jit(solution)/shard_map/ppermute | solution.py:9
  67.5 2.2 %fusion = f32[128,4,104]{0,2,1:T(8,128)S(1)} fusion(f32[128,4,104]{0,2,1:T(8,128)S(1)} %fusion.1, s32[]{:T(128)S(6)} %select_n.38, f32[128,2048]{0,1:T(8,128)S(1)} %bitcast.37, f32[104,2048]{1,0:T(8,128)} %collective-permute-done.2), kind=kOutput, calls=%fused_computation.1 | convolution fusion | flops 327155712 | bytes 1953796 | tf_op jit(solution)/shard_map/dot_general | solution.py:13
  69.7 0.0 copy-start.1
  69.7 0.7 copy-done.1
  70.3 0.0 reduce-scatter.4.cloned.1.call-update
  70.4 19.2 %reduce-scatter.4.cloned.1.call-done = f32[128,104]{0,1:T(8,128)} async-done(((f32[128,416]{0,1:T(8,128)}), f32[128,104]{0,1:T(8,128)}) %reduce-scatter.4.cloned.1.call-update) | async-done | bytes 53264
  (1 shorter events, 0.0 us)
Async XLA Ops:
  6.5 34.1 %copy-start = (f32[104,2048]{1,0:T(8,128)S(1)}, f32[104,2048]{1,0:T(8,128)}, u32[]{:S(2)}) copy-start(f32[104,2048]{1,0:T(8,128)} %param.4) | copy-start | bytes 2555908
  6.5 83.1 %reduce-scatter.4.cloned.1.call-start = ((), (), s32[]{:S(2)}) async-start(), calls=%async_computation.1 | async-start | bytes 266240
  6.5 25.1 %collective-permute-start = (f32[104,2048]{1,0:T(8,128)}, f32[104,2048]{1,0:T(8,128)S(1)}, u32[]{:S(2)}, u32[]{:S(2)}) collective-permute-start(f32[104,2048]{1,0:T(8,128)} %param.4), channel_id=1, source_target_pairs={{0,4},{4,8},{8,12},{12,0},{1,5},{5,9},{9,13},{13,1},{2,6},{6,10},{... | collective-permute-start | bytes 2555912 | tf_op jit(solution)/shard_map/while/body/eval_jaxpr/ppermute | solution.py:9
  9.6 39.1 %collective-permute-start.1 = (f32[104,2048]{1,0:T(8,128)}, f32[104,2048]{1,0:T(8,128)}, u32[]{:S(2)}, u32[]{:S(2)}) collective-permute-start(f32[104,2048]{1,0:T(8,128)} %param.4), channel_id=1, source_target_pairs={{0,12},{4,0},{8,4},{12,8},{1,13},{5,1},{9,5},{13,9},{2,14},{6,2},{... | collective-permute-start | bytes 2555912 | tf_op jit(solution)/shard_map/while/body/eval_jaxpr/ppermute | solution.py:9
  31.7 35.8 %collective-permute-start.2 = (f32[104,2048]{1,0:T(8,128)S(1)}, f32[104,2048]{1,0:T(8,128)}, u32[]{:S(2)}, u32[]{:S(2)}) collective-permute-start(f32[104,2048]{1,0:T(8,128)S(1)} %collective-permute-done), channel_id=1, source_target_pairs={{0,4},{4,8},{8,12},{12,0},{1,5},{5,9},{9,13},{13,1},{2,6},{6,10},{... | collective-permute-start | bytes 2555912 | tf_op jit(solution)/shard_map/ppermute | solution.py:9
  69.7 0.7 copy-start.1
Sparse Core Ops, SparseCore 0:
  70.5 19.0 reduce-scatter.3
where the time goes:
time: 96.6 us; the launch traced here: 96.5 us
  waiting for transfers between devices  61.9 us (64%)
  matrix products  15.3 us (16%)
  between operations  13.5 us (14%)
  starting transfers between devices  5.06 us (5%)
    ppermute x3, waiting for transfers between devices, shifted(): lax.ppermute(array, axis, [(i, (i + by) % devices) for i in range(devices)])  42.6 us
    unnamed x2, waiting for transfers between devices  19.3 us
    dot_general x1, matrix products, shards(): jnp.einsum('qbi,bij->qbj', blocks, inv_gram, precision=lax.Precision.HIGH...  8.83 us
    dot_general x4, matrix products, block_scores(): jnp.dot(left, right.T, precision=lax.Precision.HIGHEST, preferred_element...  6.51 us
    ppermute x3, starting transfers between devices, shifted(): lax.ppermute(array, axis, [(i, (i + by) % devices) for i in range(devices)])  5.05 us
  transfers between devices with their start and end apart: 4, of which 4 were waited for; matrix products, arithmetic and copies ran while one was open for 14% of the time, Pallas kernels for 0%

commit v1 on v0

v1 whole, which is shorter than its diff:
```python
import jax
import jax.numpy as jnp
from jax import lax
from jax.sharding import PartitionSpec as P

HIGHEST = lax.Precision.HIGHEST


def send(array, axis, to):
    devices = lax.axis_size(axis)
    return lax.ppermute(array, axis, [(i, to(i)) for i in range(devices)])


def swap(array, axis, bit):
    return send(array, axis, lambda i: i ^ bit)


def condition(queries, inv_gram):
    rows = queries.shape[0]
    nblocks, modsize = inv_gram.shape[0], inv_gram.shape[1]
    blocks = queries.reshape(rows, nblocks, modsize)
    out = jnp.einsum("qbi,bij->qbj", blocks, inv_gram, precision=HIGHEST)
    return out.reshape(rows, nblocks * modsize)


def block_scores(left, right):
    return jnp.dot(left, right.T, precision=HIGHEST, preferred_element_type=jnp.float32)


def shards(queries, train_rows, inv_gram):
    qrows, fshard = queries.shape
    trows = train_rows.shape[0]
    nrow, nfeat = lax.axis_size("row"), lax.axis_size("feat")
    row, feat = lax.axis_index("row"), lax.axis_index("feat")
    half, nmod = fshard // 2, inv_gram.shape[0] // 2
    side = row % 2

    def mine(array):
        return lax.dynamic_slice_in_dim(array, side * half, half, 1)

    def others(array):
        return lax.dynamic_slice_in_dim(array, (1 - side) * half, half, 1)

    q_mine, q_others = mine(queries), others(queries)
    t_mine, t_others = mine(train_rows), others(train_rows)
    q_pair = swap(q_others, "row", 1)
    blocks = [(t_mine, row), (swap(t_others, "row", 1), row ^ 1)]
    for step in range(2, nrow, 2):
        blocks.append((send(t_mine, "row", lambda i: (i + step) % nrow), (row - step) % nrow))
        blocks.append((send(t_others, "row", lambda i: ((i + step) % nrow) ^ 1), ((row ^ 1) - step) % nrow))

    gram = lax.dynamic_slice_in_dim(inv_gram, side * nmod, nmod, 0)
    conditioned = condition(jnp.concatenate([q_mine, q_pair], axis=0), gram)
    partial = jnp.zeros((nrow, 2 * qrows, trows), jnp.float32)
    for block, source in blocks:
        partial = lax.dynamic_update_slice(partial, block_scores(conditioned, block)[None], (source, 0, 0))

    left, bit = nfeat, 1
    partial = partial.reshape(nfeat, nrow // nfeat, 2 * qrows, trows)
    while left > 1:
        pairs = partial.reshape(left // 2, 2, *partial.shape[1:])
        odd = (feat // bit) % 2 == 1
        keep = jnp.where(odd, pairs[:, 1], pairs[:, 0])
        give = jnp.where(odd, pairs[:, 0], pairs[:, 1])
        partial = keep + swap(give, "feat", bit)
        left, bit = left // 2, bit * 2
    partial = partial[0]
    scores = partial[:, :qrows] + swap(partial[:, qrows:], "row", 1)
    return scores.transpose(1, 0, 2).reshape(qrows, -1)


def solution(mesh):
    return jax.shard_map(
        shards,
        mesh=mesh,
        in_specs=(P("row", "feat"), P(("grp", "row"), "feat"), P("feat", None, None)),
        out_specs=P("row", ("grp", "feat")),
        check_vma=False,
    )
```

time: 96.6 us -> 60 us (0.62)
  waiting for transfers between devices: 61.9 us -> 35.8 us
  between operations: 13.5 us -> 0.2 us
  matrix products: 15.3 us -> 9.89 us
  starting transfers between devices: 5.06 us -> 10.1 us
  local copies, waits for them, and re-layouts: 0.68 us -> 2.87 us
    unnamed x2 -> x0, waiting for transfers between devices: 19.3 us -> none
    ppermute x3 -> x7, waiting for transfers between devices: 42.6 us -> 35.8 us  [send(): return lax.ppermute(array, axis, [(i, to(i)) for i in range(devices)])]
    dot_general x5, matrix products: 15.3 us -> 9.89 us  [the longest x1 5.08 us: condition(): out = jnp.einsum('qbi,bij->qbj', blocks, inv_gram, precision=HIGHEST)]
    ppermute x3 -> x7, starting transfers between devices: 5.05 us -> 10.1 us  [send(): return lax.ppermute(array, axis, [(i, to(i)) for i in range(devices)])]
    dynamic_slice x0 -> x2, local copies, waits for them, and re-layouts: none -> 2.46 us  [the longest x1 1.27 us: mine(): return lax.dynamic_slice_in_dim(array, side * half, half, 1)]
  transfers between devices with their start and end apart: 4 -> 7, of which waited for: 4 -> 5; matrix products, arithmetic and copies ran while one was open for 14% -> 18% of each run, Pallas kernels for 0% -> 0%
where the time goes in v1:
time: 60 us; the launch traced here: 59.7 us
  waiting for transfers between devices  35.8 us (60%)
  starting transfers between devices  10.1 us (17%)
  matrix products  9.89 us (16%)
  local copies, waits for them, and re-layouts  2.87 us (5%)
  other arithmetic  0.81 us (1%)
    ppermute x7, waiting for transfers between devices, send(): return lax.ppermute(array, axis, [(i, to(i)) for i in range(devices)])  35.8 us
    ppermute x7, starting transfers between devices, send(): return lax.ppermute(array, axis, [(i, to(i)) for i in range(devices)])  10.1 us
    dot_general x1, matrix products, condition(): out = jnp.einsum('qbi,bij->qbj', blocks, inv_gram, precision=HIGHEST)  5.08 us
    dot_general x4, matrix products, block_scores(): jnp.dot(left, right.T, precision=HIGHEST, preferred_element_type=jnp.floa...  4.8 us
    dynamic_slice x1, local copies, waits for them, and re-layouts, mine(): return lax.dynamic_slice_in_dim(array, side * half, half, 1)  1.27 us
  transfers between devices with their start and end apart: 7, of which 5 were waited for; matrix products, arithmetic and copies ran while one was open for 18% of the time, Pallas kernels for 0%

profile of v1, /device:TPU:0, one launch (start us, length us, event | category | flops | bytes accessed | tf_op | source)
XLA Modules:
  0.0 59.7 jit_solution(7990279320793497632)
XLA Ops:
  0.0 1.3 %constant_dynamic-slice_fusion.3 = (f32[128,1024]{1,0:T(8,128)S(1)}, f32[128,1024]{1,0:T(8,128)S(1)}) fusion(f32[128,2048]{1,0:T(8,128)} %param.3, s32[]{:T(128)S(6)} %select_n.126, s32[]{:T(128)S(6)} %select_n.127), kind=kLoop, calls=%fused_computation.25 | loop fusion | bytes 2097160 | tf_op jit(solution)/shard_map/dynamic_slice | solution.py:39
  1.3 0.2 copy.20
  1.5 3.1 %collective-permute-start = (f32[128,1024]{0,1:T(8,128)S(1)}, f32[128,1024]{0,1:T(8,128)S(1)}, u32[]{:S(2)}, u32[]{:S(2)}) collective-permute-start(f32[128,1024]{0,1:T(8,128)S(1)} %copy.20), channel_id=1, source_target_pairs={{0,4},{4,0},{8,12},{12,8},{1,5},{5,1},{9,13},{13,9},{2,6},{6,2},{1... | collective-permute-start | bytes 1572872 | tf_op jit(solution)/shard_map/ppermute | solution.py:11
  4.6 1.2 %constant_dynamic-slice_fusion = (f32[104,1024]{1,0:T(8,128)S(1)}, f32[104,1024]{1,0:T(8,128)S(1)}) fusion(f32[104,2048]{1,0:T(8,128)} %param.4, s32[]{:T(128)S(6)} %select_n.127, s32[]{:T(128)S(6)} %select_n.126), kind=kLoop, calls=%fused_computation.22 | loop fusion | bytes 1703944 | tf_op jit(solution)/shard_map/dynamic_slice | solution.py:42
  5.8 0.1 collective-permute-start.1
  5.8 4.0 %collective-permute-start.3 = (f32[104,1024]{1,0:T(8,128)S(1)}, f32[104,1024]{1,0:T(8,128)S(1)}, u32[]{:S(2)}, u32[]{:S(2)}) collective-permute-start(f32[104,1024]{1,0:T(8,128)S(1)} %get-tuple-element.7), channel_id=1, source_target_pairs={{0,12},{4,8},{8,4},{12,0},{1,13},{5,9},{9,5},{13,1},{2,14},{6,10},... | collective-permute-start | bytes 1277960 | tf_op jit(solution)/shard_map/ppermute | solution.py:11
  9.9 0.0 collective-permute-start.2
  9.9 0.2 copy.19
  10.1 8.0 %collective-permute-done = f32[128,1024]{0,1:T(8,128)S(1)} collective-permute-done((f32[128,1024]{0,1:T(8,128)S(1)}, f32[128,1024]{0,1:T(8,128)S(1)}, u32[]{:S(2)}, u32[]{:S(2)}) %collective-permute-start) | collective-permute-done | bytes 524320 | tf_op jit(solution)/shard_map/ppermute | solution.py:11
  18.1 0.1 pad_maximum_fusion
  18.2 5.1 %fusion = f32[2,512,256]{2,1,0:T(8,128)S(1)} fusion(f32[256,2,512]{0,2,1:T(8,128)S(1)} %bitcast.74, f32[4,512,512]{2,1,0:T(8,128)} %param.5, s32[]{:T(128)S(6)} %select_n.125), kind=kOutput, calls=%fused_computation | convolution fusion | flops 1610612736 | bytes 4194308 | tf_op jit(solution)/shard_map/qbi,bij->qbj/dot_general | solution.py:22
  23.3 0.7 %fusion.5 = f32[4,256,104]{1,2,0:T(8,128)S(1)} fusion(f32[4,256,104]{1,2,0:T(8,128)S(1)} %broadcast_in_dim.15, s32[]{:T(128)S(6)} %select_n.128, f32[256,1024]{0,1:T(8,128)S(1)} %bitcast.70, f32[104,1024]{1,0:T(8,128)S(1)} %get-tuple-element.8), kind=kOutput, calls=%fused_computation.9 | convolution fusion | flops 327155712 | bytes 1581060 | tf_op jit(solution)/shard_map/dot_general | solution.py:27
  24.0 20.0 %collective-permute-done.1 = f32[104,1024]{1,0:T(8,128)} collective-permute-done((f32[104,1024]{1,0:T(8,128)S(1)}, f32[104,1024]{1,0:T(8,128)}, u32[]{:S(2)}, u32[]{:S(2)}) %collective-permute-start.1) | collective-permute-done | bytes 426016 | tf_op jit(solution)/shard_map/ppermute | solution.py:11
  44.0 1.7 %fusion.4 = f32[4,256,104]{1,2,0:T(8,128)S(1)} fusion(f32[4,256,104]{1,2,0:T(8,128)S(1)} %fusion.5, s32[]{:T(128)S(6)} %select_n.129, f32[256,1024]{0,1:T(8,128)S(1)} %bitcast.71, f32[104,1024]{1,0:T(8,128)} %collective-permute-done.1), kind=kOutput, calls=%fused_computation.7 | convolution fusion | flops 327155712 | bytes 1581060 | tf_op jit(solution)/shard_map/dot_general | solution.py:27
  45.7 0.0 collective-permute-done.2
  45.7 1.7 %fusion.3 = f32[4,256,104]{1,2,0:T(8,128)S(1)} fusion(f32[4,256,104]{1,2,0:T(8,128)S(1)} %fusion.4, s32[]{:T(128)S(6)} %select_n.131, f32[256,1024]{0,1:T(8,128)S(1)} %bitcast.72, f32[104,1024]{1,0:T(8,128)} %collective-permute-done.2), kind=kOutput, calls=%fused_computation.5 | convolution fusion | flops 327155712 | bytes 1581060 | tf_op jit(solution)/shard_map/dot_general | solution.py:27
  47.4 0.0 collective-permute-done.3
  47.4 0.7 %fusion.2 = f32[4,256,104]{1,2,0:T(8,128)S(1)} fusion(f32[4,256,104]{1,2,0:T(8,128)S(1)} %fusion.3, s32[]{:T(128)S(6)} %select_n.133, f32[256,1024]{0,1:T(8,128)S(1)} %bitcast.73, f32[104,1024]{1,0:T(8,128)S(1)} %collective-permute-done.3), kind=kOutput, calls=%fused_computation.3 | convolution fusion | flops 327155712 | bytes 1581060 | tf_op jit(solution)/shard_map/dot_general | solution.py:27
  48.2 0.1 collective-permute-start.4
  48.3 1.4 %collective-permute-done.4 = f32[2,1,256,104]{2,3,0,1:T(8,128)S(1)} collective-permute-done((f32[2,1,256,104]{2,3,0,1:T(8,128)S(1)}, f32[2,1,256,104]{2,3,0,1:T(8,128)S(1)}, u32[]{:S(2)}, u32[]{:S(2)}) %collective-permute-start.4) | collective-permute-done | bytes 213024 | tf_op jit(solution)/shard_map/ppermute | solution.py:11
  49.8 1.7 %collective-permute-start.5 = (f32[1,1,256,104]{2,3,1,0:T(8,128)S(1)}, f32[1,1,256,104]{2,3,1,0:T(8,128)S(1)}, u32[]{:S(2)}, u32[]{:S(2)}) collective-permute-start(f32[1,1,256,104]{2,3,1,0:T(8,128)S(1)} %fusion.8), channel_id=1, source_target_pairs={{0,2},{1,3},{2,0},{3,1},{4,6},{5,7},{6,4},{7,5},{8,10},{9,11},{10,... | collective-permute-start | bytes 319496 | tf_op jit(solution)/shard_map/ppermute | solution.py:11
  51.5 3.4 %collective-permute-done.5 = f32[1,1,256,104]{2,3,1,0:T(8,128)S(1)} collective-permute-done((f32[1,1,256,104]{2,3,1,0:T(8,128)S(1)}, f32[1,1,256,104]{2,3,1,0:T(8,128)S(1)}, u32[]{:S(2)}, u32[]{:S(2)}) %collective-permute-start.5) | collective-permute-done | bytes 106528 | tf_op jit(solution)/shard_map/ppermute | solution.py:11
  54.9 1.1 %collective-permute-start.6 = (f32[1,128,104]{1,2,0:T(8,128)S(1)}, f32[1,128,104]{1,2,0:T(8,128)S(1)}, u32[]{:S(2)}, u32[]{:S(2)}) collective-permute-start(f32[1,128,104]{1,2,0:T(8,128)S(1)} %slice.33), channel_id=1, source_target_pairs={{0,4},{4,0},{8,12},{12,8},{1,5},{5,1},{9,13},{13,9},{2,6},{6,2},{1... | collective-permute-start | bytes 159752 | tf_op jit(solution)/shard_map/ppermute | solution.py:11
  56.0 3.1 %collective-permute-done.6 = f32[1,128,104]{1,2,0:T(8,128)S(1)} collective-permute-done((f32[1,128,104]{1,2,0:T(8,128)S(1)}, f32[1,128,104]{1,2,0:T(8,128)S(1)}, u32[]{:S(2)}, u32[]{:S(2)}) %collective-permute-start.6) | collective-permute-done | bytes 53280 | tf_op jit(solution)/shard_map/ppermute | solution.py:11
  59.1 0.6 %fusion.10 = f32[128,104]{0,1:T(8,128)} fusion(f32[1,128,104]{1,2,0:T(8,128)S(1)} %collective-permute-done.6, f32[1,256,104]{1,2,0:T(8,128)S(1)} %fusion.9), kind=kLoop, calls=%fused_computation.21 | loop fusion | flops 13312 | bytes 159744 | tf_op jit(solution)/shard_map/reshape;transpose | solution.py:69
  (6 shorter events, 0.1 us)
Async XLA Ops:
  1.5 16.6 %collective-permute-start = (f32[128,1024]{0,1:T(8,128)S(1)}, f32[128,1024]{0,1:T(8,128)S(1)}, u32[]{:S(2)}, u32[]{:S(2)}) collective-permute-start(f32[128,1024]{0,1:T(8,128)S(1)} %copy.20), channel_id=1, source_target_pairs={{0,4},{4,0},{8,12},{12,8},{1,5},{5,1},{9,13},{13,9},{2,6},{6,2},{1... | collective-permute-start | bytes 1572872 | tf_op jit(solution)/shard_map/ppermute | solution.py:11
  5.8 38.2 %collective-permute-start.1 = (f32[104,1024]{1,0:T(8,128)S(1)}, f32[104,1024]{1,0:T(8,128)}, u32[]{:S(2)}, u32[]{:S(2)}) collective-permute-start(f32[104,1024]{1,0:T(8,128)S(1)} %get-tuple-element.7), channel_id=1, source_target_pairs={{0,4},{4,0},{8,12},{12,8},{1,5},{5,1},{9,13},{13,9},{2,6},{6,2},{1... | collective-permute-start | bytes 1277960 | tf_op jit(solution)/shard_map/ppermute | solution.py:11
  5.8 41.6 %collective-permute-start.3 = (f32[104,1024]{1,0:T(8,128)S(1)}, f32[104,1024]{1,0:T(8,128)S(1)}, u32[]{:S(2)}, u32[]{:S(2)}) collective-permute-start(f32[104,1024]{1,0:T(8,128)S(1)} %get-tuple-element.7), channel_id=1, source_target_pairs={{0,12},{4,8},{8,4},{12,0},{1,13},{5,9},{9,5},{13,1},{2,14},{6,10},... | collective-permute-start | bytes 1277960 | tf_op jit(solution)/shard_map/ppermute | solution.py:11
  9.9 35.8 %collective-permute-start.2 = (f32[104,1024]{1,0:T(8,128)S(1)}, f32[104,1024]{1,0:T(8,128)}, u32[]{:S(2)}, u32[]{:S(2)}) collective-permute-start(f32[104,1024]{1,0:T(8,128)S(1)} %get-tuple-element.8), channel_id=1, source_target_pairs={{0,8},{4,12},{8,0},{12,4},{1,9},{5,13},{9,1},{13,5},{2,10},{6,14},... | collective-permute-start | bytes 1277960 | tf_op jit(solution)/shard_map/ppermute | solution.py:11
  48.2 1.5 %collective-permute-start.4 = (f32[2,1,256,104]{2,3,0,1:T(8,128)S(1)}, f32[2,1,256,104]{2,3,0,1:T(8,128)S(1)}, u32[]{:S(2)}, u32[]{:S(2)}) collective-permute-start(f32[2,1,256,104]{2,3,0,1:T(8,128)S(1)} %select_bitcast_fusion), channel_id=1, source_target_pairs={{0,1},{1,0},{2,3},{3,2},{4,5},{5,4},{6,7},{7,6},{8,9},{9,8},{10,11... | collective-permute-start | bytes 638984 | tf_op jit(solution)/shard_map/ppermute | solution.py:11
  49.8 5.1 %collective-permute-start.5 = (f32[1,1,256,104]{2,3,1,0:T(8,128)S(1)}, f32[1,1,256,104]{2,3,1,0:T(8,128)S(1)}, u32[]{:S(2)}, u32[]{:S(2)}) collective-permute-start(f32[1,1,256,104]{2,3,1,0:T(8,128)S(1)} %fusion.8), channel_id=1, source_target_pairs={{0,2},{1,3},{2,0},{3,1},{4,6},{5,7},{6,4},{7,5},{8,10},{9,11},{10,... | collective-permute-start | bytes 319496 | tf_op jit(solution)/shard_map/ppermute | solution.py:11
  54.9 4.2 %collective-permute-start.6 = (f32[1,128,104]{1,2,0:T(8,128)S(1)}, f32[1,128,104]{1,2,0:T(8,128)S(1)}, u32[]{:S(2)}, u32[]{:S(2)}) collective-permute-start(f32[1,128,104]{1,2,0:T(8,128)S(1)} %slice.33), channel_id=1, source_target_pairs={{0,4},{4,0},{8,12},{12,8},{1,5},{5,1},{9,13},{13,9},{2,6},{6,2},{1... | collective-permute-start | bytes 159752 | tf_op jit(solution)/shard_map/ppermute | solution.py:11

commit v2 on v1

--- a/solution.py
+++ b/solution.py
@@ -1,9 +1,16 @@
+import functools
+
 import jax
 import jax.numpy as jnp
 from jax import lax
+from jax.experimental import pallas as pl
+from jax.experimental.pallas import tpu as pltpu
 from jax.sharding import PartitionSpec as P
 
 HIGHEST = lax.Precision.HIGHEST
+ANYWHERE = pl.BlockSpec(memory_space=pl.ANY)
+VMEM = pl.BlockSpec(memory_space=pltpu.VMEM)
+FREE = pl.CostEstimate(flops=0, bytes_accessed=0, transcendentals=0)
 
 
 def send(array, axis, to):
@@ -27,7 +34,7 @@
     return jnp.dot(left, right.T, precision=HIGHEST, preferred_element_type=jnp.float32)
 
 
-def shards(queries, train_rows, inv_gram):
+def any_shards(queries, train_rows, inv_gram):
     qrows, fshard = queries.shape
     trows = train_rows.shape[0]
     nrow, nfeat = lax.axis_size("row"), lax.axis_size("feat")
@@ -69,9 +76,102 @@
     return scores.transpose(1, 0, 2).reshape(qrows, -1)
 
 
+def split(x):
+    high = x.astype(jnp.bfloat16)
+    return high, (x - high.astype(jnp.float32)).astype(jnp.bfloat16)
+
+
+def condition_kernel(side_ref, q_ref, pair_ref, gram_ref, high_ref, low_ref):
+    q_high, q_low = split(jnp.concatenate([q_ref[...], pair_ref[...]], axis=0))
+    g_high, g_low = split(gram_ref[0])
+    dot = functools.partial(jnp.dot, preferred_element_type=jnp.float32)
+    out = dot(q_high, g_low) + dot(q_low, g_high) + dot(q_high, g_high)
+    high_ref[...], low_ref[...] = split(out)
+
+
+def condition_pair(queries, pair, inv_gram, side):
+    qrows = queries.shape[0]
+    nmod, modsize = inv_gram.shape[0] // 2, inv_gram.shape[1]
+    out = jax.ShapeDtypeStruct((2 * qrows, nmod * modsize), jnp.bfloat16)
+    return pl.pallas_call(
+        condition_kernel,
+        out_shape=[out, out],
+        grid_spec=pltpu.PrefetchScalarGridSpec(
+            num_scalar_prefetch=1,
+            grid=(nmod,),
+            in_specs=[
+                pl.BlockSpec((qrows, modsize), lambda m, side: (0, side[0] * nmod + m)),
+                pl.BlockSpec((qrows, modsize), lambda m, side: (0, m)),
+                pl.BlockSpec((1, modsize, modsize), lambda m, side: (side[0] * nmod + m, 0, 0)),
+            ],
+            out_specs=[pl.BlockSpec((2 * qrows, modsize), lambda m, side: (0, m))] * 2,
+        ),
+        cost_estimate=FREE,
+        compiler_params=pltpu.CompilerParams(vmem_limit_bytes=24 << 20),
+    )(side.reshape(1), queries, pair, inv_gram)
+
+
+def scores_kernel(high_ref, low_ref, t_ref, *refs):
+    out_ref = refs[-1]
+    t_high, t_low = split(t_ref[...])
+    dot = functools.partial(
+        lax.dot_general, dimension_numbers=(((1,), (1,)), ((), ())), preferred_element_type=jnp.float32
+    )
+    high, low = high_ref[...], low_ref[...]
+    out_ref[...] = dot(high, t_low) + dot(low, t_high) + dot(high, t_high)
+
+
+def score(conditioned, block, *after):
+    high, low = conditioned
+    return pl.pallas_call(
+        scores_kernel,
+        out_shape=jax.ShapeDtypeStruct((high.shape[0], block.shape[0]), jnp.float32),
+        in_specs=[VMEM] * 3 + [ANYWHERE] * len(after),
+        out_specs=VMEM,
+        cost_estimate=FREE,
+        compiler_params=pltpu.CompilerParams(vmem_limit_bytes=16 << 20),
+    )(high, low, block, *after)
+
+
+def swap_both(array, row_bit, feat_bit):
+    nrow, nfeat = lax.axis_size("row"), lax.axis_size("feat")
+    pairs = [
+        (r * nfeat + f, (r ^ row_bit) * nfeat + (f ^ feat_bit)) for r in range(nrow) for f in range(nfeat)
+    ]
+    return lax.ppermute(array, ("row", "feat"), pairs)
+
+
+def four_shards(queries, train_rows, inv_gram):
+    qrows, half = queries.shape[0], queries.shape[1] // 2
+    row, feat = lax.axis_index("row"), lax.axis_index("feat")
+    side = row % 2
+    t_others = lax.dynamic_slice_in_dim(train_rows, (1 - side) * half, half, 1)
+    cross = swap(t_others, "row", 3)
+    q_others = lax.dynamic_slice_in_dim(queries, (1 - side) * half, half, 1)
+    q_pair = swap(q_others, "row", 1)
+    t_mine = lax.dynamic_slice_in_dim(train_rows, side * half, half, 1)
+    far = swap(t_mine, "row", 2)
+    near = swap(t_others, "row", 1)
+    conditioned = condition_pair(queries, q_pair, inv_gram, side)
+
+    blocks = [score(conditioned, block) for block in (t_mine, near, far, cross)]
+    own, odd = (row ^ feat) % 2 == 0, ((row ^ feat) // 2) % 2 == 1
+    give = jnp.stack([jnp.where(own, blocks[1], blocks[0]), jnp.where(own, blocks[3], blocks[2])])
+    keep = jnp.stack([jnp.where(own, blocks[0], blocks[1]), jnp.where(own, blocks[2], blocks[3])])
+    keep = keep + swap(give, "feat", 1)
+    give, keep = jnp.where(odd, keep[0], keep[1]), jnp.where(odd, keep[1], keep[0])
+    return (
+        keep[:qrows]
+        + swap_both(give[:qrows], 0, 2)
+        + swap_both(keep[qrows:], 1, 0)
+        + swap_both(give[qrows:], 1, 2)
+    )
+
+
 def solution(mesh):
+    four = mesh.shape["row"] == 4 and mesh.shape["feat"] == 4
     return jax.shard_map(
-        shards,
+        four_shards if four else any_shards,
         mesh=mesh,
         in_specs=(P("row", "feat"), P(("grp", "row"), "feat"), P("feat", None, None)),
         out_specs=P("row", ("grp", "feat")),

time: 60 us -> 56.3 us (0.938)
  matrix products: 9.89 us -> 0 us
  Pallas kernels: 0 us -> 3.73 us
  local copies, waits for them, and re-layouts: 2.87 us -> 6.41 us
  waiting for transfers between devices: 35.8 us -> 34.5 us
  starting transfers between devices: 10.1 us -> 11.1 us
  other arithmetic: 0.81 us -> 0.13 us
    dot_general x5 -> x0, matrix products: 9.89 us -> none  [the longest x1 5.08 us: condition(): out = jnp.einsum('qbi,bij->qbj', blocks, inv_gram, precision=HIGHEST)]
    ppermute x7 -> x5, waiting for transfers between devices: 35.8 us -> 29.4 us  [send(): return lax.ppermute(array, axis, [(i, to(i)) for i in range(devices)])]
    ppermute x0 -> x3, waiting for transfers between devices: none -> 5.13 us  [swap_both(): return lax.ppermute(array, ('row', 'feat'), pairs)]
    ppermute x0 -> x3, starting transfers between devices: none -> 4.38 us  [swap_both(): return lax.ppermute(array, ('row', 'feat'), pairs)]
    pallas_call x0 -> x5, Pallas kernels: none -> 3.73 us  [the longest x4 2.27 us: score(): pl.pallas_call(scores_kernel, out_shape=jax.ShapeDtypeStruct((high.shape[...]
    ppermute x7 -> x5, starting transfers between devices: 10.1 us -> 6.71 us  [send(): return lax.ppermute(array, axis, [(i, to(i)) for i in range(devices)])]
    unnamed x2 -> x4, local copies, waits for them, and re-layouts: 0.38 us -> 3.41 us
    add x0 -> x1, local copies, waits for them, and re-layouts: none -> 0.72 us  [four_shards(): keep[:qrows] + swap_both(give[:qrows], 0, 2) + swap_both(keep[qrows:], 1, 0)]
  transfers between devices with their start and end apart: 7 -> 8, of which waited for: 5 -> 8; matrix products, arithmetic and copies ran while one was open for 18% -> 2% of each run, Pallas kernels for 0% -> 6%
where the time goes in v2:
time: 56.3 us; the launch traced here: 56.1 us
  waiting for transfers between devices  34.5 us (61%)
  starting transfers between devices  11.1 us (20%)
  local copies, waits for them, and re-layouts  6.41 us (11%)
  Pallas kernels  3.73 us (7%)
    ppermute x5, waiting for transfers between devices, send(): return lax.ppermute(array, axis, [(i, to(i)) for i in range(devices)])  29.4 us
    ppermute x5, starting transfers between devices, send(): return lax.ppermute(array, axis, [(i, to(i)) for i in range(devices)])  6.71 us
    ppermute x3, waiting for transfers between devices, swap_both(): return lax.ppermute(array, ('row', 'feat'), pairs)  5.13 us
    ppermute x3, starting transfers between devices, swap_both(): return lax.ppermute(array, ('row', 'feat'), pairs)  4.38 us
    unnamed x4, local copies, waits for them, and re-layouts  3.41 us
    pallas_call x4, Pallas kernels, score(): pl.pallas_call(scores_kernel, out_shape=jax.ShapeDtypeStruct((high.shape[...  2.27 us
    pallas_call x1, Pallas kernels, condition_pair(): pl.pallas_call(condition_kernel, out_shape=[out, out], grid_spec=pltpu.Pr...  1.46 us
    dynamic_slice x1, local copies, waits for them, and re-layouts, four_shards(): t_mine = lax.dynamic_slice_in_dim(train_rows, side * half, half, 1)  1.19 us
  transfers between devices with their start and end apart: 8, of which 8 were waited for; matrix products, arithmetic and copies ran while one was open for 2% of the time, Pallas kernels for 6%

profile of v2, /device:TPU:0, one launch (start us, length us, event | category | flops | bytes accessed | tf_op | source)
XLA Modules:
  0.0 56.1 jit_solution(17738483630378088319)
XLA Ops:
  0.0 1.1 %constant_dynamic-slice_fusion.2 = f32[128,1024]{1,0:T(8,128)S(1)} fusion(f32[128,2048]{1,0:T(8,128)} %q_ref.1, s32[]{:T(128)S(6)} %select_n.64), kind=kLoop, calls=%fused_computation.17 | loop fusion | bytes 1048580 | tf_op jit(solution)/shard_map/dynamic_slice | solution.py:150
  1.1 3.1 %collective-permute-start = (f32[128,1024]{1,0:T(8,128)S(1)}, f32[128,1024]{1,0:T(8,128)S(1)}, u32[]{:S(2)}, u32[]{:S(2)}) collective-permute-start(f32[128,1024]{1,0:T(8,128)S(1)} %constant_dynamic-slice_fusion.2), channel_id=1, source_target_pairs={{0,4},{4,0},{8,12},{12,8},{1,5},{5,1},{9,13},{13,9},{2,6},{6,2},{1... | collective-permute-start | bytes 1572872 | tf_op jit(solution)/shard_map/ppermute | solution.py:18
  4.2 1.2 %constant_dynamic-slice_fusion.1 = (f32[104,1024]{1,0:T(8,128)S(1)}, f32[104,1024]{1,0:T(8,128)S(1)}) fusion(f32[104,2048]{1,0:T(8,128)} %param.4, s32[]{:T(128)S(6)} %select_n.65, s32[]{:T(128)S(6)} %select_n.64), kind=kLoop, calls=%fused_computation.16 | loop fusion | bytes 1703944 | tf_op jit(solution)/shard_map/dynamic_slice | solution.py:152
  5.4 2.7 %collective-permute-start.2 = (f32[104,1024]{1,0:T(8,128)S(1)}, f32[104,1024]{1,0:T(8,128)S(1)}, u32[]{:S(2)}, u32[]{:S(2)}) collective-permute-start(f32[104,1024]{1,0:T(8,128)S(1)} %get-tuple-element.9.t_ref), channel_id=1, source_target_pairs={{0,8},{4,12},{8,0},{12,4},{1,9},{5,13},{9,1},{13,5},{2,10},{6,14},... | collective-permute-start | bytes 1277960 | tf_op jit(solution)/shard_map/ppermute | solution.py:18
  8.0 0.0 collective-permute-start.3
  8.0 0.9 %collective-permute-start.1 = (f32[104,1024]{1,0:T(8,128)S(1)}, f32[104,1024]{1,0:T(8,128)S(1)}, u32[]{:S(2)}, u32[]{:S(2)}) collective-permute-start(f32[104,1024]{1,0:T(8,128)S(1)} %get-tuple-element.10), channel_id=1, source_target_pairs={{0,4},{4,0},{8,12},{12,8},{1,5},{5,1},{9,13},{13,9},{2,6},{6,2},{1... | collective-permute-start | bytes 1277960 | tf_op jit(solution)/shard_map/ppermute | solution.py:18
  8.9 16.8 %collective-permute-done.pair_ref = f32[128,1024]{1,0:T(8,128)S(1)} collective-permute-done((f32[128,1024]{1,0:T(8,128)S(1)}, f32[128,1024]{1,0:T(8,128)S(1)}, u32[]{:S(2)}, u32[]{:S(2)}) %collective-permute-start) | collective-permute-done | bytes 524320 | tf_op jit(solution)/shard_map/ppermute | solution.py:18
  25.7 0.0 copy-start
  25.7 2.2 %copy-done = f32[4,512,512]{2,1,0:T(8,128)S(1)} copy-done((f32[4,512,512]{2,1,0:T(8,128)S(1)}, f32[4,512,512]{2,1,0:T(8,128)}, u32[]{:S(2)}) %copy-start) | copy-done | bytes 4194328
  27.9 0.0 copy-start.1
  27.9 1.2 %copy-done.1 = f32[128,2048]{1,0:T(8,128)S(1)} copy-done((f32[128,2048]{1,0:T(8,128)S(1)}, f32[128,2048]{1,0:T(8,128)}, u32[]{:S(2)}) %copy-start.1) | copy-done | bytes 1048600
  29.1 1.5 %shard_map.37 = (bf16[256,1024]{1,0:T(8,128)(2,1)S(1)}, bf16[256,1024]{1,0:T(8,128)(2,1)S(1)}) custom-call(s32[1]{0:T(128)} %bitcast.side_ref, f32[128,2048]{1,0:T(8,128)S(1)} %copy-done.1, f32[128,1024]{1,0:T(8,128)S(1)} %collective-permute-done.pair_ref, f32[4,512,512]{2,1,0:T(8,128)S(1)} %copy-done), custom_call_target="tpu_custom_call" | custom-call | tf_op jit(solution)/shard_map/pallas_call | solution.py:96
  30.6 0.6 %shard_map.38 = f32[256,104]{1,0:T(8,128)S(1)} custom-call(bf16[256,1024]{1,0:T(8,128)(2,1)S(1)} %get-tuple-element.7.high_ref, bf16[256,1024]{1,0:T(8,128)(2,1)S(1)} %get-tuple-element.8.low_ref, f32[104,1024]{1,0:T(8,128)S(1)} %get-tuple-element.9.t_ref), custom_call_target="tpu_custom_call" | custom-call | tf_op jit(solution)/shard_map/pallas_call | solution.py:126
  31.2 5.8 %collective-permute-done.2.t_ref = f32[104,1024]{1,0:T(8,128)S(1)} collective-permute-done((f32[104,1024]{1,0:T(8,128)S(1)}, f32[104,1024]{1,0:T(8,128)S(1)}, u32[]{:S(2)}, u32[]{:S(2)}) %collective-permute-start.2) | collective-permute-done | bytes 426016 | tf_op jit(solution)/shard_map/ppermute | solution.py:18
  37.0 0.6 %shard_map.40 = f32[256,104]{1,0:T(8,128)S(1)} custom-call(bf16[256,1024]{1,0:T(8,128)(2,1)S(1)} %get-tuple-element.7.high_ref, bf16[256,1024]{1,0:T(8,128)(2,1)S(1)} %get-tuple-element.8.low_ref, f32[104,1024]{1,0:T(8,128)S(1)} %collective-permute-done.2.t_ref), custom_call_target="tpu_custom_call" | custom-call | tf_op jit(solution)/shard_map/pallas_call | solution.py:126
  37.5 0.2 collective-permute-done.3.t_ref
  37.8 0.6 %shard_map.41 = f32[256,104]{1,0:T(8,128)S(1)} custom-call(bf16[256,1024]{1,0:T(8,128)(2,1)S(1)} %get-tuple-element.7.high_ref, bf16[256,1024]{1,0:T(8,128)(2,1)S(1)} %get-tuple-element.8.low_ref, f32[104,1024]{1,0:T(8,128)S(1)} %collective-permute-done.3.t_ref), custom_call_target="tpu_custom_call" | custom-call | tf_op jit(solution)/shard_map/pallas_call | solution.py:126
  38.4 5.1 %collective-permute-done.1.t_ref = f32[104,1024]{1,0:T(8,128)S(1)} collective-permute-done((f32[104,1024]{1,0:T(8,128)S(1)}, f32[104,1024]{1,0:T(8,128)S(1)}, u32[]{:S(2)}, u32[]{:S(2)}) %collective-permute-start.1) | collective-permute-done | bytes 426016 | tf_op jit(solution)/shard_map/ppermute | solution.py:18
  43.5 0.6 %shard_map.39 = f32[256,104]{1,0:T(8,128)S(1)} custom-call(bf16[256,1024]{1,0:T(8,128)(2,1)S(1)} %get-tuple-element.7.high_ref, bf16[256,1024]{1,0:T(8,128)(2,1)S(1)} %get-tuple-element.8.low_ref, f32[104,1024]{1,0:T(8,128)S(1)} %collective-permute-done.1.t_ref), custom_call_target="tpu_custom_call" | custom-call | tf_op jit(solution)/shard_map/pallas_call | solution.py:126
  44.1 0.1 collective-permute-start.4
  44.2 1.5 %collective-permute-done.4 = f32[2,256,104]{2,1,0:T(8,128)S(1)} collective-permute-done((f32[2,256,104]{2,1,0:T(8,128)S(1)}, f32[2,256,104]{2,1,0:T(8,128)S(1)}, u32[]{:S(2)}, u32[]{:S(2)}) %collective-permute-start.4) | collective-permute-done | bytes 213024 | tf_op jit(solution)/shard_map/ppermute | solution.py:18
  45.8 2.8 %collective-permute-start.6 = (f32[128,104]{1,0:T(8,128)S(1)}, f32[128,104]{1,0:T(8,128)S(1)}, u32[]{:S(2)}, u32[]{:S(2)}) collective-permute-start(f32[128,104]{1,0:T(8,128)S(1)} %slice_bitcast_fusion.1), channel_id=1, source_target_pairs={{0,4},{1,5},{2,6},{3,7},{4,0},{5,1},{6,2},{7,3},{8,12},{9,13},{10,... | collective-permute-start | bytes 159752 | tf_op jit(solution)/shard_map/ppermute | solution.py:141
  48.6 1.5 %collective-permute-start.5 = (f32[128,104]{1,0:T(8,128)S(1)}, f32[128,104]{1,0:T(8,128)S(1)}, u32[]{:S(2)}, u32[]{:S(2)}) collective-permute-start(f32[128,104]{1,0:T(8,128)S(1)} %get-tuple-element.17), channel_id=1, source_target_pairs={{0,2},{1,3},{2,0},{3,1},{4,6},{5,7},{6,4},{7,5},{8,10},{9,11},{10,... | collective-permute-start | bytes 159752 | tf_op jit(solution)/shard_map/ppermute | solution.py:141
  50.2 0.0 collective-permute-start.7
  50.2 0.9 %collective-permute-done.6 = f32[128,104]{1,0:T(8,128)S(1)} collective-permute-done((f32[128,104]{1,0:T(8,128)S(1)}, f32[128,104]{1,0:T(8,128)S(1)}, u32[]{:S(2)}, u32[]{:S(2)}) %collective-permute-start.6) | collective-permute-done | bytes 53280 | tf_op jit(solution)/shard_map/ppermute | solution.py:141
  51.0 1.9 %collective-permute-done.5 = f32[128,104]{1,0:T(8,128)S(1)} collective-permute-done((f32[128,104]{1,0:T(8,128)S(1)}, f32[128,104]{1,0:T(8,128)S(1)}, u32[]{:S(2)}, u32[]{:S(2)}) %collective-permute-start.5) | collective-permute-done | bytes 53280 | tf_op jit(solution)/shard_map/ppermute | solution.py:141
  52.9 2.4 %collective-permute-done.7 = f32[128,104]{1,0:T(8,128)S(1)} collective-permute-done((f32[128,104]{1,0:T(8,128)S(1)}, f32[128,104]{1,0:T(8,128)S(1)}, u32[]{:S(2)}, u32[]{:S(2)}) %collective-permute-start.7) | collective-permute-done | bytes 53280 | tf_op jit(solution)/shard_map/ppermute | solution.py:141
  55.3 0.7 %copy.4 = f32[128,104]{0,1:T(8,128)} copy(f32[128,104]{1,0:T(8,128)S(1)} %fusion.2) | data formatting | bytes 106496 | tf_op jit(solution)/shard_map/add | solution.py:164
  (8 shorter events, 0.1 us)
Async XLA Ops:
  1.1 24.6 %collective-permute-start = (f32[128,1024]{1,0:T(8,128)S(1)}, f32[128,1024]{1,0:T(8,128)S(1)}, u32[]{:S(2)}, u32[]{:S(2)}) collective-permute-start(f32[128,1024]{1,0:T(8,128)S(1)} %constant_dynamic-slice_fusion.2), channel_id=1, source_target_pairs={{0,4},{4,0},{8,12},{12,8},{1,5},{5,1},{9,13},{13,9},{2,6},{6,2},{1... | collective-permute-start | bytes 1572872 | tf_op jit(solution)/shard_map/ppermute | solution.py:18
  5.4 31.6 %collective-permute-start.2 = (f32[104,1024]{1,0:T(8,128)S(1)}, f32[104,1024]{1,0:T(8,128)S(1)}, u32[]{:S(2)}, u32[]{:S(2)}) collective-permute-start(f32[104,1024]{1,0:T(8,128)S(1)} %get-tuple-element.9.t_ref), channel_id=1, source_target_pairs={{0,8},{4,12},{8,0},{12,4},{1,9},{5,13},{9,1},{13,5},{2,10},{6,14},... | collective-permute-start | bytes 1277960 | tf_op jit(solution)/shard_map/ppermute | solution.py:18
  8.0 29.8 %collective-permute-start.3 = (f32[104,1024]{1,0:T(8,128)S(1)}, f32[104,1024]{1,0:T(8,128)S(1)}, u32[]{:S(2)}, u32[]{:S(2)}) collective-permute-start(f32[104,1024]{1,0:T(8,128)S(1)} %get-tuple-element.10), channel_id=1, source_target_pairs={{0,12},{4,8},{8,4},{12,0},{1,13},{5,9},{9,5},{13,1},{2,14},{6,10},... | collective-permute-start | bytes 1277960 | tf_op jit(solution)/shard_map/ppermute | solution.py:18
  8.0 35.5 %collective-permute-start.1 = (f32[104,1024]{1,0:T(8,128)S(1)}, f32[104,1024]{1,0:T(8,128)S(1)}, u32[]{:S(2)}, u32[]{:S(2)}) collective-permute-start(f32[104,1024]{1,0:T(8,128)S(1)} %get-tuple-element.10), channel_id=1, source_target_pairs={{0,4},{4,0},{8,12},{12,8},{1,5},{5,1},{9,13},{13,9},{2,6},{6,2},{1... | collective-permute-start | bytes 1277960 | tf_op jit(solution)/shard_map/ppermute | solution.py:18
  25.7 2.2 %copy-start = (f32[4,512,512]{2,1,0:T(8,128)S(1)}, f32[4,512,512]{2,1,0:T(8,128)}, u32[]{:S(2)}) copy-start(f32[4,512,512]{2,1,0:T(8,128)} %gram_ref.1) | copy-start | bytes 12582916
  27.9 1.2 %copy-start.1 = (f32[128,2048]{1,0:T(8,128)S(1)}, f32[128,2048]{1,0:T(8,128)}, u32[]{:S(2)}) copy-start(f32[128,2048]{1,0:T(8,128)} %q_ref.1) | copy-start | bytes 3145732
  44.1 1.6 %collective-permute-start.4 = (f32[2,256,104]{2,1,0:T(8,128)S(1)}, f32[2,256,104]{2,1,0:T(8,128)S(1)}, u32[]{:S(2)}, u32[]{:S(2)}) collective-permute-start(f32[2,256,104]{2,1,0:T(8,128)S(1)} %pad_maximum_fusion), channel_id=1, source_target_pairs={{0,1},{1,0},{2,3},{3,2},{4,5},{5,4},{6,7},{7,6},{8,9},{9,8},{10,11... | collective-permute-start | bytes 638984 | tf_op jit(solution)/shard_map/ppermute | solution.py:18
  45.8 5.2 %collective-permute-start.6 = (f32[128,104]{1,0:T(8,128)S(1)}, f32[128,104]{1,0:T(8,128)S(1)}, u32[]{:S(2)}, u32[]{:S(2)}) collective-permute-start(f32[128,104]{1,0:T(8,128)S(1)} %slice_bitcast_fusion.1), channel_id=1, source_target_pairs={{0,4},{1,5},{2,6},{3,7},{4,0},{5,1},{6,2},{7,3},{8,12},{9,13},{10,... | collective-permute-start | bytes 159752 | tf_op jit(solution)/shard_map/ppermute | solution.py:141
  48.6 4.3 %collective-permute-start.5 = (f32[128,104]{1,0:T(8,128)S(1)}, f32[128,104]{1,0:T(8,128)S(1)}, u32[]{:S(2)}, u32[]{:S(2)}) collective-permute-start(f32[128,104]{1,0:T(8,128)S(1)} %get-tuple-element.17), channel_id=1, source_target_pairs={{0,2},{1,3},{2,0},{3,1},{4,6},{5,7},{6,4},{7,5},{8,10},{9,11},{10,... | collective-permute-start | bytes 159752 | tf_op jit(solution)/shard_map/ppermute | solution.py:141
  50.2 5.2 %collective-permute-start.7 = (f32[128,104]{1,0:T(8,128)S(1)}, f32[128,104]{1,0:T(8,128)S(1)}, u32[]{:S(2)}, u32[]{:S(2)}) collective-permute-start(f32[128,104]{1,0:T(8,128)S(1)} %get-tuple-element.18), channel_id=1, source_target_pairs={{0,6},{1,7},{2,4},{3,5},{4,2},{5,3},{6,0},{7,1},{8,14},{9,15},{10,... | collective-permute-start | bytes 159752 | tf_op jit(solution)/shard_map/ppermute | solution.py:141

commit v3 on v2

--- a/solution.py
+++ b/solution.py
@@ -76,12 +76,41 @@
     return scores.transpose(1, 0, 2).reshape(qrows, -1)
 
 
+def pack_kernel(q_ref, t_ref, q_others, t_others, t_mine, sems):
+    side = lax.axis_index("row") % 2
+    half = t_mine.shape[1]
+    mine = pl.ds(pl.multiple_of(side * half, half), half)
+    others = pl.ds(pl.multiple_of((1 - side) * half, half), half)
+    copies = [
+        pltpu.make_async_copy(q_ref.at[:, others], q_others, sems.at[0]),
+        pltpu.make_async_copy(t_ref.at[:, others], t_others, sems.at[1]),
+        pltpu.make_async_copy(t_ref.at[:, mine], t_mine, sems.at[2]),
+    ]
+    for copy in copies:
+        copy.start()
+    for copy in copies:
+        copy.wait()
+
+
+def pack(queries, train_rows):
+    qrows, half = queries.shape[0], queries.shape[1] // 2
+    trows = train_rows.shape[0]
+    return pl.pallas_call(
+        pack_kernel,
+        out_shape=[pltpu.VMEM((rows, half), jnp.float32) for rows in (qrows, trows, trows)],
+        in_specs=[ANYWHERE] * 2,
+        out_specs=[VMEM] * 3,
+        scratch_shapes=[pltpu.SemaphoreType.DMA((3,))],
+        cost_estimate=FREE,
+    )(queries, train_rows)
+
+
 def split(x):
     high = x.astype(jnp.bfloat16)
     return high, (x - high.astype(jnp.float32)).astype(jnp.bfloat16)
 
 
-def condition_kernel(side_ref, q_ref, pair_ref, gram_ref, high_ref, low_ref):
+def condition_kernel(side_ref, q_ref, pair_ref, gram_ref, after_ref, high_ref, low_ref):
     q_high, q_low = split(jnp.concatenate([q_ref[...], pair_ref[...]], axis=0))
     g_high, g_low = split(gram_ref[0])
     dot = functools.partial(jnp.dot, preferred_element_type=jnp.float32)
@@ -89,7 +118,7 @@
     high_ref[...], low_ref[...] = split(out)
 
 
-def condition_pair(queries, pair, inv_gram, side):
+def condition_pair(queries, pair, inv_gram, side, after):
     qrows = queries.shape[0]
     nmod, modsize = inv_gram.shape[0] // 2, inv_gram.shape[1]
     out = jax.ShapeDtypeStruct((2 * qrows, nmod * modsize), jnp.bfloat16)
@@ -103,34 +132,58 @@
                 pl.BlockSpec((qrows, modsize), lambda m, side: (0, side[0] * nmod + m)),
                 pl.BlockSpec((qrows, modsize), lambda m, side: (0, m)),
                 pl.BlockSpec((1, modsize, modsize), lambda m, side: (side[0] * nmod + m, 0, 0)),
+                ANYWHERE,
             ],
             out_specs=[pl.BlockSpec((2 * qrows, modsize), lambda m, side: (0, m))] * 2,
         ),
         cost_estimate=FREE,
         compiler_params=pltpu.CompilerParams(vmem_limit_bytes=24 << 20),
-    )(side.reshape(1), queries, pair, inv_gram)
-
-
-def scores_kernel(high_ref, low_ref, t_ref, *refs):
-    out_ref = refs[-1]
+    )(side.reshape(1), queries, pair, inv_gram, after)
+
+
+def block_scores_of(high, low, t_ref):
+    rows = t_ref.shape[0]
     t_high, t_low = split(t_ref[...])
     dot = functools.partial(
         lax.dot_general, dimension_numbers=(((1,), (1,)), ((), ())), preferred_element_type=jnp.float32
     )
-    high, low = high_ref[...], low_ref[...]
-    out_ref[...] = dot(high, t_low) + dot(low, t_high) + dot(high, t_high)
-
-
-def score(conditioned, block, *after):
-    high, low = conditioned
+    both = dot(jnp.concatenate([t_high, t_low], axis=0), high)
+    return both[rows:] + dot(t_high, low) + both[:rows]
+
+
+def scores_kernel(high_ref, low_ref, t_ref, out_ref):
+    out_ref[...] = block_scores_of(high_ref[...], low_ref[...], t_ref)
+
+
+def score(conditioned, block):
     return pl.pallas_call(
         scores_kernel,
-        out_shape=jax.ShapeDtypeStruct((high.shape[0], block.shape[0]), jnp.float32),
-        in_specs=[VMEM] * 3 + [ANYWHERE] * len(after),
+        out_shape=jax.ShapeDtypeStruct((block.shape[0], conditioned[0].shape[0]), jnp.float32),
+        in_specs=[VMEM] * 3,
         out_specs=VMEM,
         cost_estimate=FREE,
         compiler_params=pltpu.CompilerParams(vmem_limit_bytes=16 << 20),
-    )(high, low, block, *after)
+    )(*conditioned, block)
+
+
+def last_kernel(flip_ref, high_ref, low_ref, near_ref, own_ref, far_ref, cross_ref, keep_ref, give_ref):
+    near = block_scores_of(high_ref[...], low_ref[...], near_ref)
+    own, far, cross = own_ref[...], far_ref[...], cross_ref[...]
+    flip = flip_ref[0] != 0
+    keep_ref[0], give_ref[0] = jnp.where(flip, near, own), jnp.where(flip, own, near)
+    keep_ref[1], give_ref[1] = jnp.where(flip, cross, far), jnp.where(flip, far, cross)
+
+
+def last_scores(conditioned, near, others, flip):
+    out = jax.ShapeDtypeStruct((2, *others[0].shape), jnp.float32)
+    return pl.pallas_call(
+        last_kernel,
+        out_shape=[out, out],
+        in_specs=[pl.BlockSpec(memory_space=pltpu.SMEM)] + [VMEM] * 6,
+        out_specs=[VMEM] * 2,
+        cost_estimate=FREE,
+        compiler_params=pltpu.CompilerParams(vmem_limit_bytes=16 << 20),
+    )(flip.reshape(1), *conditioned, near, *others)
 
 
 def swap_both(array, row_bit, feat_bit):
@@ -142,30 +195,27 @@
 
 
 def four_shards(queries, train_rows, inv_gram):
-    qrows, half = queries.shape[0], queries.shape[1] // 2
+    qrows = queries.shape[0]
     row, feat = lax.axis_index("row"), lax.axis_index("feat")
     side = row % 2
-    t_others = lax.dynamic_slice_in_dim(train_rows, (1 - side) * half, half, 1)
+    q_others, t_others, t_mine = pack(queries, train_rows)
+    q_pair = swap(q_others, "row", 1)
     cross = swap(t_others, "row", 3)
-    q_others = lax.dynamic_slice_in_dim(queries, (1 - side) * half, half, 1)
-    q_pair = swap(q_others, "row", 1)
-    t_mine = lax.dynamic_slice_in_dim(train_rows, side * half, half, 1)
     far = swap(t_mine, "row", 2)
     near = swap(t_others, "row", 1)
-    conditioned = condition_pair(queries, q_pair, inv_gram, side)
-
-    blocks = [score(conditioned, block) for block in (t_mine, near, far, cross)]
-    own, odd = (row ^ feat) % 2 == 0, ((row ^ feat) // 2) % 2 == 1
-    give = jnp.stack([jnp.where(own, blocks[1], blocks[0]), jnp.where(own, blocks[3], blocks[2])])
-    keep = jnp.stack([jnp.where(own, blocks[0], blocks[1]), jnp.where(own, blocks[2], blocks[3])])
+    conditioned = condition_pair(queries, q_pair, inv_gram, side, cross)
+
+    others = [score(conditioned, block) for block in (t_mine, far, cross)]
+    flip = (row ^ feat) % 2
+    keep, give = last_scores(conditioned, near, others, flip)
     keep = keep + swap(give, "feat", 1)
+    odd = ((row ^ feat) // 2) % 2 == 1
     give, keep = jnp.where(odd, keep[0], keep[1]), jnp.where(odd, keep[1], keep[0])
-    return (
-        keep[:qrows]
-        + swap_both(give[:qrows], 0, 2)
-        + swap_both(keep[qrows:], 1, 0)
-        + swap_both(give[qrows:], 1, 2)
-    )
+    own, other = slice(0, qrows), slice(qrows, 2 * qrows)
+    there = swap_both(keep[:, other], 1, 0)
+    across = swap_both(give[:, other], 1, 2)
+    beside = swap_both(give[:, own], 0, 2)
+    return (keep[:, own] + there + across + beside).T
 
 
 def solution(mesh):

time: 56.3 us -> 54.1 us (0.961)
  local copies, waits for them, and re-layouts: 6.41 us -> 3.43 us
  Pallas kernels: 3.73 us -> 4.79 us
  waiting for transfers between devices: 34.5 us -> 33.8 us
    dynamic_slice x2 -> x0, local copies, waits for them, and re-layouts: 2.27 us -> none  [the longest x1 1.19 us: four_shards(): t_mine = lax.dynamic_slice_in_dim(train_rows, side * half, half, 1)]
    ppermute x3, waiting for transfers between devices: 5.13 us -> 3.17 us  [swap_both(): return lax.ppermute(array, ('row', 'feat'), pairs)]
    ppermute x5, waiting for transfers between devices: 29.4 us -> 30.6 us  [send(): return lax.ppermute(array, axis, [(i, to(i)) for i in range(devices)])]
    pallas_call x4 -> x5, Pallas kernels: 2.27 us -> 3.32 us  [the longest x3 1.49 us: score(): pl.pallas_call(scores_kernel, out_shape=jax.ShapeDtypeStruct((block.shape...]
    ppermute x5, starting transfers between devices: 6.71 us -> 7.55 us  [send(): return lax.ppermute(array, axis, [(i, to(i)) for i in range(devices)])]
    ppermute x3, starting transfers between devices: 4.38 us -> 3.55 us  [swap_both(): return lax.ppermute(array, ('row', 'feat'), pairs)]
    add x1 -> x0, local copies, waits for them, and re-layouts: 0.72 us -> none  [four_shards(): keep[:qrows] + swap_both(give[:qrows], 0, 2) + swap_both(keep[qrows:], 1, 0)]
    transpose x0 -> x1, other arithmetic: none -> 0.64 us  [four_shards(): return (keep[:, own] + there + across + beside).T]
  transfers between devices with their start and end apart: 8 -> 8, of which waited for: 8 -> 6; matrix products, arithmetic and copies ran while one was open for 2% -> 0% of each run, Pallas kernels for 6% -> 5%
where the time goes in v3:
time: 54.1 us; the launch traced here: 53.9 us
  waiting for transfers between devices  33.8 us (62%)
  starting transfers between devices  11.1 us (21%)
  Pallas kernels  4.79 us (9%)
  local copies, waits for them, and re-layouts  3.43 us (6%)
  other arithmetic  0.68 us (1%)
    ppermute x5, waiting for transfers between devices, send(): return lax.ppermute(array, axis, [(i, to(i)) for i in range(devices)])  30.6 us
    ppermute x5, starting transfers between devices, send(): return lax.ppermute(array, axis, [(i, to(i)) for i in range(devices)])  7.55 us
    ppermute x3, starting transfers between devices, swap_both(): return lax.ppermute(array, ('row', 'feat'), pairs)  3.55 us
    unnamed x4, local copies, waits for them, and re-layouts  3.41 us
    ppermute x3, waiting for transfers between devices, swap_both(): return lax.ppermute(array, ('row', 'feat'), pairs)  3.17 us
    pallas_call x3, Pallas kernels, score(): pl.pallas_call(scores_kernel, out_shape=jax.ShapeDtypeStruct((block.shape...  1.49 us
    pallas_call x1, Pallas kernels, condition_pair(): pl.pallas_call(condition_kernel, out_shape=[out, out], grid_spec=pltpu.Pr...  1.47 us
    pallas_call x1, Pallas kernels, pack(): pl.pallas_call(pack_kernel, out_shape=[pltpu.VMEM((rows, half), jnp.float...  1.32 us
  transfers between devices with their start and end apart: 8, of which 6 were waited for; matrix products, arithmetic and copies ran while one was open for 0% of the time, Pallas kernels for 5%

profile of v3, /device:TPU:0, one launch (start us, length us, event | category | flops | bytes accessed | tf_op | source)
XLA Modules:
  0.0 53.9 jit_solution(9632653705741480691)
XLA Ops:
  0.0 1.3 %shard_map.37 = (f32[128,1024]{1,0:T(8,128)S(1)}, f32[104,1024]{1,0:T(8,128)S(1)}, f32[104,1024]{1,0:T(8,128)S(1)}) custom-call(f32[128,2048]{1,0:T(8,128)} %q_ref.3, f32[104,2048]{1,0:T(8,128)} %t_ref.1), custom_call_target="tpu_custom_call" | custom-call | tf_op jit(solution)/shard_map/pallas_call | solution.py:98
  1.3 3.1 %collective-permute-start = (f32[128,1024]{1,0:T(8,128)S(1)}, f32[128,1024]{1,0:T(8,128)S(1)}, u32[]{:S(2)}, u32[]{:S(2)}) collective-permute-start(f32[128,1024]{1,0:T(8,128)S(1)} %get-tuple-element.12), channel_id=1, source_target_pairs={{0,4},{4,0},{8,12},{12,8},{1,5},{5,1},{9,13},{13,9},{2,6},{6,2},{1... | collective-permute-start | bytes 1572872 | tf_op jit(solution)/shard_map/ppermute | solution.py:18
  4.4 2.5 %collective-permute-start.1 = (f32[104,1024]{1,0:T(8,128)S(1)}, f32[104,1024]{1,0:T(8,128)S(1)}, u32[]{:S(2)}, u32[]{:S(2)}) collective-permute-start(f32[104,1024]{1,0:T(8,128)S(1)} %get-tuple-element.13), channel_id=1, source_target_pairs={{0,12},{4,8},{8,4},{12,0},{1,13},{5,9},{9,5},{13,1},{2,14},{6,10},... | collective-permute-start | bytes 1277960 | tf_op jit(solution)/shard_map/ppermute | solution.py:18
  6.9 0.1 collective-permute-start.3
  7.0 1.8 %collective-permute-start.2 = (f32[104,1024]{1,0:T(8,128)S(1)}, f32[104,1024]{1,0:T(8,128)S(1)}, u32[]{:S(2)}, u32[]{:S(2)}) collective-permute-start(f32[104,1024]{1,0:T(8,128)S(1)} %get-tuple-element.13), channel_id=1, source_target_pairs={{0,4},{4,0},{8,12},{12,8},{1,5},{5,1},{9,13},{13,9},{2,6},{6,2},{1... | collective-permute-start | bytes 1277960 | tf_op jit(solution)/shard_map/ppermute | solution.py:18
  8.8 20.1 %collective-permute-done.1.after_ref.t_ref = f32[104,1024]{1,0:T(8,128)S(1)} collective-permute-done((f32[104,1024]{1,0:T(8,128)S(1)}, f32[104,1024]{1,0:T(8,128)S(1)}, u32[]{:S(2)}, u32[]{:S(2)}) %collective-permute-start.1) | collective-permute-done | bytes 426016 | tf_op jit(solution)/shard_map/ppermute | solution.py:18
  28.9 0.0 collective-permute-done.pair_ref
  28.9 0.0 copy-start
  28.9 1.2 %copy-done = f32[128,2048]{1,0:T(8,128)S(1)} copy-done((f32[128,2048]{1,0:T(8,128)S(1)}, f32[128,2048]{1,0:T(8,128)}, u32[]{:S(2)}) %copy-start) | copy-done | bytes 1048600
  30.1 0.0 copy-start.1
  30.1 2.2 %copy-done.1 = f32[4,512,512]{2,1,0:T(8,128)S(1)} copy-done((f32[4,512,512]{2,1,0:T(8,128)S(1)}, f32[4,512,512]{2,1,0:T(8,128)}, u32[]{:S(2)}) %copy-start.1) | copy-done | bytes 4194328
  32.3 1.5 %shard_map.38 = (bf16[256,1024]{1,0:T(8,128)(2,1)S(1)}, bf16[256,1024]{1,0:T(8,128)(2,1)S(1)}) custom-call(s32[1]{0:T(128)} %bitcast.1.side_ref, f32[128,2048]{1,0:T(8,128)S(1)} %copy-done, f32[128,1024]{1,0:T(8,128)S(1)} %collective-permute-done.pair_ref, f32[4,512,512]{2,1,0:T(8,128)S(1)} %copy-done.1, f32[104,1024]{1,0:T(8,128)S(1)} %collective-permute-done.1.after_ref.t_ref), custom_call_target="tpu_custom_call" | custom-call | tf_op jit(solution)/shard_map/pallas_call | solution.py:125
  33.8 0.5 shard_map.39.own_ref
  34.3 0.5 shard_map.41.cross_ref
  34.8 9.1 %collective-permute-done.3.t_ref = f32[104,1024]{1,0:T(8,128)S(1)} collective-permute-done((f32[104,1024]{1,0:T(8,128)S(1)}, f32[104,1024]{1,0:T(8,128)S(1)}, u32[]{:S(2)}, u32[]{:S(2)}) %collective-permute-start.3) | collective-permute-done | bytes 426016 | tf_op jit(solution)/shard_map/ppermute | solution.py:18
  43.9 0.5 shard_map.40.far_ref
  44.4 0.0 collective-permute-done.2.near_ref
  44.4 0.5 shard_map.42
  45.0 0.1 collective-permute-start.4
  45.1 1.4 %collective-permute-done.4 = f32[2,104,256]{2,1,0:T(8,128)S(1)} collective-permute-done((f32[2,104,256]{2,1,0:T(8,128)S(1)}, f32[2,104,256]{2,1,0:T(8,128)S(1)}, u32[]{:S(2)}, u32[]{:S(2)}) %collective-permute-start.4) | collective-permute-done | bytes 213024 | tf_op jit(solution)/shard_map/ppermute | solution.py:18
  46.6 2.1 %collective-permute-start.6 = (f32[104,128]{1,0:T(8,128)S(1)}, f32[104,128]{1,0:T(8,128)S(1)}, u32[]{:S(2)}, u32[]{:S(2)}) collective-permute-start(f32[104,128]{1,0:T(8,128)S(1)} %get-tuple-element.21), channel_id=1, source_target_pairs={{0,6},{1,7},{2,4},{3,5},{4,2},{5,3},{6,0},{7,1},{8,14},{9,15},{10,... | collective-permute-start | bytes 159752 | tf_op jit(solution)/shard_map/ppermute | solution.py:194
  48.6 0.5 collective-permute-start.7
  49.2 1.0 %collective-permute-start.5 = (f32[104,128]{1,0:T(8,128)S(1)}, f32[104,128]{1,0:T(8,128)S(1)}, u32[]{:S(2)}, u32[]{:S(2)}) collective-permute-start(f32[104,128]{1,0:T(8,128)S(1)} %slice.29), channel_id=1, source_target_pairs={{0,4},{1,5},{2,6},{3,7},{4,0},{5,1},{6,2},{7,3},{8,12},{9,13},{10,... | collective-permute-start | bytes 159752 | tf_op jit(solution)/shard_map/ppermute | solution.py:194
  50.1 1.6 %collective-permute-done.6 = f32[104,128]{1,0:T(8,128)S(1)} collective-permute-done((f32[104,128]{1,0:T(8,128)S(1)}, f32[104,128]{1,0:T(8,128)S(1)}, u32[]{:S(2)}, u32[]{:S(2)}) %collective-permute-start.6) | collective-permute-done | bytes 53280 | tf_op jit(solution)/shard_map/ppermute | solution.py:194
  51.8 1.0 %collective-permute-done.7 = f32[104,128]{1,0:T(8,128)S(1)} collective-permute-done((f32[104,128]{1,0:T(8,128)S(1)}, f32[104,128]{1,0:T(8,128)S(1)}, u32[]{:S(2)}, u32[]{:S(2)}) %collective-permute-start.7) | collective-permute-done | bytes 53280 | tf_op jit(solution)/shard_map/ppermute | solution.py:194
  52.8 0.5 collective-permute-done.5
  53.3 0.6 %fusion.2 = f32[128,104]{0,1:T(8,128)} fusion(f32[104,128]{1,0:T(8,128)S(1)} %collective-permute-done.7, f32[104,128]{1,0:T(8,128)S(1)} %collective-permute-done.6, f32[104,128]{1,0:T(8,128)S(1)} %collective-permute-done.5, f32[104,256]{1,0:T(8,128)S(1)} %get-tuple-element.19), kind=kLoop, calls=%fused_computation.5 | loop fusion | flops 39936 | bytes 266240 | tf_op jit(solution)/shard_map/transpose | solution.py:218
  (4 shorter events, 0.1 us)
Async XLA Ops:
  1.3 27.6 %collective-permute-start = (f32[128,1024]{1,0:T(8,128)S(1)}, f32[128,1024]{1,0:T(8,128)S(1)}, u32[]{:S(2)}, u32[]{:S(2)}) collective-permute-start(f32[128,1024]{1,0:T(8,128)S(1)} %get-tuple-element.12), channel_id=1, source_target_pairs={{0,4},{4,0},{8,12},{12,8},{1,5},{5,1},{9,13},{13,9},{2,6},{6,2},{1... | collective-permute-start | bytes 1572872 | tf_op jit(solution)/shard_map/ppermute | solution.py:18
  4.4 24.5 %collective-permute-start.1 = (f32[104,1024]{1,0:T(8,128)S(1)}, f32[104,1024]{1,0:T(8,128)S(1)}, u32[]{:S(2)}, u32[]{:S(2)}) collective-permute-start(f32[104,1024]{1,0:T(8,128)S(1)} %get-tuple-element.13), channel_id=1, source_target_pairs={{0,12},{4,8},{8,4},{12,0},{1,13},{5,9},{9,5},{13,1},{2,14},{6,10},... | collective-permute-start | bytes 1277960 | tf_op jit(solution)/shard_map/ppermute | solution.py:18
  6.9 37.0 %collective-permute-start.3 = (f32[104,1024]{1,0:T(8,128)S(1)}, f32[104,1024]{1,0:T(8,128)S(1)}, u32[]{:S(2)}, u32[]{:S(2)}) collective-permute-start(f32[104,1024]{1,0:T(8,128)S(1)} %get-tuple-element.16.t_ref), channel_id=1, source_target_pairs={{0,8},{4,12},{8,0},{12,4},{1,9},{5,13},{9,1},{13,5},{2,10},{6,14},... | collective-permute-start | bytes 1277960 | tf_op jit(solution)/shard_map/ppermute | solution.py:18
  7.0 37.4 %collective-permute-start.2 = (f32[104,1024]{1,0:T(8,128)S(1)}, f32[104,1024]{1,0:T(8,128)S(1)}, u32[]{:S(2)}, u32[]{:S(2)}) collective-permute-start(f32[104,1024]{1,0:T(8,128)S(1)} %get-tuple-element.13), channel_id=1, source_target_pairs={{0,4},{4,0},{8,12},{12,8},{1,5},{5,1},{9,13},{13,9},{2,6},{6,2},{1... | collective-permute-start | bytes 1277960 | tf_op jit(solution)/shard_map/ppermute | solution.py:18
  28.9 1.2 %copy-start = (f32[128,2048]{1,0:T(8,128)S(1)}, f32[128,2048]{1,0:T(8,128)}, u32[]{:S(2)}) copy-start(f32[128,2048]{1,0:T(8,128)} %q_ref.3) | copy-start | bytes 3145732
  30.1 2.2 %copy-start.1 = (f32[4,512,512]{2,1,0:T(8,128)S(1)}, f32[4,512,512]{2,1,0:T(8,128)}, u32[]{:S(2)}) copy-start(f32[4,512,512]{2,1,0:T(8,128)} %gram_ref.1) | copy-start | bytes 12582916
  45.0 1.5 %collective-permute-start.4 = (f32[2,104,256]{2,1,0:T(8,128)S(1)}, f32[2,104,256]{2,1,0:T(8,128)S(1)}, u32[]{:S(2)}, u32[]{:S(2)}) collective-permute-start(f32[2,104,256]{2,1,0:T(8,128)S(1)} %get-tuple-element.18), channel_id=1, source_target_pairs={{0,1},{1,0},{2,3},{3,2},{4,5},{5,4},{6,7},{7,6},{8,9},{9,8},{10,11... | collective-permute-start | bytes 638984 | tf_op jit(solution)/shard_map/ppermute | solution.py:18
  46.6 5.2 %collective-permute-start.6 = (f32[104,128]{1,0:T(8,128)S(1)}, f32[104,128]{1,0:T(8,128)S(1)}, u32[]{:S(2)}, u32[]{:S(2)}) collective-permute-start(f32[104,128]{1,0:T(8,128)S(1)} %get-tuple-element.21), channel_id=1, source_target_pairs={{0,6},{1,7},{2,4},{3,5},{4,2},{5,3},{6,0},{7,1},{8,14},{9,15},{10,... | collective-permute-start | bytes 159752 | tf_op jit(solution)/shard_map/ppermute | solution.py:194
  48.6 4.2 %collective-permute-start.7 = (f32[104,128]{1,0:T(8,128)S(1)}, f32[104,128]{1,0:T(8,128)S(1)}, u32[]{:S(2)}, u32[]{:S(2)}) collective-permute-start(f32[104,128]{1,0:T(8,128)S(1)} %get-tuple-element.22), channel_id=1, source_target_pairs={{0,2},{1,3},{2,0},{3,1},{4,6},{5,7},{6,4},{7,5},{8,10},{9,11},{10,... | collective-permute-start | bytes 159752 | tf_op jit(solution)/shard_map/ppermute | solution.py:194
  49.2 4.1 %collective-permute-start.5 = (f32[104,128]{1,0:T(8,128)S(1)}, f32[104,128]{1,0:T(8,128)S(1)}, u32[]{:S(2)}, u32[]{:S(2)}) collective-permute-start(f32[104,128]{1,0:T(8,128)S(1)} %slice.29), channel_id=1, source_target_pairs={{0,4},{1,5},{2,6},{3,7},{4,0},{5,1},{6,2},{7,3},{8,12},{9,13},{10,... | collective-permute-start | bytes 159752 | tf_op jit(solution)/shard_map/ppermute | solution.py:194

commit v4 on v3

--- a/solution.py
+++ b/solution.py
@@ -20,6 +20,10 @@
 
 def swap(array, axis, bit):
     return send(array, axis, lambda i: i ^ bit)
+
+
+SPLIT_COST = pl.CostEstimate(flops=8589934592, bytes_accessed=67108864, transcendentals=0)
+PREPARE_COST = pl.CostEstimate(flops=1 << 31, bytes_accessed=8 << 20, transcendentals=0)
 
 
 def condition(queries, inv_gram):
@@ -78,11 +82,13 @@
 
 def pack_kernel(q_ref, t_ref, q_others, t_others, t_mine, sems):
     side = lax.axis_index("row") % 2
+    qrows = q_others.shape[0]
+    rows = pl.ds(pl.multiple_of(lax.axis_index("grp") * qrows, qrows), qrows)
     half = t_mine.shape[1]
     mine = pl.ds(pl.multiple_of(side * half, half), half)
     others = pl.ds(pl.multiple_of((1 - side) * half, half), half)
     copies = [
-        pltpu.make_async_copy(q_ref.at[:, others], q_others, sems.at[0]),
+        pltpu.make_async_copy(q_ref.at[rows, others], q_others, sems.at[0]),
         pltpu.make_async_copy(t_ref.at[:, others], t_others, sems.at[1]),
         pltpu.make_async_copy(t_ref.at[:, mine], t_mine, sems.at[2]),
     ]
@@ -93,7 +99,7 @@
 
 
 def pack(queries, train_rows):
-    qrows, half = queries.shape[0], queries.shape[1] // 2
+    qrows, half = queries.shape[0] // 2, queries.shape[1] // 2
     trows = train_rows.shape[0]
     return pl.pallas_call(
         pack_kernel,
@@ -110,40 +116,83 @@
     return high, (x - high.astype(jnp.float32)).astype(jnp.bfloat16)
 
 
-def condition_kernel(side_ref, q_ref, pair_ref, gram_ref, after_ref, high_ref, low_ref):
-    q_high, q_low = split(jnp.concatenate([q_ref[...], pair_ref[...]], axis=0))
-    g_high, g_low = split(gram_ref[0])
-    dot = functools.partial(jnp.dot, preferred_element_type=jnp.float32)
-    out = dot(q_high, g_low) + dot(q_low, g_high) + dot(q_high, g_high)
-    high_ref[...], low_ref[...] = split(out)
-
-
-def condition_pair(queries, pair, inv_gram, side, after):
-    qrows = queries.shape[0]
+def dot3(left, right, dimension_numbers):
+    dot = functools.partial(
+        lax.dot_general, dimension_numbers=dimension_numbers, preferred_element_type=jnp.float32
+    )
+    return dot(left[0], right[1]) + dot(left[1], right[0]) + dot(left[0], right[0])
+
+
+PLAIN = (((1,), (0,)), ((), ()))
+
+
+def prepare_kernel(q_hbm, gram_hbm, high_ref, low_ref, g_high_ref, g_low_ref, q_ref, gram_ref, sems):
+    side = lax.axis_index("row") % 2
+    nmod, modsize = gram_ref.shape[0], gram_ref.shape[1]
+    half = nmod * modsize
+    get_q = pltpu.make_async_copy(q_hbm.at[:, pl.ds(pl.multiple_of(side * half, half), half)], q_ref, sems.at[0])
+    get_gram = pltpu.make_async_copy(gram_hbm.at[pl.ds(side * nmod, nmod)], gram_ref, sems.at[1])
+    get_q.start()
+    get_gram.start()
+    get_q.wait()
+    get_gram.wait()
+    for m in range(nmod):
+        columns = slice(m * modsize, (m + 1) * modsize)
+        gram = split(gram_ref[m])
+        g_high_ref[m], g_low_ref[m] = gram
+        high_ref[:, columns], low_ref[:, columns] = split(dot3(split(q_ref[:, columns]), gram, PLAIN))
+
+
+def prepare(queries, inv_gram):
+    qrows, half = queries.shape[0], queries.shape[1] // 2
     nmod, modsize = inv_gram.shape[0] // 2, inv_gram.shape[1]
-    out = jax.ShapeDtypeStruct((2 * qrows, nmod * modsize), jnp.bfloat16)
+    conditioned = pltpu.VMEM((qrows, half), jnp.bfloat16)
+    gram = pltpu.VMEM((nmod, modsize, modsize), jnp.bfloat16)
+    return pl.pallas_call(
+        prepare_kernel,
+        out_shape=[conditioned, conditioned, gram, gram],
+        in_specs=[ANYWHERE] * 2,
+        out_specs=[VMEM] * 4,
+        scratch_shapes=[
+            pltpu.VMEM((qrows, half), jnp.float32),
+            pltpu.VMEM((nmod, modsize, modsize), jnp.float32),
+            pltpu.SemaphoreType.DMA((2,)),
+        ],
+        cost_estimate=PREPARE_COST,
+        compiler_params=pltpu.CompilerParams(vmem_limit_bytes=24 << 20),
+    )(queries, inv_gram)
+
+
+def condition_kernel(own_high, own_low, g_high, g_low, straight_ref, swapped_ref, after_ref, high_ref, low_ref):
+    qrows, modsize = own_high.shape[0], g_high.shape[1]
+    first = lax.axis_index("grp") == 0
+    high_ref[:qrows], low_ref[:qrows] = own_high[...], own_low[...]
+    for m in range(g_high.shape[0]):
+        columns = slice(m * modsize, (m + 1) * modsize)
+        straight, swapped = straight_ref[:, columns], swapped_ref[:, columns]
+        pair = [jnp.where(first, straight, swapped), jnp.where(first, swapped, straight)]
+        out = dot3(split(jnp.concatenate(pair, axis=0)), (g_high[m], g_low[m]), PLAIN)
+        high_ref[qrows:, columns], low_ref[qrows:, columns] = split(out)
+
+
+def condition_pair(prepared, straight, swapped, after):
+    out = jax.ShapeDtypeStruct((4 * straight.shape[0], straight.shape[1]), jnp.bfloat16)
     return pl.pallas_call(
         condition_kernel,
         out_shape=[out, out],
-        grid_spec=pltpu.PrefetchScalarGridSpec(
-            num_scalar_prefetch=1,
-            grid=(nmod,),
-            in_specs=[
-                pl.BlockSpec((qrows, modsize), lambda m, side: (0, side[0] * nmod + m)),
-                pl.BlockSpec((qrows, modsize), lambda m, side: (0, m)),
-                pl.BlockSpec((1, modsize, modsize), lambda m, side: (side[0] * nmod + m, 0, 0)),
-                ANYWHERE,
-            ],
-            out_specs=[pl.BlockSpec((2 * qrows, modsize), lambda m, side: (0, m))] * 2,
-        ),
+        in_specs=[VMEM] * 6 + [ANYWHERE],
+        out_specs=[VMEM] * 2,
         cost_estimate=FREE,
         compiler_params=pltpu.CompilerParams(vmem_limit_bytes=24 << 20),
-    )(side.reshape(1), queries, pair, inv_gram, after)
+    )(*prepared, straight, swapped, after)
 
 
 def block_scores_of(high, low, t_ref):
-    rows = t_ref.shape[0]
-    t_high, t_low = split(t_ref[...])
+    return split_scores_of(high, low, *split(t_ref[...]))
+
+
+def split_scores_of(high, low, t_high, t_low):
+    rows = t_high.shape[0]
     dot = functools.partial(
         lax.dot_general, dimension_numbers=(((1,), (1,)), ((), ())), preferred_element_type=jnp.float32
     )
@@ -186,6 +235,37 @@
     )(flip.reshape(1), *conditioned, near, *others)
 
 
+def split_kernel(given_ref, high_ref, low_ref):
+    high_ref[...], low_ref[...] = split(given_ref[...])
+
+
+def split_block(block):
+    out = jax.ShapeDtypeStruct(block.shape, jnp.bfloat16)
+    return pl.pallas_call(
+        split_kernel,
+        out_shape=[out, out],
+        in_specs=[VMEM],
+        out_specs=[VMEM] * 2,
+        cost_estimate=SPLIT_COST,
+        compiler_params=pltpu.CompilerParams(vmem_limit_bytes=16 << 20),
+    )(block)
+
+
+def split_scores_kernel(high_ref, low_ref, t_high_ref, t_low_ref, out_ref):
+    out_ref[...] = split_scores_of(high_ref[...], low_ref[...], t_high_ref[...], t_low_ref[...])
+
+
+def split_score(conditioned, halves):
+    return pl.pallas_call(
+        split_scores_kernel,
+        out_shape=jax.ShapeDtypeStruct((halves[0].shape[0], conditioned[0].shape[0]), jnp.float32),
+        in_specs=[VMEM] * 4,
+        out_specs=VMEM,
+        cost_estimate=FREE,
+        compiler_params=pltpu.CompilerParams(vmem_limit_bytes=16 << 20),
+    )(*conditioned, *halves)
+
+
 def swap_both(array, row_bit, feat_bit):
     nrow, nfeat = lax.axis_size("row"), lax.axis_size("feat")
     pairs = [
@@ -197,15 +277,15 @@
 def four_shards(queries, train_rows, inv_gram):
     qrows = queries.shape[0]
     row, feat = lax.axis_index("row"), lax.axis_index("feat")
-    side = row % 2
     q_others, t_others, t_mine = pack(queries, train_rows)
     q_pair = swap(q_others, "row", 1)
     cross = swap(t_others, "row", 3)
     far = swap(t_mine, "row", 2)
     near = swap(t_others, "row", 1)
-    conditioned = condition_pair(queries, q_pair, inv_gram, side, cross)
-
-    others = [score(conditioned, block) for block in (t_mine, far, cross)]
+    halves = split_block(cross)
+    conditioned = condition_pair(prepare(queries, inv_gram), q_pair, swap(q_pair, "grp", 1), halves[1])
+
+    others = [score(conditioned, t_mine), score(conditioned, far), split_score(conditioned, halves)]
     flip = (row ^ feat) % 2
     keep, give = last_scores(conditioned, near, others, flip)
     keep = keep + swap(give, "feat", 1)

time: 54.1 us -> 52.2 us (0.965)
  waiting for transfers between devices: 33.8 us -> 30.7 us
  starting transfers between devices: 11.1 us -> 12.3 us
    ppermute x5 -> x6, waiting for transfers between devices: 30.6 us -> 28.2 us  [send(): return lax.ppermute(array, axis, [(i, to(i)) for i in range(devices)])]
    ppermute x5 -> x6, starting transfers between devices: 7.55 us -> 8.73 us  [send(): return lax.ppermute(array, axis, [(i, to(i)) for i in range(devices)])]
    ppermute x3, waiting for transfers between devices: 3.17 us -> 2.44 us  [swap_both(): return lax.ppermute(array, ('row', 'feat'), pairs)]
    pallas_call x1 -> x4, Pallas kernels: 1.47 us -> 2.09 us  [the longest x1 0.91 us: prepare(): pl.pallas_call(prepare_kernel, out_shape=[conditioned, conditioned, gram,...]
    pallas_call x3 -> x2, Pallas kernels: 1.49 us -> 0.97 us  [score(): pl.pallas_call(scores_kernel, out_shape=jax.ShapeDtypeStruct((block.shape...]
  transfers between devices with their start and end apart: 8 -> 9, of which waited for: 6 -> 6; matrix products, arithmetic and copies ran while one was open for 0% -> 0% of each run, Pallas kernels for 5% -> 6%
where the time goes in v4:
time: 52.2 us; the launch traced here: 52 us
  waiting for transfers between devices  30.7 us (59%)
  starting transfers between devices  12.3 us (24%)
  Pallas kernels  4.79 us (9%)
  local copies, waits for them, and re-layouts  3.43 us (7%)
  other arithmetic  0.68 us (1%)
    ppermute x6, waiting for transfers between devices, send(): return lax.ppermute(array, axis, [(i, to(i)) for i in range(devices)])  28.2 us
    ppermute x6, starting transfers between devices, send(): return lax.ppermute(array, axis, [(i, to(i)) for i in range(devices)])  8.73 us
    ppermute x3, starting transfers between devices, swap_both(): return lax.ppermute(array, ('row', 'feat'), pairs)  3.55 us
    unnamed x4, local copies, waits for them, and re-layouts  3.41 us
    ppermute x3, waiting for transfers between devices, swap_both(): return lax.ppermute(array, ('row', 'feat'), pairs)  2.44 us
    pallas_call x1, Pallas kernels, pack(): pl.pallas_call(pack_kernel, out_shape=[pltpu.VMEM((rows, half), jnp.float...  1.24 us
  transfers between devices with their start and end apart: 9, of which 6 were waited for; matrix products, arithmetic and copies ran while one was open for 0% of the time, Pallas kernels for 6%

profile of v4, /device:TPU:0, one launch (start us, length us, event | category | flops | bytes accessed | tf_op | source)
XLA Modules:
  0.0 52.0 jit_solution(12262009123526094257)
XLA Ops:
  0.0 1.2 %shard_map.38 = (f32[64,1024]{1,0:T(8,128)S(1)}, f32[104,1024]{1,0:T(8,128)S(1)}, f32[104,1024]{1,0:T(8,128)S(1)}) custom-call(f32[128,2048]{1,0:T(8,128)} %q_ref.1, f32[104,2048]{1,0:T(8,128)} %t_ref.1), custom_call_target="tpu_custom_call" | custom-call | tf_op jit(solution)/shard_map/pallas_call | solution.py:104
  1.2 5.1 %collective-permute-start.2 = (f32[104,1024]{1,0:T(8,128)S(1)}, f32[104,1024]{1,0:T(8,128)S(1)}, u32[]{:S(2)}, u32[]{:S(2)}) collective-permute-start(f32[104,1024]{1,0:T(8,128)S(1)} %get-tuple-element.23), channel_id=1, source_target_pairs={{0,12},{4,8},{8,4},{12,0},{1,13},{5,9},{9,5},{13,1},{2,14},{6,10},... | collective-permute-start | bytes 1277960 | tf_op jit(solution)/shard_map/ppermute | solution.py:18
  6.4 0.0 collective-permute-start
  6.4 2.0 %collective-permute-start.3 = (f32[104,1024]{1,0:T(8,128)S(1)}, f32[104,1024]{1,0:T(8,128)S(1)}, u32[]{:S(2)}, u32[]{:S(2)}) collective-permute-start(f32[104,1024]{1,0:T(8,128)S(1)} %get-tuple-element.23), channel_id=1, source_target_pairs={{0,4},{4,0},{8,12},{12,8},{1,5},{5,1},{9,13},{13,9},{2,6},{6,2},{1... | collective-permute-start | bytes 1277960 | tf_op jit(solution)/shard_map/ppermute | solution.py:18
  8.4 0.0 collective-permute-start.4
  8.4 0.0 copy-start
  8.4 1.2 %copy-done = f32[128,2048]{1,0:T(8,128)S(1)} copy-done((f32[128,2048]{1,0:T(8,128)S(1)}, f32[128,2048]{1,0:T(8,128)}, u32[]{:S(2)}) %copy-start) | copy-done | bytes 1048600
  9.6 0.0 copy-start.1
  9.6 2.2 %copy-done.1 = f32[4,512,512]{2,1,0:T(8,128)S(1)} copy-done((f32[4,512,512]{2,1,0:T(8,128)S(1)}, f32[4,512,512]{2,1,0:T(8,128)}, u32[]{:S(2)}) %copy-start.1) | copy-done | bytes 4194328
  11.8 0.9 %shard_map.37 = (bf16[128,1024]{1,0:T(8,128)(2,1)S(1)}, bf16[128,1024]{1,0:T(8,128)(2,1)S(1)}, bf16[2,512,512]{2,1,0:T(8,128)(2,1)S(1)}, bf16[2,512,512]{2,1,0:T(8,128)(2,1)S(1)}) custom-call(f32[128,2048]{1,0:T(8,128)S(1)} %copy-done, f32[4,512,512]{2,1,0:T(8,128)S(1)} %copy-done.1), custom_call_target="tpu_custom_call" | custom-call | flops 2147483648 | bytes 8388608 | tf_op jit(solution)/shard_map/pallas_call | solution.py:151
  12.7 9.5 %collective-permute-done.straight_ref = f32[64,1024]{1,0:T(8,128)S(1)} collective-permute-done((f32[64,1024]{1,0:T(8,128)S(1)}, f32[64,1024]{1,0:T(8,128)S(1)}, u32[]{:S(2)}, u32[]{:S(2)}) %collective-permute-start) | collective-permute-done | bytes 262176 | tf_op jit(solution)/shard_map/ppermute | solution.py:18
  22.2 1.5 %collective-permute-start.1 = (f32[64,1024]{1,0:T(8,128)S(1)}, f32[64,1024]{1,0:T(8,128)S(1)}, u32[]{:S(2)}, u32[]{:S(2)}) collective-permute-start(f32[64,1024]{1,0:T(8,128)S(1)} %collective-permute-done.straight_ref), channel_id=1, source_target_pairs={{0,16},{16,0},{1,17},{17,1},{2,18},{18,2},{3,19},{19,3},{4,20},{20... | collective-permute-start | bytes 786440 | tf_op jit(solution)/shard_map/ppermute | solution.py:18
  23.7 0.0 collective-permute-done.2.given_ref
  23.7 0.1 shard_map.39
  23.8 6.3 %collective-permute-done.1.swapped_ref = f32[64,1024]{1,0:T(8,128)S(1)} collective-permute-done((f32[64,1024]{1,0:T(8,128)S(1)}, f32[64,1024]{1,0:T(8,128)S(1)}, u32[]{:S(2)}, u32[]{:S(2)}) %collective-permute-start.1) | collective-permute-done | bytes 262176 | tf_op jit(solution)/shard_map/ppermute | solution.py:18
  30.1 0.6 %shard_map.40 = (bf16[256,1024]{1,0:T(8,128)(2,1)S(1)}, bf16[256,1024]{1,0:T(8,128)(2,1)S(1)}) custom-call(bf16[128,1024]{1,0:T(8,128)(2,1)S(1)} %get-tuple-element.18.own_high, bf16[128,1024]{1,0:T(8,128)(2,1)S(1)} %get-tuple-element.19.own_low, bf16[2,512,512]{2,1,0:T(8,128)(2,1)S(1)} %get-tuple-element.20.g_high, ...), custom_call_target="tpu_custom_call" | custom-call | tf_op jit(solution)/shard_map/pallas_call | solution.py:180
  30.8 0.5 shard_map.41.own_ref
  31.3 0.5 shard_map.43.cross_ref
  31.7 11.0 %collective-permute-done.4.t_ref = f32[104,1024]{1,0:T(8,128)S(1)} collective-permute-done((f32[104,1024]{1,0:T(8,128)S(1)}, f32[104,1024]{1,0:T(8,128)S(1)}, u32[]{:S(2)}, u32[]{:S(2)}) %collective-permute-start.4) | collective-permute-done | bytes 426016 | tf_op jit(solution)/shard_map/ppermute | solution.py:18
  42.8 0.5 shard_map.42.far_ref
  43.3 0.0 collective-permute-done.3.near_ref
  43.3 0.5 shard_map.44
  43.8 0.1 collective-permute-start.5
  43.9 1.4 %collective-permute-done.5 = f32[2,104,256]{2,1,0:T(8,128)S(1)} collective-permute-done((f32[2,104,256]{2,1,0:T(8,128)S(1)}, f32[2,104,256]{2,1,0:T(8,128)S(1)}, u32[]{:S(2)}, u32[]{:S(2)}) %collective-permute-start.5) | collective-permute-done | bytes 213024 | tf_op jit(solution)/shard_map/ppermute | solution.py:18
  45.4 0.7 %collective-permute-start.7 = (f32[104,128]{1,0:T(8,128)S(1)}, f32[104,128]{1,0:T(8,128)S(1)}, u32[]{:S(2)}, u32[]{:S(2)}) collective-permute-start(f32[104,128]{1,0:T(8,128)S(1)} %get-tuple-element.33), channel_id=1, source_target_pairs={{0,6},{1,7},{2,4},{3,5},{4,2},{5,3},{6,0},{7,1},{8,14},{9,15},{10,... | collective-permute-start | bytes 159752 | tf_op jit(solution)/shard_map/ppermute | solution.py:274
  46.0 1.0 %collective-permute-start.8 = (f32[104,128]{1,0:T(8,128)S(1)}, f32[104,128]{1,0:T(8,128)S(1)}, u32[]{:S(2)}, u32[]{:S(2)}) collective-permute-start(f32[104,128]{1,0:T(8,128)S(1)} %get-tuple-element.34), channel_id=1, source_target_pairs={{0,2},{1,3},{2,0},{3,1},{4,6},{5,7},{6,4},{7,5},{8,10},{9,11},{10,... | collective-permute-start | bytes 159752 | tf_op jit(solution)/shard_map/ppermute | solution.py:274
  47.0 1.9 %collective-permute-start.6 = (f32[104,128]{1,0:T(8,128)S(1)}, f32[104,128]{1,0:T(8,128)S(1)}, u32[]{:S(2)}, u32[]{:S(2)}) collective-permute-start(f32[104,128]{1,0:T(8,128)S(1)} %slice.29), channel_id=1, source_target_pairs={{0,4},{1,5},{2,6},{3,7},{4,0},{5,1},{6,2},{7,3},{8,12},{9,13},{10,... | collective-permute-start | bytes 159752 | tf_op jit(solution)/shard_map/ppermute | solution.py:274
  48.9 1.8 %collective-permute-done.7 = f32[104,128]{1,0:T(8,128)S(1)} collective-permute-done((f32[104,128]{1,0:T(8,128)S(1)}, f32[104,128]{1,0:T(8,128)S(1)}, u32[]{:S(2)}, u32[]{:S(2)}) %collective-permute-start.7) | collective-permute-done | bytes 53280 | tf_op jit(solution)/shard_map/ppermute | solution.py:274
  50.7 0.0 collective-permute-done.8
  50.8 0.6 %collective-permute-done.6 = f32[104,128]{1,0:T(8,128)S(1)} collective-permute-done((f32[104,128]{1,0:T(8,128)S(1)}, f32[104,128]{1,0:T(8,128)S(1)}, u32[]{:S(2)}, u32[]{:S(2)}) %collective-permute-start.6) | collective-permute-done | bytes 53280 | tf_op jit(solution)/shard_map/ppermute | solution.py:274
  51.4 0.6 %fusion.2 = f32[128,104]{0,1:T(8,128)} fusion(f32[104,128]{1,0:T(8,128)S(1)} %collective-permute-done.8, f32[104,128]{1,0:T(8,128)S(1)} %collective-permute-done.7, f32[104,128]{1,0:T(8,128)S(1)} %collective-permute-done.6, f32[104,256]{1,0:T(8,128)S(1)} %get-tuple-element.31), kind=kLoop, calls=%fused_computation.5 | loop fusion | flops 39936 | bytes 266240 | tf_op jit(solution)/shard_map/transpose | solution.py:298
  (4 shorter events, 0.1 us)
Async XLA Ops:
  1.2 22.5 %collective-permute-start.2 = (f32[104,1024]{1,0:T(8,128)S(1)}, f32[104,1024]{1,0:T(8,128)S(1)}, u32[]{:S(2)}, u32[]{:S(2)}) collective-permute-start(f32[104,1024]{1,0:T(8,128)S(1)} %get-tuple-element.23), channel_id=1, source_target_pairs={{0,12},{4,8},{8,4},{12,0},{1,13},{5,9},{9,5},{13,1},{2,14},{6,10},... | collective-permute-start | bytes 1277960 | tf_op jit(solution)/shard_map/ppermute | solution.py:18
  6.4 15.8 %collective-permute-start = (f32[64,1024]{1,0:T(8,128)S(1)}, f32[64,1024]{1,0:T(8,128)S(1)}, u32[]{:S(2)}, u32[]{:S(2)}) collective-permute-start(f32[64,1024]{1,0:T(8,128)S(1)} %get-tuple-element.22), channel_id=1, source_target_pairs={{0,4},{4,0},{8,12},{12,8},{1,5},{5,1},{9,13},{13,9},{2,6},{6,2},{1... | collective-permute-start | bytes 786440 | tf_op jit(solution)/shard_map/ppermute | solution.py:18
  6.4 36.9 %collective-permute-start.3 = (f32[104,1024]{1,0:T(8,128)S(1)}, f32[104,1024]{1,0:T(8,128)S(1)}, u32[]{:S(2)}, u32[]{:S(2)}) collective-permute-start(f32[104,1024]{1,0:T(8,128)S(1)} %get-tuple-element.23), channel_id=1, source_target_pairs={{0,4},{4,0},{8,12},{12,8},{1,5},{5,1},{9,13},{13,9},{2,6},{6,2},{1... | collective-permute-start | bytes 1277960 | tf_op jit(solution)/shard_map/ppermute | solution.py:18
  8.4 34.4 %collective-permute-start.4 = (f32[104,1024]{1,0:T(8,128)S(1)}, f32[104,1024]{1,0:T(8,128)S(1)}, u32[]{:S(2)}, u32[]{:S(2)}) collective-permute-start(f32[104,1024]{1,0:T(8,128)S(1)} %get-tuple-element.27.t_ref), channel_id=1, source_target_pairs={{0,8},{4,12},{8,0},{12,4},{1,9},{5,13},{9,1},{13,5},{2,10},{6,14},... | collective-permute-start | bytes 1277960 | tf_op jit(solution)/shard_map/ppermute | solution.py:18
  8.4 1.2 %copy-start = (f32[128,2048]{1,0:T(8,128)S(1)}, f32[128,2048]{1,0:T(8,128)}, u32[]{:S(2)}) copy-start(f32[128,2048]{1,0:T(8,128)} %q_ref.1) | copy-start | bytes 3145732
  9.6 2.2 %copy-start.1 = (f32[4,512,512]{2,1,0:T(8,128)S(1)}, f32[4,512,512]{2,1,0:T(8,128)}, u32[]{:S(2)}) copy-start(f32[4,512,512]{2,1,0:T(8,128)} %gram_hbm.1) | copy-start | bytes 12582916
  22.2 7.9 %collective-permute-start.1 = (f32[64,1024]{1,0:T(8,128)S(1)}, f32[64,1024]{1,0:T(8,128)S(1)}, u32[]{:S(2)}, u32[]{:S(2)}) collective-permute-start(f32[64,1024]{1,0:T(8,128)S(1)} %collective-permute-done.straight_ref), channel_id=1, source_target_pairs={{0,16},{16,0},{1,17},{17,1},{2,18},{18,2},{3,19},{19,3},{4,20},{20... | collective-permute-start | bytes 786440 | tf_op jit(solution)/shard_map/ppermute | solution.py:18
  43.8 1.5 %collective-permute-start.5 = (f32[2,104,256]{2,1,0:T(8,128)S(1)}, f32[2,104,256]{2,1,0:T(8,128)S(1)}, u32[]{:S(2)}, u32[]{:S(2)}) collective-permute-start(f32[2,104,256]{2,1,0:T(8,128)S(1)} %get-tuple-element.30), channel_id=1, source_target_pairs={{0,1},{1,0},{2,3},{3,2},{4,5},{5,4},{6,7},{7,6},{8,9},{9,8},{10,11... | collective-permute-start | bytes 638984 | tf_op jit(solution)/shard_map/ppermute | solution.py:18
  45.4 5.4 %collective-permute-start.7 = (f32[104,128]{1,0:T(8,128)S(1)}, f32[104,128]{1,0:T(8,128)S(1)}, u32[]{:S(2)}, u32[]{:S(2)}) collective-permute-start(f32[104,128]{1,0:T(8,128)S(1)} %get-tuple-element.33), channel_id=1, source_target_pairs={{0,6},{1,7},{2,4},{3,5},{4,2},{5,3},{6,0},{7,1},{8,14},{9,15},{10,... | collective-permute-start | bytes 159752 | tf_op jit(solution)/shard_map/ppermute | solution.py:274
  46.0 4.8 %collective-permute-start.8 = (f32[104,128]{1,0:T(8,128)S(1)}, f32[104,128]{1,0:T(8,128)S(1)}, u32[]{:S(2)}, u32[]{:S(2)}) collective-permute-start(f32[104,128]{1,0:T(8,128)S(1)} %get-tuple-element.34), channel_id=1, source_target_pairs={{0,2},{1,3},{2,0},{3,1},{4,6},{5,7},{6,4},{7,5},{8,10},{9,11},{10,... | collective-permute-start | bytes 159752 | tf_op jit(solution)/shard_map/ppermute | solution.py:274
  47.0 4.4 %collective-permute-start.6 = (f32[104,128]{1,0:T(8,128)S(1)}, f32[104,128]{1,0:T(8,128)S(1)}, u32[]{:S(2)}, u32[]{:S(2)}) collective-permute-start(f32[104,128]{1,0:T(8,128)S(1)} %slice.29), channel_id=1, source_target_pairs={{0,4},{1,5},{2,6},{3,7},{4,0},{5,1},{6,2},{7,3},{8,12},{9,13},{10,... | collective-permute-start | bytes 159752 | tf_op jit(solution)/shard_map/ppermute | solution.py:274

commit v5 on v4

--- a/solution.py
+++ b/solution.py
@@ -10,6 +10,7 @@
 HIGHEST = lax.Precision.HIGHEST
 ANYWHERE = pl.BlockSpec(memory_space=pl.ANY)
 VMEM = pl.BlockSpec(memory_space=pltpu.VMEM)
+TURNS = ((3, 2, 1, 0), (2, 0, 3, 1), (1, 3, 0, 2))
 FREE = pl.CostEstimate(flops=0, bytes_accessed=0, transcendentals=0)
 
 
@@ -80,35 +81,44 @@
     return scores.transpose(1, 0, 2).reshape(qrows, -1)
 
 
-def pack_kernel(q_ref, t_ref, q_others, t_others, t_mine, sems):
-    side = lax.axis_index("row") % 2
-    qrows = q_others.shape[0]
-    rows = pl.ds(pl.multiple_of(lax.axis_index("grp") * qrows, qrows), qrows)
-    half = t_mine.shape[1]
-    mine = pl.ds(pl.multiple_of(side * half, half), half)
-    others = pl.ds(pl.multiple_of((1 - side) * half, half), half)
+def at_row(table):
+    row = lax.axis_index("row")
+    return sum(jnp.where(row == i, value, 0) for i, value in enumerate(table))
+
+
+def pack_kernel(*refs, turns, queries):
+    outs, sems = refs[-1 - len(turns) - queries : -1], refs[-1]
+    t_ref = refs[0]
+    half = t_ref.shape[1] // 2
+
+    def columns(which):
+        return pl.ds(pl.multiple_of(which * half, half), half)
+
     copies = [
-        pltpu.make_async_copy(q_ref.at[rows, others], q_others, sems.at[0]),
-        pltpu.make_async_copy(t_ref.at[:, others], t_others, sems.at[1]),
-        pltpu.make_async_copy(t_ref.at[:, mine], t_mine, sems.at[2]),
+        (t_ref.at[:, columns(at_row([target % 2 for target in TURNS[turn]]))], out) for turn, out in zip(turns, outs)
     ]
+    if queries:
+        qrows = outs[-1].shape[0]
+        rows = pl.ds(pl.multiple_of(lax.axis_index("grp") * qrows, qrows), qrows)
+        copies.append((refs[1].at[rows, columns(1 - lax.axis_index("row") % 2)], outs[-1]))
+    copies = [pltpu.make_async_copy(*pair, sems.at[i]) for i, pair in enumerate(copies)]
     for copy in copies:
         copy.start()
     for copy in copies:
         copy.wait()
 
 
-def pack(queries, train_rows):
-    qrows, half = queries.shape[0] // 2, queries.shape[1] // 2
-    trows = train_rows.shape[0]
-    return pl.pallas_call(
-        pack_kernel,
-        out_shape=[pltpu.VMEM((rows, half), jnp.float32) for rows in (qrows, trows, trows)],
-        in_specs=[ANYWHERE] * 2,
-        out_specs=[VMEM] * 3,
-        scratch_shapes=[pltpu.SemaphoreType.DMA((3,))],
-        cost_estimate=FREE,
-    )(queries, train_rows)
+def pack(turns, train_rows, *rest):
+    trows, half = train_rows.shape[0], train_rows.shape[1] // 2
+    rows = [trows for _ in turns] + [array.shape[0] // 2 for array in rest[:1]]
+    return pl.pallas_call(
+        functools.partial(pack_kernel, turns=turns, queries=len(rest[:1])),
+        out_shape=[pltpu.VMEM((size, half), jnp.float32) for size in rows],
+        in_specs=[ANYWHERE] * (1 + len(rest)),
+        out_specs=[VMEM] * len(rows),
+        scratch_shapes=[pltpu.SemaphoreType.DMA((len(rows),))],
+        cost_estimate=FREE,
+    )(train_rows, *rest)
 
 
 def split(x):
@@ -126,16 +136,18 @@
 PLAIN = (((1,), (0,)), ((), ()))
 
 
-def prepare_kernel(q_hbm, gram_hbm, high_ref, low_ref, g_high_ref, g_low_ref, q_ref, gram_ref, sems):
+def prepare_kernel(q_hbm, gram_hbm, t_hbm, high_ref, low_ref, g_high_ref, g_low_ref, t_ref, q_ref, gram_ref, sems):
     side = lax.axis_index("row") % 2
     nmod, modsize = gram_ref.shape[0], gram_ref.shape[1]
     half = nmod * modsize
-    get_q = pltpu.make_async_copy(q_hbm.at[:, pl.ds(pl.multiple_of(side * half, half), half)], q_ref, sems.at[0])
+    columns = pl.ds(pl.multiple_of(side * half, half), half)
+    get_q = pltpu.make_async_copy(q_hbm.at[:, columns], q_ref, sems.at[0])
+    get_t = pltpu.make_async_copy(t_hbm.at[:, columns], t_ref, sems.at[2])
     get_gram = pltpu.make_async_copy(gram_hbm.at[pl.ds(side * nmod, nmod)], gram_ref, sems.at[1])
-    get_q.start()
-    get_gram.start()
-    get_q.wait()
-    get_gram.wait()
+    for copy in (get_q, get_gram, get_t):
+        copy.start()
+    for copy in (get_q, get_gram, get_t):
+        copy.wait()
     for m in range(nmod):
         columns = slice(m * modsize, (m + 1) * modsize)
         gram = split(gram_ref[m])
@@ -143,24 +155,24 @@
         high_ref[:, columns], low_ref[:, columns] = split(dot3(split(q_ref[:, columns]), gram, PLAIN))
 
 
-def prepare(queries, inv_gram):
+def prepare(queries, inv_gram, train_rows):
     qrows, half = queries.shape[0], queries.shape[1] // 2
     nmod, modsize = inv_gram.shape[0] // 2, inv_gram.shape[1]
     conditioned = pltpu.VMEM((qrows, half), jnp.bfloat16)
     gram = pltpu.VMEM((nmod, modsize, modsize), jnp.bfloat16)
     return pl.pallas_call(
         prepare_kernel,
-        out_shape=[conditioned, conditioned, gram, gram],
-        in_specs=[ANYWHERE] * 2,
-        out_specs=[VMEM] * 4,
+        out_shape=[conditioned, conditioned, gram, gram, pltpu.VMEM((train_rows.shape[0], half), jnp.float32)],
+        in_specs=[ANYWHERE] * 3,
+        out_specs=[VMEM] * 5,
         scratch_shapes=[
             pltpu.VMEM((qrows, half), jnp.float32),
             pltpu.VMEM((nmod, modsize, modsize), jnp.float32),
-            pltpu.SemaphoreType.DMA((2,)),
+            pltpu.SemaphoreType.DMA((3,)),
         ],
         cost_estimate=PREPARE_COST,
         compiler_params=pltpu.CompilerParams(vmem_limit_bytes=24 << 20),
-    )(queries, inv_gram)
+    )(queries, inv_gram, train_rows)
 
 
 def condition_kernel(own_high, own_low, g_high, g_low, straight_ref, swapped_ref, after_ref, high_ref, low_ref):
@@ -215,24 +227,30 @@
     )(*conditioned, block)
 
 
-def last_kernel(flip_ref, high_ref, low_ref, near_ref, own_ref, far_ref, cross_ref, keep_ref, give_ref):
-    near = block_scores_of(high_ref[...], low_ref[...], near_ref)
-    own, far, cross = own_ref[...], far_ref[...], cross_ref[...]
-    flip = flip_ref[0] != 0
+def last_kernel(high_ref, low_ref, t_ref, own_ref, first_ref, second_ref, keep_ref, give_ref):
+    third = block_scores_of(high_ref[...], low_ref[...], t_ref)
+    own, first, second = own_ref[...], first_ref[...], second_ref[...]
+    kinds = [at_row([row ^ targets.index(row) for row in range(len(targets))]) for targets in TURNS]
+
+    def of_kind(kind):
+        return jnp.where(kinds[0] == kind, first, jnp.where(kinds[1] == kind, second, third))
+
+    near, far, cross = of_kind(1), of_kind(2), of_kind(3)
+    flip = (lax.axis_index("row") + lax.axis_index("feat")) % 2 != 0
     keep_ref[0], give_ref[0] = jnp.where(flip, near, own), jnp.where(flip, own, near)
     keep_ref[1], give_ref[1] = jnp.where(flip, cross, far), jnp.where(flip, far, cross)
 
 
-def last_scores(conditioned, near, others, flip):
+def last_scores(conditioned, third, others):
     out = jax.ShapeDtypeStruct((2, *others[0].shape), jnp.float32)
     return pl.pallas_call(
         last_kernel,
         out_shape=[out, out],
-        in_specs=[pl.BlockSpec(memory_space=pltpu.SMEM)] + [VMEM] * 6,
+        in_specs=[VMEM] * 6,
         out_specs=[VMEM] * 2,
         cost_estimate=FREE,
         compiler_params=pltpu.CompilerParams(vmem_limit_bytes=16 << 20),
-    )(flip.reshape(1), *conditioned, near, *others)
+    )(*conditioned, third, *others)
 
 
 def split_kernel(given_ref, high_ref, low_ref):
@@ -277,17 +295,18 @@
 def four_shards(queries, train_rows, inv_gram):
     qrows = queries.shape[0]
     row, feat = lax.axis_index("row"), lax.axis_index("feat")
-    q_others, t_others, t_mine = pack(queries, train_rows)
+    (t_first,) = pack((0,), train_rows)
+    *t_later, q_others = pack((1, 2), train_rows, queries, t_first)
     q_pair = swap(q_others, "row", 1)
-    cross = swap(t_others, "row", 3)
-    far = swap(t_mine, "row", 2)
-    near = swap(t_others, "row", 1)
-    halves = split_block(cross)
-    conditioned = condition_pair(prepare(queries, inv_gram), q_pair, swap(q_pair, "grp", 1), halves[1])
-
-    others = [score(conditioned, t_mine), score(conditioned, far), split_score(conditioned, halves)]
-    flip = (row ^ feat) % 2
-    keep, give = last_scores(conditioned, near, others, flip)
+    first, second, third = [
+        send(block, "row", lambda i: targets[i]) for block, targets in zip([t_first, *t_later], TURNS)
+    ]
+    halves = split_block(first)
+    *prepared, t_mine = prepare(queries, inv_gram, train_rows)
+    conditioned = condition_pair(prepared, q_pair, swap(q_pair, "grp", 1), halves[1])
+
+    others = [score(conditioned, t_mine), split_score(conditioned, halves), score(conditioned, second)]
+    keep, give = last_scores(conditioned, third, others)
     keep = keep + swap(give, "feat", 1)
     odd = ((row ^ feat) // 2) % 2 == 1
     give, keep = jnp.where(odd, keep[0], keep[1]), jnp.where(odd, keep[1], keep[0])

time: 52.2 us -> 51.6 us (0.989)
  waiting for transfers between devices: 30.7 us -> 27.6 us
  local copies, waits for them, and re-layouts: 3.43 us -> 4.59 us
  Pallas kernels: 4.79 us -> 5.86 us
    ppermute x6, waiting for transfers between devices: 28.2 us -> 25.1 us  [send(): return lax.ppermute(array, axis, [(i, to(i)) for i in range(devices)])]
    unnamed x4 -> x8, local copies, waits for them, and re-layouts: 3.41 us -> 4.57 us
    pallas_call x2 -> x3, Pallas kernels: 1.73 us -> 2.76 us  [the longest x2 2.25 us: pack(): pl.pallas_call(functools.partial(pack_kernel, turns=turns, queries=len(re...]
  transfers between devices with their start and end apart: 9 -> 9, of which waited for: 6 -> 6; matrix products, arithmetic and copies ran while one was open for 0% -> 0% of each run, Pallas kernels for 6% -> 8%
where the time goes in v5:
time: 51.6 us; the launch traced here: 51.3 us
  waiting for transfers between devices  27.6 us (53%)
  starting transfers between devices  12.4 us (24%)
  Pallas kernels  5.86 us (11%)
  local copies, waits for them, and re-layouts  4.59 us (9%)
  other arithmetic  0.68 us (1%)
    ppermute x6, waiting for transfers between devices, send(): return lax.ppermute(array, axis, [(i, to(i)) for i in range(devices)])  25.1 us
    ppermute x6, starting transfers between devices, send(): return lax.ppermute(array, axis, [(i, to(i)) for i in range(devices)])  8.85 us
    unnamed x8, local copies, waits for them, and re-layouts  4.57 us
    ppermute x3, starting transfers between devices, swap_both(): return lax.ppermute(array, ('row', 'feat'), pairs)  3.55 us
    ppermute x3, waiting for transfers between devices, swap_both(): return lax.ppermute(array, ('row', 'feat'), pairs)  2.44 us
    pallas_call x2, Pallas kernels, pack(): pl.pallas_call(functools.partial(pack_kernel, turns=turns, queries=len(re...  2.25 us
  transfers between devices with their start and end apart: 9, of which 6 were waited for; matrix products, arithmetic and copies ran while one was open for 0% of the time, Pallas kernels for 8%

profile of v5, /device:TPU:0, one launch (start us, length us, event | category | flops | bytes accessed | tf_op | source)
XLA Modules:
  0.0 51.3 jit_solution(3703832425401253148)
XLA Ops:
  0.0 1.0 %shard_map.38.refs_2_ = f32[104,1024]{1,0:T(8,128)S(1)} custom-call(f32[104,2048]{1,0:T(8,128)} %refs_0_.3), custom_call_target="tpu_custom_call" | custom-call | tf_op jit(solution)/shard_map/pallas_call | solution.py:114
  1.0 0.0 copy-start.1
  1.0 5.1 %collective-permute-start.2 = (f32[104,1024]{1,0:T(8,128)S(1)}, f32[104,1024]{1,0:T(8,128)S(1)}, u32[]{:S(2)}, u32[]{:S(2)}) collective-permute-start(f32[104,1024]{1,0:T(8,128)S(1)} %shard_map.38.refs_2_), channel_id=1, source_target_pairs={{0,12},{4,8},{8,4},{12,0},{1,13},{5,9},{9,5},{13,1},{2,14},{6,10},... | collective-permute-start | bytes 1277960 | tf_op jit(solution)/shard_map/ppermute | solution.py:19
  6.1 0.0 copy-done.1
  6.2 1.2 %shard_map.39 = (f32[104,1024]{1,0:T(8,128)S(1)}, f32[104,1024]{1,0:T(8,128)S(1)}, f32[64,1024]{1,0:T(8,128)S(1)}) custom-call(f32[104,2048]{1,0:T(8,128)} %refs_0_.3, f32[128,2048]{1,0:T(8,128)} %refs_1_.1, f32[104,1024]{1,0:T(8,128)} %copy-done.1), custom_call_target="tpu_custom_call" | custom-call | tf_op jit(solution)/shard_map/pallas_call | solution.py:114
  7.4 0.1 collective-permute-start
  7.5 1.2 %collective-permute-start.4 = (f32[104,1024]{1,0:T(8,128)S(1)}, f32[104,1024]{1,0:T(8,128)S(1)}, u32[]{:S(2)}, u32[]{:S(2)}) collective-permute-start(f32[104,1024]{1,0:T(8,128)S(1)} %get-tuple-element.30), channel_id=1, source_target_pairs={{0,8},{4,0},{8,12},{12,4},{1,9},{5,1},{9,13},{13,5},{2,10},{6,2},{... | collective-permute-start | bytes 1277960 | tf_op jit(solution)/shard_map/ppermute | solution.py:19
  8.7 0.8 %collective-permute-start.3 = (f32[104,1024]{1,0:T(8,128)S(1)}, f32[104,1024]{1,0:T(8,128)S(1)}, u32[]{:S(2)}, u32[]{:S(2)}) collective-permute-start(f32[104,1024]{1,0:T(8,128)S(1)} %get-tuple-element.27), channel_id=1, source_target_pairs={{0,4},{4,12},{8,0},{12,8},{1,5},{5,13},{9,1},{13,9},{2,6},{6,14},{... | collective-permute-start | bytes 1277960 | tf_op jit(solution)/shard_map/ppermute | solution.py:19
  9.5 0.0 copy-start
  9.6 1.2 %copy-done = f32[104,2048]{1,0:T(8,128)S(1)} copy-done((f32[104,2048]{1,0:T(8,128)S(1)}, f32[104,2048]{1,0:T(8,128)}, u32[]{:S(2)}) %copy-start) | copy-done | bytes 851992
  10.7 0.0 copy-start.2
  10.7 1.2 %copy-done.2 = f32[128,2048]{1,0:T(8,128)S(1)} copy-done((f32[128,2048]{1,0:T(8,128)S(1)}, f32[128,2048]{1,0:T(8,128)}, u32[]{:S(2)}) %copy-start.2) | copy-done | bytes 1048600
  11.9 0.0 copy-start.3
  11.9 2.2 %copy-done.3 = f32[4,512,512]{2,1,0:T(8,128)S(1)} copy-done((f32[4,512,512]{2,1,0:T(8,128)S(1)}, f32[4,512,512]{2,1,0:T(8,128)}, u32[]{:S(2)}) %copy-start.3) | copy-done | bytes 4194328
  14.1 0.9 %shard_map.37 = (bf16[128,1024]{1,0:T(8,128)(2,1)S(1)}, bf16[128,1024]{1,0:T(8,128)(2,1)S(1)}, bf16[2,512,512]{2,1,0:T(8,128)(2,1)S(1)}, bf16[2,512,512]{2,1,0:T(8,128)(2,1)S(1)}, f32[104,1024]{1,0:T(8,128)S(1)}) custom-call(f32[128,2048]{1,0:T(8,128)S(1)} %copy-done.2, f32[4,512,512]{2,1,0:T(8,128)S(1)} %copy-done.3, f32[104,2048]{1,0:T(8,128)S(1)} %copy-done), custom_call_target="tpu_custom_call" | custom-call | flops 2147483648 | bytes 8388608 | tf_op jit(solution)/shard_map/pallas_call | solution.py:163
  15.1 7.0 %collective-permute-done.straight_ref = f32[64,1024]{1,0:T(8,128)S(1)} collective-permute-done((f32[64,1024]{1,0:T(8,128)S(1)}, f32[64,1024]{1,0:T(8,128)S(1)}, u32[]{:S(2)}, u32[]{:S(2)}) %collective-permute-start) | collective-permute-done | bytes 262176 | tf_op jit(solution)/shard_map/ppermute | solution.py:19
  22.0 1.5 %collective-permute-start.1 = (f32[64,1024]{1,0:T(8,128)S(1)}, f32[64,1024]{1,0:T(8,128)S(1)}, u32[]{:S(2)}, u32[]{:S(2)}) collective-permute-start(f32[64,1024]{1,0:T(8,128)S(1)} %collective-permute-done.straight_ref), channel_id=1, source_target_pairs={{0,16},{16,0},{1,17},{17,1},{2,18},{18,2},{3,19},{19,3},{4,20},{20... | collective-permute-start | bytes 786440 | tf_op jit(solution)/shard_map/ppermute | solution.py:19
  23.6 0.0 collective-permute-done.2.given_ref
  23.6 0.1 shard_map.40
  23.6 6.3 %collective-permute-done.1.swapped_ref = f32[64,1024]{1,0:T(8,128)S(1)} collective-permute-done((f32[64,1024]{1,0:T(8,128)S(1)}, f32[64,1024]{1,0:T(8,128)S(1)}, u32[]{:S(2)}, u32[]{:S(2)}) %collective-permute-start.1) | collective-permute-done | bytes 262176 | tf_op jit(solution)/shard_map/ppermute | solution.py:19
  29.9 0.6 %shard_map.41 = (bf16[256,1024]{1,0:T(8,128)(2,1)S(1)}, bf16[256,1024]{1,0:T(8,128)(2,1)S(1)}) custom-call(bf16[128,1024]{1,0:T(8,128)(2,1)S(1)} %get-tuple-element.19.own_high, bf16[128,1024]{1,0:T(8,128)(2,1)S(1)} %get-tuple-element.20.own_low, bf16[2,512,512]{2,1,0:T(8,128)(2,1)S(1)} %get-tuple-element.21.g_high, ...), custom_call_target="tpu_custom_call" | custom-call | tf_op jit(solution)/shard_map/pallas_call | solution.py:192
  30.5 0.5 shard_map.43.first_ref
  31.0 0.5 shard_map.42.own_ref
  31.5 0.0 collective-permute-done.4.t_ref
  31.5 0.5 shard_map.44.second_ref
  32.0 10.5 %collective-permute-done.3.t_ref = f32[104,1024]{1,0:T(8,128)S(1)} collective-permute-done((f32[104,1024]{1,0:T(8,128)S(1)}, f32[104,1024]{1,0:T(8,128)S(1)}, u32[]{:S(2)}, u32[]{:S(2)}) %collective-permute-start.3) | collective-permute-done | bytes 426016 | tf_op jit(solution)/shard_map/ppermute | solution.py:19
  42.5 0.5 shard_map.45
  43.0 0.1 collective-permute-start.5
  43.1 1.4 %collective-permute-done.5 = f32[2,104,256]{2,1,0:T(8,128)S(1)} collective-permute-done((f32[2,104,256]{2,1,0:T(8,128)S(1)}, f32[2,104,256]{2,1,0:T(8,128)S(1)}, u32[]{:S(2)}, u32[]{:S(2)}) %collective-permute-start.5) | collective-permute-done | bytes 213024 | tf_op jit(solution)/shard_map/ppermute | solution.py:19
  44.6 0.7 %collective-permute-start.7 = (f32[104,128]{1,0:T(8,128)S(1)}, f32[104,128]{1,0:T(8,128)S(1)}, u32[]{:S(2)}, u32[]{:S(2)}) collective-permute-start(f32[104,128]{1,0:T(8,128)S(1)} %get-tuple-element.35), channel_id=1, source_target_pairs={{0,6},{1,7},{2,4},{3,5},{4,2},{5,3},{6,0},{7,1},{8,14},{9,15},{10,... | collective-permute-start | bytes 159752 | tf_op jit(solution)/shard_map/ppermute | solution.py:292
  45.3 1.0 %collective-permute-start.8 = (f32[104,128]{1,0:T(8,128)S(1)}, f32[104,128]{1,0:T(8,128)S(1)}, u32[]{:S(2)}, u32[]{:S(2)}) collective-permute-start(f32[104,128]{1,0:T(8,128)S(1)} %get-tuple-element.36), channel_id=1, source_target_pairs={{0,2},{1,3},{2,0},{3,1},{4,6},{5,7},{6,4},{7,5},{8,10},{9,11},{10,... | collective-permute-start | bytes 159752 | tf_op jit(solution)/shard_map/ppermute | solution.py:292
  46.3 1.9 %collective-permute-start.6 = (f32[104,128]{1,0:T(8,128)S(1)}, f32[104,128]{1,0:T(8,128)S(1)}, u32[]{:S(2)}, u32[]{:S(2)}) collective-permute-start(f32[104,128]{1,0:T(8,128)S(1)} %slice.29), channel_id=1, source_target_pairs={{0,4},{1,5},{2,6},{3,7},{4,0},{5,1},{6,2},{7,3},{8,12},{9,13},{10,... | collective-permute-start | bytes 159752 | tf_op jit(solution)/shard_map/ppermute | solution.py:292
  48.2 1.8 %collective-permute-done.7 = f32[104,128]{1,0:T(8,128)S(1)} collective-permute-done((f32[104,128]{1,0:T(8,128)S(1)}, f32[104,128]{1,0:T(8,128)S(1)}, u32[]{:S(2)}, u32[]{:S(2)}) %collective-permute-start.7) | collective-permute-done | bytes 53280 | tf_op jit(solution)/shard_map/ppermute | solution.py:292
  50.0 0.0 collective-permute-done.8
  50.0 0.6 %collective-permute-done.6 = f32[104,128]{1,0:T(8,128)S(1)} collective-permute-done((f32[104,128]{1,0:T(8,128)S(1)}, f32[104,128]{1,0:T(8,128)S(1)}, u32[]{:S(2)}, u32[]{:S(2)}) %collective-permute-start.6) | collective-permute-done | bytes 53280 | tf_op jit(solution)/shard_map/ppermute | solution.py:292
  50.6 0.6 %fusion.2 = f32[128,104]{0,1:T(8,128)} fusion(f32[104,128]{1,0:T(8,128)S(1)} %collective-permute-done.8, f32[104,128]{1,0:T(8,128)S(1)} %collective-permute-done.7, f32[104,128]{1,0:T(8,128)S(1)} %collective-permute-done.6, f32[104,256]{1,0:T(8,128)S(1)} %get-tuple-element.33), kind=kLoop, calls=%fused_computation.5 | loop fusion | flops 39936 | bytes 266240 | tf_op jit(solution)/shard_map/transpose | solution.py:317
  (4 shorter events, 0.1 us)
Async XLA Ops:
  1.0 5.1 %copy-start.1 = (f32[104,1024]{1,0:T(8,128)}, f32[104,1024]{1,0:T(8,128)S(1)}, u32[]{:S(2)}) copy-start(f32[104,1024]{1,0:T(8,128)S(1)} %shard_map.38.refs_2_) | copy-start | bytes 1277956
  1.0 22.5 %collective-permute-start.2 = (f32[104,1024]{1,0:T(8,128)S(1)}, f32[104,1024]{1,0:T(8,128)S(1)}, u32[]{:S(2)}, u32[]{:S(2)}) collective-permute-start(f32[104,1024]{1,0:T(8,128)S(1)} %shard_map.38.refs_2_), channel_id=1, source_target_pairs={{0,12},{4,8},{8,4},{12,0},{1,13},{5,9},{9,5},{13,1},{2,14},{6,10},... | collective-permute-start | bytes 1277960 | tf_op jit(solution)/shard_map/ppermute | solution.py:19
  7.4 14.6 %collective-permute-start = (f32[64,1024]{1,0:T(8,128)S(1)}, f32[64,1024]{1,0:T(8,128)S(1)}, u32[]{:S(2)}, u32[]{:S(2)}) collective-permute-start(f32[64,1024]{1,0:T(8,128)S(1)} %get-tuple-element.23), channel_id=1, source_target_pairs={{0,4},{4,0},{8,12},{12,8},{1,5},{5,1},{9,13},{13,9},{2,6},{6,2},{1... | collective-permute-start | bytes 786440 | tf_op jit(solution)/shard_map/ppermute | solution.py:19
  7.5 24.1 %collective-permute-start.4 = (f32[104,1024]{1,0:T(8,128)S(1)}, f32[104,1024]{1,0:T(8,128)S(1)}, u32[]{:S(2)}, u32[]{:S(2)}) collective-permute-start(f32[104,1024]{1,0:T(8,128)S(1)} %get-tuple-element.30), channel_id=1, source_target_pairs={{0,8},{4,0},{8,12},{12,4},{1,9},{5,1},{9,13},{13,5},{2,10},{6,2},{... | collective-permute-start | bytes 1277960 | tf_op jit(solution)/shard_map/ppermute | solution.py:19
  8.7 33.8 %collective-permute-start.3 = (f32[104,1024]{1,0:T(8,128)S(1)}, f32[104,1024]{1,0:T(8,128)S(1)}, u32[]{:S(2)}, u32[]{:S(2)}) collective-permute-start(f32[104,1024]{1,0:T(8,128)S(1)} %get-tuple-element.27), channel_id=1, source_target_pairs={{0,4},{4,12},{8,0},{12,8},{1,5},{5,13},{9,1},{13,9},{2,6},{6,14},{... | collective-permute-start | bytes 1277960 | tf_op jit(solution)/shard_map/ppermute | solution.py:19
  9.5 1.2 %copy-start = (f32[104,2048]{1,0:T(8,128)S(1)}, f32[104,2048]{1,0:T(8,128)}, u32[]{:S(2)}) copy-start(f32[104,2048]{1,0:T(8,128)} %refs_0_.3) | copy-start | bytes 2555908
  10.7 1.2 %copy-start.2 = (f32[128,2048]{1,0:T(8,128)S(1)}, f32[128,2048]{1,0:T(8,128)}, u32[]{:S(2)}) copy-start(f32[128,2048]{1,0:T(8,128)} %refs_1_.1) | copy-start | bytes 3145732
  11.9 2.2 %copy-start.3 = (f32[4,512,512]{2,1,0:T(8,128)S(1)}, f32[4,512,512]{2,1,0:T(8,128)}, u32[]{:S(2)}) copy-start(f32[4,512,512]{2,1,0:T(8,128)} %gram_hbm.1) | copy-start | bytes 12582916
  22.0 7.9 %collective-permute-start.1 = (f32[64,1024]{1,0:T(8,128)S(1)}, f32[64,1024]{1,0:T(8,128)S(1)}, u32[]{:S(2)}, u32[]{:S(2)}) collective-permute-start(f32[64,1024]{1,0:T(8,128)S(1)} %collective-permute-done.straight_ref), channel_id=1, source_target_pairs={{0,16},{16,0},{1,17},{17,1},{2,18},{18,2},{3,19},{19,3},{4,20},{20... | collective-permute-start | bytes 786440 | tf_op jit(solution)/shard_map/ppermute | solution.py:19
  43.0 1.5 %collective-permute-start.5 = (f32[2,104,256]{2,1,0:T(8,128)S(1)}, f32[2,104,256]{2,1,0:T(8,128)S(1)}, u32[]{:S(2)}, u32[]{:S(2)}) collective-permute-start(f32[2,104,256]{2,1,0:T(8,128)S(1)} %get-tuple-element.32), channel_id=1, source_target_pairs={{0,1},{1,0},{2,3},{3,2},{4,5},{5,4},{6,7},{7,6},{8,9},{9,8},{10,11... | collective-permute-start | bytes 638984 | tf_op jit(solution)/shard_map/ppermute | solution.py:19
  44.6 5.4 %collective-permute-start.7 = (f32[104,128]{1,0:T(8,128)S(1)}, f32[104,128]{1,0:T(8,128)S(1)}, u32[]{:S(2)}, u32[]{:S(2)}) collective-permute-start(f32[104,128]{1,0:T(8,128)S(1)} %get-tuple-element.35), channel_id=1, source_target_pairs={{0,6},{1,7},{2,4},{3,5},{4,2},{5,3},{6,0},{7,1},{8,14},{9,15},{10,... | collective-permute-start | bytes 159752 | tf_op jit(solution)/shard_map/ppermute | solution.py:292
  45.3 4.8 %collective-permute-start.8 = (f32[104,128]{1,0:T(8,128)S(1)}, f32[104,128]{1,0:T(8,128)S(1)}, u32[]{:S(2)}, u32[]{:S(2)}) collective-permute-start(f32[104,128]{1,0:T(8,128)S(1)} %get-tuple-element.36), channel_id=1, source_target_pairs={{0,2},{1,3},{2,0},{3,1},{4,6},{5,7},{6,4},{7,5},{8,10},{9,11},{10,... | collective-permute-start | bytes 159752 | tf_op jit(solution)/shard_map/ppermute | solution.py:292
  46.3 4.4 %collective-permute-start.6 = (f32[104,128]{1,0:T(8,128)S(1)}, f32[104,128]{1,0:T(8,128)S(1)}, u32[]{:S(2)}, u32[]{:S(2)}) collective-permute-start(f32[104,128]{1,0:T(8,128)S(1)} %slice.29), channel_id=1, source_target_pairs={{0,4},{1,5},{2,6},{3,7},{4,0},{5,1},{6,2},{7,3},{8,12},{9,13},{10,... | collective-permute-start | bytes 159752 | tf_op jit(solution)/shard_map/ppermute | solution.py:292

commit v6 on v5

--- a/solution.py
+++ b/solution.py
@@ -23,6 +23,7 @@
     return send(array, axis, lambda i: i ^ bit)
 
 
+MID_COST = pl.CostEstimate(flops=1 << 31, bytes_accessed=8 << 20, transcendentals=0)
 SPLIT_COST = pl.CostEstimate(flops=8589934592, bytes_accessed=67108864, transcendentals=0)
 PREPARE_COST = pl.CostEstimate(flops=1 << 31, bytes_accessed=8 << 20, transcendentals=0)
 
@@ -94,9 +95,10 @@
     def columns(which):
         return pl.ds(pl.multiple_of(which * half, half), half)
 
-    copies = [
-        (t_ref.at[:, columns(at_row([target % 2 for target in TURNS[turn]]))], out) for turn, out in zip(turns, outs)
-    ]
+    other = (lax.axis_index("row") + lax.axis_index("feat")) % 2 != 0
+    wanted = [at_row([target % 2 for target in targets]) for targets in TURNS]
+    wanted = [wanted[0], jnp.where(other, wanted[2], wanted[1]), jnp.where(other, wanted[1], wanted[2])]
+    copies = [(t_ref.at[:, columns(wanted[turn])], out) for turn, out in zip(turns, outs)]
     if queries:
         qrows = outs[-1].shape[0]
         rows = pl.ds(pl.multiple_of(lax.axis_index("grp") * qrows, qrows), qrows)
@@ -175,7 +177,7 @@
     )(queries, inv_gram, train_rows)
 
 
-def condition_kernel(own_high, own_low, g_high, g_low, straight_ref, swapped_ref, after_ref, high_ref, low_ref):
+def condition_kernel(own_high, own_low, g_high, g_low, straight_ref, swapped_ref, after_ref, high_ref, low_ref, whole_ref):
     qrows, modsize = own_high.shape[0], g_high.shape[1]
     first = lax.axis_index("grp") == 0
     high_ref[:qrows], low_ref[:qrows] = own_high[...], own_low[...]
@@ -185,22 +187,26 @@
         pair = [jnp.where(first, straight, swapped), jnp.where(first, swapped, straight)]
         out = dot3(split(jnp.concatenate(pair, axis=0)), (g_high[m], g_low[m]), PLAIN)
         high_ref[qrows:, columns], low_ref[qrows:, columns] = split(out)
+    whole_ref[...] = high_ref[...].astype(jnp.float32) + low_ref[...].astype(jnp.float32)
 
 
 def condition_pair(prepared, straight, swapped, after):
     out = jax.ShapeDtypeStruct((4 * straight.shape[0], straight.shape[1]), jnp.bfloat16)
     return pl.pallas_call(
         condition_kernel,
-        out_shape=[out, out],
+        out_shape=[out, out, jax.ShapeDtypeStruct(out.shape, jnp.float32)],
         in_specs=[VMEM] * 6 + [ANYWHERE],
-        out_specs=[VMEM] * 2,
+        out_specs=[VMEM] * 3,
         cost_estimate=FREE,
         compiler_params=pltpu.CompilerParams(vmem_limit_bytes=24 << 20),
     )(*prepared, straight, swapped, after)
 
 
-def block_scores_of(high, low, t_ref):
-    return split_scores_of(high, low, *split(t_ref[...]))
+def split_rows(block):
+    rows = block.shape[0]
+    if rows % 16:
+        block = jnp.concatenate([block, jnp.zeros((-rows % 16, block.shape[1]), block.dtype)], axis=0)
+    return split(block)
 
 
 def split_scores_of(high, low, t_high, t_low):
@@ -213,7 +219,7 @@
 
 
 def scores_kernel(high_ref, low_ref, t_ref, out_ref):
-    out_ref[...] = block_scores_of(high_ref[...], low_ref[...], t_ref)
+    out_ref[...] = split_scores_of(high_ref[...], low_ref[...], *split_rows(t_ref[...]))[: out_ref.shape[0]]
 
 
 def score(conditioned, block):
@@ -227,56 +233,73 @@
     )(*conditioned, block)
 
 
-def last_kernel(high_ref, low_ref, t_ref, own_ref, first_ref, second_ref, keep_ref, give_ref):
-    third = block_scores_of(high_ref[...], low_ref[...], t_ref)
-    own, first, second = own_ref[...], first_ref[...], second_ref[...]
-    kinds = [at_row([row ^ targets.index(row) for row in range(len(targets))]) for targets in TURNS]
-
-    def of_kind(kind):
-        return jnp.where(kinds[0] == kind, first, jnp.where(kinds[1] == kind, second, third))
-
-    near, far, cross = of_kind(1), of_kind(2), of_kind(3)
-    flip = (lax.axis_index("row") + lax.axis_index("feat")) % 2 != 0
-    keep_ref[0], give_ref[0] = jnp.where(flip, near, own), jnp.where(flip, own, near)
-    keep_ref[1], give_ref[1] = jnp.where(flip, cross, far), jnp.where(flip, far, cross)
-
-
-def last_scores(conditioned, third, others):
-    out = jax.ShapeDtypeStruct((2, *others[0].shape), jnp.float32)
+def last_kernel(*refs):
+    mine, other, second, third = refs[:2], refs[2:4], refs[4:6], refs[6:8]
+    early_ref, late_ref = refs[8], refs[13]
+    row, feat = lax.axis_index("row"), lax.axis_index("feat")
+    here = feat % 2 == row // 2
+
+    def scores(left, right):
+        left, right = [ref[...] for ref in left], [ref[...] for ref in right]
+        total = split_scores_of(*left, *[ref[...] for ref in third])
+        return (total + split_scores_of(*right, *[ref[...] for ref in second]))[: late_ref.shape[0]]
+
+    @pl.when(here)
+    def _():
+        late_ref[...] = scores(mine, other)
+
+    @pl.when(jnp.logical_not(here))
+    def _():
+        late_ref[...] = scores(other, mine)
+
+    late, early = late_ref[...], early_ref[...]
+    own = (row + feat + row // 2 + feat // 2) % 2 != 0
+    qrows = early.shape[1] // 2
+    keep, give = jnp.where(own, late, early), jnp.where(own, early, late)
+    refs[9][...], refs[10][...] = keep[:, :qrows], keep[:, qrows:]
+    refs[11][...], refs[12][...] = give[:, :qrows], give[:, qrows:]
+
+
+def last_scores(mine, other, second, third, early):
+    trows, queries = early.shape
+    out = jax.ShapeDtypeStruct((trows, queries // 2), jnp.float32)
     return pl.pallas_call(
         last_kernel,
-        out_shape=[out, out],
-        in_specs=[VMEM] * 6,
-        out_specs=[VMEM] * 2,
+        out_shape=[out] * 4,
+        in_specs=[VMEM] * 9,
+        out_specs=[VMEM] * 4,
+        scratch_shapes=[pltpu.VMEM((trows, queries), jnp.float32)],
         cost_estimate=FREE,
         compiler_params=pltpu.CompilerParams(vmem_limit_bytes=16 << 20),
-    )(*conditioned, third, *others)
+    )(*mine, *other, *second, *third, early)
 
 
 def split_kernel(given_ref, high_ref, low_ref):
-    high_ref[...], low_ref[...] = split(given_ref[...])
-
-
-def split_block(block):
-    out = jax.ShapeDtypeStruct(block.shape, jnp.bfloat16)
+    high_ref[...], low_ref[...] = split_rows(given_ref[...])
+
+
+def split_block(block, cost):
+    rows, columns = block.shape
+    out = jax.ShapeDtypeStruct((rows + -rows % 16, columns), jnp.bfloat16)
     return pl.pallas_call(
         split_kernel,
         out_shape=[out, out],
         in_specs=[VMEM],
         out_specs=[VMEM] * 2,
-        cost_estimate=SPLIT_COST,
+        cost_estimate=cost,
         compiler_params=pltpu.CompilerParams(vmem_limit_bytes=16 << 20),
     )(block)
 
 
 def split_scores_kernel(high_ref, low_ref, t_high_ref, t_low_ref, out_ref):
-    out_ref[...] = split_scores_of(high_ref[...], low_ref[...], t_high_ref[...], t_low_ref[...])
-
-
-def split_score(conditioned, halves):
+    out = split_scores_of(high_ref[...], low_ref[...], t_high_ref[...], t_low_ref[...])
+    out_ref[...] = out[: out_ref.shape[0]]
+
+
+def split_score(conditioned, halves, trows):
     return pl.pallas_call(
         split_scores_kernel,
-        out_shape=jax.ShapeDtypeStruct((halves[0].shape[0], conditioned[0].shape[0]), jnp.float32),
+        out_shape=jax.ShapeDtypeStruct((trows, conditioned[0].shape[0]), jnp.float32),
         in_specs=[VMEM] * 4,
         out_specs=VMEM,
         cost_estimate=FREE,
@@ -284,37 +307,45 @@
     )(*conditioned, *halves)
 
 
-def swap_both(array, row_bit, feat_bit):
+def permute(array, to):
     nrow, nfeat = lax.axis_size("row"), lax.axis_size("feat")
-    pairs = [
-        (r * nfeat + f, (r ^ row_bit) * nfeat + (f ^ feat_bit)) for r in range(nrow) for f in range(nfeat)
-    ]
+    pairs = []
+    for row in range(nrow):
+        for feat in range(nfeat):
+            to_row, to_feat = to(row, feat)
+            pairs.append((row * nfeat + feat, to_row * nfeat + to_feat))
     return lax.ppermute(array, ("row", "feat"), pairs)
 
 
+def mixed(array, turn):
+    def to(row, feat):
+        straight = (row + feat) % 2 == 0
+        return TURNS[turn if straight else 3 - turn][row], feat if straight else feat ^ 1
+
+    return permute(array, to)
+
+
 def four_shards(queries, train_rows, inv_gram):
-    qrows = queries.shape[0]
     row, feat = lax.axis_index("row"), lax.axis_index("feat")
     (t_first,) = pack((0,), train_rows)
-    *t_later, q_others = pack((1, 2), train_rows, queries, t_first)
+    t_second, t_third, q_others = pack((1, 2), train_rows, queries, t_first)
     q_pair = swap(q_others, "row", 1)
-    first, second, third = [
-        send(block, "row", lambda i: targets[i]) for block, targets in zip([t_first, *t_later], TURNS)
-    ]
-    halves = split_block(first)
+    cross = send(t_first, "row", lambda i: TURNS[0][i])
+    second, third = mixed(t_second, 1), mixed(t_third, 2)
+    halves = split_block(cross, SPLIT_COST)
     *prepared, t_mine = prepare(queries, inv_gram, train_rows)
-    conditioned = condition_pair(prepared, q_pair, swap(q_pair, "grp", 1), halves[1])
-
-    others = [score(conditioned, t_mine), split_score(conditioned, halves), score(conditioned, second)]
-    keep, give = last_scores(conditioned, third, others)
-    keep = keep + swap(give, "feat", 1)
-    odd = ((row ^ feat) // 2) % 2 == 1
-    give, keep = jnp.where(odd, keep[0], keep[1]), jnp.where(odd, keep[1], keep[0])
-    own, other = slice(0, qrows), slice(qrows, 2 * qrows)
-    there = swap_both(keep[:, other], 1, 0)
-    across = swap_both(give[:, other], 1, 2)
-    beside = swap_both(give[:, own], 0, 2)
-    return (keep[:, own] + there + across + beside).T
+    *conditioned, whole = condition_pair(prepared, q_pair, swap(q_pair, "grp", 1), halves[1])
+    other = split_block(swap(whole, "feat", 1), FREE)
+
+    own_core = (row + feat) % 2 == 0
+    own, cross = score(conditioned, t_mine), split_score(conditioned, halves, t_mine.shape[0])
+    early = jnp.where(own_core, own, cross) + swap(jnp.where(own_core, cross, own), "feat", 1)
+    second, third = split_block(second, FREE), split_block(third, SPLIT_COST)
+    keep, keep_pair, give, give_pair = last_scores(conditioned, other, second, third, early)
+    there = permute(keep_pair, lambda r, f: (r ^ 1, f))
+    across = permute(give_pair, lambda r, f: (r ^ 1, f ^ 2))
+    beside = permute(give, lambda r, f: (r, f ^ 2))
+    return (keep + there + across + beside).T
 
 
 def solution(mesh):

time: 51.6 us -> 51.3 us (level)
  waiting for transfers between devices: 27.6 us -> 26.6 us
    ppermute x6 -> x5, waiting for transfers between devices: 25.1 us -> 13.3 us  [send(): return lax.ppermute(array, axis, [(i, to(i)) for i in range(devices)])]
    ppermute x3 -> x5, waiting for transfers between devices: 2.44 us -> 13.4 us  [permute(): return lax.ppermute(array, ('row', 'feat'), pairs)]
    ppermute x3 -> x5, starting transfers between devices: 3.55 us -> 5.6 us  [permute(): return lax.ppermute(array, ('row', 'feat'), pairs)]
    ppermute x6 -> x5, starting transfers between devices: 8.85 us -> 7.34 us  [send(): return lax.ppermute(array, axis, [(i, to(i)) for i in range(devices)])]
  transfers between devices with their start and end apart: 9 -> 10, of which waited for: 6 -> 5; matrix products, arithmetic and copies ran while one was open for 0% -> 0% of each run, Pallas kernels for 8% -> 8%
where the time goes in v6:
time: 51.3 us; the launch traced here: 51 us
  waiting for transfers between devices  26.6 us (52%)
  starting transfers between devices  12.9 us (25%)
  Pallas kernels  6.02 us (12%)
  local copies, waits for them, and re-layouts  4.57 us (9%)
  other arithmetic  0.68 us (1%)
    ppermute x5, waiting for transfers between devices, permute(): return lax.ppermute(array, ('row', 'feat'), pairs)  13.4 us
    ppermute x5, waiting for transfers between devices, send(): return lax.ppermute(array, axis, [(i, to(i)) for i in range(devices)])  13.3 us
    ppermute x5, starting transfers between devices, send(): return lax.ppermute(array, axis, [(i, to(i)) for i in range(devices)])  7.34 us
    ppermute x5, starting transfers between devices, permute(): return lax.ppermute(array, ('row', 'feat'), pairs)  5.6 us
    unnamed x8, local copies, waits for them, and re-layouts  4.57 us
    pallas_call x2, Pallas kernels, pack(): pl.pallas_call(functools.partial(pack_kernel, turns=turns, queries=len(re...  2.25 us
  transfers between devices with their start and end apart: 10, of which 5 were waited for; matrix products, arithmetic and copies ran while one was open for 0% of the time, Pallas kernels for 8%

profile of v6, /device:TPU:0, one launch (start us, length us, event | category | flops | bytes accessed | tf_op | source)
XLA Modules:
  0.0 51.0 jit_solution(11742869533180811326)
XLA Ops:
  0.0 1.0 %shard_map.38.refs_2_ = f32[104,1024]{1,0:T(8,128)S(1)} custom-call(f32[104,2048]{1,0:T(8,128)} %refs_0_.3), custom_call_target="tpu_custom_call" | custom-call | tf_op jit(solution)/shard_map/pallas_call | solution.py:116
  1.0 0.0 copy-start.1
  1.0 5.1 %collective-permute-start.2 = (f32[104,1024]{1,0:T(8,128)S(1)}, f32[104,1024]{1,0:T(8,128)S(1)}, u32[]{:S(2)}, u32[]{:S(2)}) collective-permute-start(f32[104,1024]{1,0:T(8,128)S(1)} %shard_map.38.refs_2_), channel_id=1, source_target_pairs={{0,12},{4,8},{8,4},{12,0},{1,13},{5,9},{9,5},{13,1},{2,14},{6,10},... | collective-permute-start | bytes 1277960 | tf_op jit(solution)/shard_map/ppermute | solution.py:19
  6.1 0.0 copy-done.1
  6.2 1.2 %shard_map.39 = (f32[104,1024]{1,0:T(8,128)S(1)}, f32[104,1024]{1,0:T(8,128)S(1)}, f32[64,1024]{1,0:T(8,128)S(1)}) custom-call(f32[104,2048]{1,0:T(8,128)} %refs_0_.3, f32[128,2048]{1,0:T(8,128)} %refs_1_.1, f32[104,1024]{1,0:T(8,128)} %copy-done.1), custom_call_target="tpu_custom_call" | custom-call | tf_op jit(solution)/shard_map/pallas_call | solution.py:116
  7.4 0.1 collective-permute-start
  7.5 1.2 %collective-permute-start.4 = (f32[104,1024]{1,0:T(8,128)S(1)}, f32[104,1024]{1,0:T(8,128)S(1)}, u32[]{:S(2)}, u32[]{:S(2)}) collective-permute-start(f32[104,1024]{1,0:T(8,128)S(1)} %get-tuple-element.39), channel_id=1, source_target_pairs={{0,8},{1,4},{2,10},{3,6},{4,13},{5,1},{6,15},{7,3},{8,12},{9,0},{1... | collective-permute-start | bytes 1277960 | tf_op jit(solution)/shard_map/ppermute | solution.py:317
  8.7 0.8 %collective-permute-start.5 = (f32[104,1024]{1,0:T(8,128)S(1)}, f32[104,1024]{1,0:T(8,128)S(1)}, u32[]{:S(2)}, u32[]{:S(2)}) collective-permute-start(f32[104,1024]{1,0:T(8,128)S(1)} %get-tuple-element.42), channel_id=1, source_target_pairs={{0,4},{1,8},{2,6},{3,10},{4,1},{5,13},{6,3},{7,15},{8,0},{9,12},{1... | collective-permute-start | bytes 1277960 | tf_op jit(solution)/shard_map/ppermute | solution.py:317
  9.5 0.0 copy-start
  9.5 1.2 %copy-done = f32[104,2048]{1,0:T(8,128)S(1)} copy-done((f32[104,2048]{1,0:T(8,128)S(1)}, f32[104,2048]{1,0:T(8,128)}, u32[]{:S(2)}) %copy-start) | copy-done | bytes 851992
  10.7 0.0 copy-start.2
  10.7 1.2 %copy-done.2 = f32[128,2048]{1,0:T(8,128)S(1)} copy-done((f32[128,2048]{1,0:T(8,128)S(1)}, f32[128,2048]{1,0:T(8,128)}, u32[]{:S(2)}) %copy-start.2) | copy-done | bytes 1048600
  11.9 0.0 copy-start.3
  11.9 2.2 %copy-done.3 = f32[4,512,512]{2,1,0:T(8,128)S(1)} copy-done((f32[4,512,512]{2,1,0:T(8,128)S(1)}, f32[4,512,512]{2,1,0:T(8,128)}, u32[]{:S(2)}) %copy-start.3) | copy-done | bytes 4194328
  14.1 1.0 %shard_map.37 = (bf16[128,1024]{1,0:T(8,128)(2,1)S(1)}, bf16[128,1024]{1,0:T(8,128)(2,1)S(1)}, bf16[2,512,512]{2,1,0:T(8,128)(2,1)S(1)}, bf16[2,512,512]{2,1,0:T(8,128)(2,1)S(1)}, f32[104,1024]{1,0:T(8,128)S(1)}) custom-call(f32[128,2048]{1,0:T(8,128)S(1)} %copy-done.2, f32[4,512,512]{2,1,0:T(8,128)S(1)} %copy-done.3, f32[104,2048]{1,0:T(8,128)S(1)} %copy-done), custom_call_target="tpu_custom_call" | custom-call | flops 2147483648 | bytes 8388608 | tf_op jit(solution)/shard_map/pallas_call | solution.py:165
  15.0 7.0 %collective-permute-done.straight_ref = f32[64,1024]{1,0:T(8,128)S(1)} collective-permute-done((f32[64,1024]{1,0:T(8,128)S(1)}, f32[64,1024]{1,0:T(8,128)S(1)}, u32[]{:S(2)}, u32[]{:S(2)}) %collective-permute-start) | collective-permute-done | bytes 262176 | tf_op jit(solution)/shard_map/ppermute | solution.py:19
  22.0 1.5 %collective-permute-start.1 = (f32[64,1024]{1,0:T(8,128)S(1)}, f32[64,1024]{1,0:T(8,128)S(1)}, u32[]{:S(2)}, u32[]{:S(2)}) collective-permute-start(f32[64,1024]{1,0:T(8,128)S(1)} %collective-permute-done.straight_ref), channel_id=1, source_target_pairs={{0,16},{16,0},{1,17},{17,1},{2,18},{18,2},{3,19},{19,3},{4,20},{20... | collective-permute-start | bytes 786440 | tf_op jit(solution)/shard_map/ppermute | solution.py:19
  23.6 0.0 collective-permute-done.2.given_ref
  23.6 0.1 shard_map.40
  23.6 6.3 %collective-permute-done.1.swapped_ref = f32[64,1024]{1,0:T(8,128)S(1)} collective-permute-done((f32[64,1024]{1,0:T(8,128)S(1)}, f32[64,1024]{1,0:T(8,128)S(1)}, u32[]{:S(2)}, u32[]{:S(2)}) %collective-permute-start.1) | collective-permute-done | bytes 262176 | tf_op jit(solution)/shard_map/ppermute | solution.py:19
  29.9 0.7 %shard_map.41 = (bf16[256,1024]{1,0:T(8,128)(2,1)S(1)}, bf16[256,1024]{1,0:T(8,128)(2,1)S(1)}, f32[256,1024]{1,0:T(8,128)S(1)}) custom-call(bf16[128,1024]{1,0:T(8,128)(2,1)S(1)} %get-tuple-element.28.own_high, bf16[128,1024]{1,0:T(8,128)(2,1)S(1)} %get-tuple-element.29.own_low, bf16[2,512,512]{2,1,0:T(8,128)(2,1)S(1)} %get-tuple-element.30.g_high, ...), custom_call_target="tpu_custom_call" | custom-call | tf_op jit(solution)/shard_map/pallas_call | solution.py:195
  30.6 0.1 collective-permute-start.3
  30.7 0.5 shard_map.46
  31.2 0.5 shard_map.45
  31.6 0.6 %collective-permute-start.6 = (f32[104,256]{1,0:T(8,128)S(1)}, f32[104,256]{1,0:T(8,128)S(1)}, u32[]{:S(2)}, u32[]{:S(2)}) collective-permute-start(f32[104,256]{1,0:T(8,128)S(1)} %broadcast_select_fusion), channel_id=1, source_target_pairs={{0,1},{1,0},{2,3},{3,2},{4,5},{5,4},{6,7},{7,6},{8,9},{9,8},{10,11... | collective-permute-start | bytes 319496 | tf_op jit(solution)/shard_map/ppermute | solution.py:19
  32.2 10.3 %collective-permute-done.5.given_ref = f32[104,1024]{1,0:T(8,128)S(1)} collective-permute-done((f32[104,1024]{1,0:T(8,128)S(1)}, f32[104,1024]{1,0:T(8,128)S(1)}, u32[]{:S(2)}, u32[]{:S(2)}) %collective-permute-start.5) | collective-permute-done | bytes 426016 | tf_op jit(solution)/shard_map/ppermute | solution.py:317
  42.5 0.1 shard_map.44
  42.6 0.0 collective-permute-done.4.given_ref
  42.6 0.1 shard_map.43
  42.7 0.0 collective-permute-done.6
  42.8 0.0 collective-permute-done.3.given_ref
  42.8 0.1 shard_map.42
  42.9 0.8 %shard_map.47 = (f32[104,128]{1,0:T(8,128)S(1)}, f32[104,128]{1,0:T(8,128)S(1)}, f32[104,128]{1,0:T(8,128)S(1)}, f32[104,128]{1,0:T(8,128)S(1)}) custom-call(bf16[256,1024]{1,0:T(8,128)(2,1)S(1)} %get-tuple-element.34.high_ref.refs_0_, bf16[256,1024]{1,0:T(8,128)(2,1)S(1)} %get-tuple-element.35.low_ref.refs_1_, ...), custom_call_target="tpu_custom_call" | custom-call | tf_op jit(solution)/shard_map/pallas_call | solution.py:266
  43.8 1.6 %collective-permute-start.9 = (f32[104,128]{1,0:T(8,128)S(1)}, f32[104,128]{1,0:T(8,128)S(1)}, u32[]{:S(2)}, u32[]{:S(2)}) collective-permute-start(f32[104,128]{1,0:T(8,128)S(1)} %get-tuple-element.50), channel_id=1, source_target_pairs={{0,2},{1,3},{2,0},{3,1},{4,6},{5,7},{6,4},{7,5},{8,10},{9,11},{10,... | collective-permute-start | bytes 159752 | tf_op jit(solution)/shard_map/ppermute | solution.py:317
  45.3 0.0 collective-permute-start.8
  45.3 2.0 %collective-permute-start.7 = (f32[104,128]{1,0:T(8,128)S(1)}, f32[104,128]{1,0:T(8,128)S(1)}, u32[]{:S(2)}, u32[]{:S(2)}) collective-permute-start(f32[104,128]{1,0:T(8,128)S(1)} %get-tuple-element.48), channel_id=1, source_target_pairs={{0,4},{1,5},{2,6},{3,7},{4,0},{5,1},{6,2},{7,3},{8,12},{9,13},{10,... | collective-permute-start | bytes 159752 | tf_op jit(solution)/shard_map/ppermute | solution.py:317
  47.3 0.6 %collective-permute-done.9 = f32[104,128]{1,0:T(8,128)S(1)} collective-permute-done((f32[104,128]{1,0:T(8,128)S(1)}, f32[104,128]{1,0:T(8,128)S(1)}, u32[]{:S(2)}, u32[]{:S(2)}) %collective-permute-start.9) | collective-permute-done | bytes 53280 | tf_op jit(solution)/shard_map/ppermute | solution.py:317
  48.0 2.4 %collective-permute-done.8 = f32[104,128]{1,0:T(8,128)S(1)} collective-permute-done((f32[104,128]{1,0:T(8,128)S(1)}, f32[104,128]{1,0:T(8,128)S(1)}, u32[]{:S(2)}, u32[]{:S(2)}) %collective-permute-start.8) | collective-permute-done | bytes 53280 | tf_op jit(solution)/shard_map/ppermute | solution.py:317
  50.3 0.0 collective-permute-done.7
  50.3 0.6 %add_bitcast_fusion = f32[128,104]{0,1:T(8,128)} fusion(f32[104,128]{1,0:T(8,128)S(1)} %collective-permute-done.9, f32[104,128]{1,0:T(8,128)S(1)} %collective-permute-done.8, f32[104,128]{1,0:T(8,128)S(1)} %get-tuple-element.47, f32[104,128]{1,0:T(8,128)S(1)} %collective-permute-done.7), kind=kLoop, calls=%fused_computation.1 | loop fusion | flops 39936 | bytes 266240 | tf_op jit(solution)/shard_map/transpose | solution.py:348
  (2 shorter events, 0.0 us)
Async XLA Ops:
  1.0 5.1 %copy-start.1 = (f32[104,1024]{1,0:T(8,128)}, f32[104,1024]{1,0:T(8,128)S(1)}, u32[]{:S(2)}) copy-start(f32[104,1024]{1,0:T(8,128)S(1)} %shard_map.38.refs_2_) | copy-start | bytes 1277956
  1.0 22.5 %collective-permute-start.2 = (f32[104,1024]{1,0:T(8,128)S(1)}, f32[104,1024]{1,0:T(8,128)S(1)}, u32[]{:S(2)}, u32[]{:S(2)}) collective-permute-start(f32[104,1024]{1,0:T(8,128)S(1)} %shard_map.38.refs_2_), channel_id=1, source_target_pairs={{0,12},{4,8},{8,4},{12,0},{1,13},{5,9},{9,5},{13,1},{2,14},{6,10},... | collective-permute-start | bytes 1277960 | tf_op jit(solution)/shard_map/ppermute | solution.py:19
  7.4 14.6 %collective-permute-start = (f32[64,1024]{1,0:T(8,128)S(1)}, f32[64,1024]{1,0:T(8,128)S(1)}, u32[]{:S(2)}, u32[]{:S(2)}) collective-permute-start(f32[64,1024]{1,0:T(8,128)S(1)} %get-tuple-element.32), channel_id=1, source_target_pairs={{0,4},{4,0},{8,12},{12,8},{1,5},{5,1},{9,13},{13,9},{2,6},{6,2},{1... | collective-permute-start | bytes 786440 | tf_op jit(solution)/shard_map/ppermute | solution.py:19
  7.5 35.2 %collective-permute-start.4 = (f32[104,1024]{1,0:T(8,128)S(1)}, f32[104,1024]{1,0:T(8,128)S(1)}, u32[]{:S(2)}, u32[]{:S(2)}) collective-permute-start(f32[104,1024]{1,0:T(8,128)S(1)} %get-tuple-element.39), channel_id=1, source_target_pairs={{0,8},{1,4},{2,10},{3,6},{4,13},{5,1},{6,15},{7,3},{8,12},{9,0},{1... | collective-permute-start | bytes 1277960 | tf_op jit(solution)/shard_map/ppermute | solution.py:317
  8.7 33.8 %collective-permute-start.5 = (f32[104,1024]{1,0:T(8,128)S(1)}, f32[104,1024]{1,0:T(8,128)S(1)}, u32[]{:S(2)}, u32[]{:S(2)}) collective-permute-start(f32[104,1024]{1,0:T(8,128)S(1)} %get-tuple-element.42), channel_id=1, source_target_pairs={{0,4},{1,8},{2,6},{3,10},{4,1},{5,13},{6,3},{7,15},{8,0},{9,12},{1... | collective-permute-start | bytes 1277960 | tf_op jit(solution)/shard_map/ppermute | solution.py:317
  9.5 1.2 %copy-start = (f32[104,2048]{1,0:T(8,128)S(1)}, f32[104,2048]{1,0:T(8,128)}, u32[]{:S(2)}) copy-start(f32[104,2048]{1,0:T(8,128)} %refs_0_.3) | copy-start | bytes 2555908
  10.7 1.2 %copy-start.2 = (f32[128,2048]{1,0:T(8,128)S(1)}, f32[128,2048]{1,0:T(8,128)}, u32[]{:S(2)}) copy-start(f32[128,2048]{1,0:T(8,128)} %refs_1_.1) | copy-start | bytes 3145732
  11.9 2.2 %copy-start.3 = (f32[4,512,512]{2,1,0:T(8,128)S(1)}, f32[4,512,512]{2,1,0:T(8,128)}, u32[]{:S(2)}) copy-start(f32[4,512,512]{2,1,0:T(8,128)} %gram_hbm.1) | copy-start | bytes 12582916
  22.0 7.9 %collective-permute-start.1 = (f32[64,1024]{1,0:T(8,128)S(1)}, f32[64,1024]{1,0:T(8,128)S(1)}, u32[]{:S(2)}, u32[]{:S(2)}) collective-permute-start(f32[64,1024]{1,0:T(8,128)S(1)} %collective-permute-done.straight_ref), channel_id=1, source_target_pairs={{0,16},{16,0},{1,17},{17,1},{2,18},{18,2},{3,19},{19,3},{4,20},{20... | collective-permute-start | bytes 786440 | tf_op jit(solution)/shard_map/ppermute | solution.py:19
  30.6 12.1 %collective-permute-start.3 = (f32[256,1024]{1,0:T(8,128)S(1)}, f32[256,1024]{1,0:T(8,128)S(1)}, u32[]{:S(2)}, u32[]{:S(2)}) collective-permute-start(f32[256,1024]{1,0:T(8,128)S(1)} %get-tuple-element.36), channel_id=1, source_target_pairs={{0,1},{1,0},{2,3},{3,2},{4,5},{5,4},{6,7},{7,6},{8,9},{9,8},{10,11... | collective-permute-start | bytes 3145736 | tf_op jit(solution)/shard_map/ppermute | solution.py:19
  31.6 11.1 %collective-permute-start.6 = (f32[104,256]{1,0:T(8,128)S(1)}, f32[104,256]{1,0:T(8,128)S(1)}, u32[]{:S(2)}, u32[]{:S(2)}) collective-permute-start(f32[104,256]{1,0:T(8,128)S(1)} %broadcast_select_fusion), channel_id=1, source_target_pairs={{0,1},{1,0},{2,3},{3,2},{4,5},{5,4},{6,7},{7,6},{8,9},{9,8},{10,11... | collective-permute-start | bytes 319496 | tf_op jit(solution)/shard_map/ppermute | solution.py:19
  43.8 4.2 %collective-permute-start.9 = (f32[104,128]{1,0:T(8,128)S(1)}, f32[104,128]{1,0:T(8,128)S(1)}, u32[]{:S(2)}, u32[]{:S(2)}) collective-permute-start(f32[104,128]{1,0:T(8,128)S(1)} %get-tuple-element.50), channel_id=1, source_target_pairs={{0,2},{1,3},{2,0},{3,1},{4,6},{5,7},{6,4},{7,5},{8,10},{9,11},{10,... | collective-permute-start | bytes 159752 | tf_op jit(solution)/shard_map/ppermute | solution.py:317
  45.3 5.0 %collective-permute-start.8 = (f32[104,128]{1,0:T(8,128)S(1)}, f32[104,128]{1,0:T(8,128)S(1)}, u32[]{:S(2)}, u32[]{:S(2)}) collective-permute-start(f32[104,128]{1,0:T(8,128)S(1)} %get-tuple-element.49), channel_id=1, source_target_pairs={{0,6},{1,7},{2,4},{3,5},{4,2},{5,3},{6,0},{7,1},{8,14},{9,15},{10,... | collective-permute-start | bytes 159752 | tf_op jit(solution)/shard_map/ppermute | solution.py:317
  45.3 5.0 %collective-permute-start.7 = (f32[104,128]{1,0:T(8,128)S(1)}, f32[104,128]{1,0:T(8,128)S(1)}, u32[]{:S(2)}, u32[]{:S(2)}) collective-permute-start(f32[104,128]{1,0:T(8,128)S(1)} %get-tuple-element.48), channel_id=1, source_target_pairs={{0,4},{1,5},{2,6},{3,7},{4,0},{5,1},{6,2},{7,3},{8,12},{9,13},{10,... | collective-permute-start | bytes 159752 | tf_op jit(solution)/shard_map/ppermute | solution.py:317

commit v7 on v6

--- a/solution.py
+++ b/solution.py
@@ -234,15 +234,15 @@
 
 
 def last_kernel(*refs):
-    mine, other, second, third = refs[:2], refs[2:4], refs[4:6], refs[6:8]
-    early_ref, late_ref = refs[8], refs[13]
+    mine, other, second_ref, third = refs[:2], refs[2:4], refs[4], refs[5:7]
+    early_ref, late_ref = refs[7], refs[12]
     row, feat = lax.axis_index("row"), lax.axis_index("feat")
     here = feat % 2 == row // 2
 
     def scores(left, right):
         left, right = [ref[...] for ref in left], [ref[...] for ref in right]
         total = split_scores_of(*left, *[ref[...] for ref in third])
-        return (total + split_scores_of(*right, *[ref[...] for ref in second]))[: late_ref.shape[0]]
+        return (total + split_scores_of(*right, *split_rows(second_ref[...])))[: late_ref.shape[0]]
 
     @pl.when(here)
     def _():
@@ -256,8 +256,8 @@
     own = (row + feat + row // 2 + feat // 2) % 2 != 0
     qrows = early.shape[1] // 2
     keep, give = jnp.where(own, late, early), jnp.where(own, early, late)
-    refs[9][...], refs[10][...] = keep[:, :qrows], keep[:, qrows:]
-    refs[11][...], refs[12][...] = give[:, :qrows], give[:, qrows:]
+    refs[8][...], refs[9][...] = keep[:, :qrows], keep[:, qrows:]
+    refs[10][...], refs[11][...] = give[:, :qrows], give[:, qrows:]
 
 
 def last_scores(mine, other, second, third, early):
@@ -266,12 +266,12 @@
     return pl.pallas_call(
         last_kernel,
         out_shape=[out] * 4,
-        in_specs=[VMEM] * 9,
+        in_specs=[VMEM] * 8,
         out_specs=[VMEM] * 4,
         scratch_shapes=[pltpu.VMEM((trows, queries), jnp.float32)],
         cost_estimate=FREE,
         compiler_params=pltpu.CompilerParams(vmem_limit_bytes=16 << 20),
-    )(*mine, *other, *second, *third, early)
+    )(*mine, *other, second, *third, early)
 
 
 def split_kernel(given_ref, high_ref, low_ref):
@@ -340,7 +340,7 @@
     own_core = (row + feat) % 2 == 0
     own, cross = score(conditioned, t_mine), split_score(conditioned, halves, t_mine.shape[0])
     early = jnp.where(own_core, own, cross) + swap(jnp.where(own_core, cross, own), "feat", 1)
-    second, third = split_block(second, FREE), split_block(third, SPLIT_COST)
+    third = split_block(third, SPLIT_COST)
     keep, keep_pair, give, give_pair = last_scores(conditioned, other, second, third, early)
     there = permute(keep_pair, lambda r, f: (r ^ 1, f))
     across = permute(give_pair, lambda r, f: (r ^ 1, f ^ 2))

time: 51.3 us -> 51.2 us (level)
  no operation moved by 1% of the time
where the time goes in v7:
time: 51.2 us; the launch traced here: 50.9 us
  waiting for transfers between devices  26.6 us (52%)
  starting transfers between devices  12.9 us (25%)
  Pallas kernels  5.95 us (12%)
  local copies, waits for them, and re-layouts  4.57 us (9%)
  other arithmetic  0.68 us (1%)
    ppermute x5, waiting for transfers between devices, permute(): return lax.ppermute(array, ('row', 'feat'), pairs)  13.4 us
    ppermute x5, waiting for transfers between devices, send(): return lax.ppermute(array, axis, [(i, to(i)) for i in range(devices)])  13.3 us
    ppermute x5, starting transfers between devices, send(): return lax.ppermute(array, axis, [(i, to(i)) for i in range(devices)])  7.34 us
    ppermute x5, starting transfers between devices, permute(): return lax.ppermute(array, ('row', 'feat'), pairs)  5.6 us
    unnamed x8, local copies, waits for them, and re-layouts  4.57 us
    pallas_call x2, Pallas kernels, pack(): pl.pallas_call(functools.partial(pack_kernel, turns=turns, queries=len(re...  2.25 us
  transfers between devices with their start and end apart: 10, of which 5 were waited for; matrix products, arithmetic and copies ran while one was open for 0% of the time, Pallas kernels for 8%

profile of v7, /device:TPU:0, one launch (start us, length us, event | category | flops | bytes accessed | tf_op | source)
XLA Modules:
  0.0 50.9 jit_solution(1364598927706307825)
XLA Ops:
  0.0 1.0 %shard_map.38.refs_2_ = f32[104,1024]{1,0:T(8,128)S(1)} custom-call(f32[104,2048]{1,0:T(8,128)} %refs_0_.3), custom_call_target="tpu_custom_call" | custom-call | tf_op jit(solution)/shard_map/pallas_call | solution.py:116
  1.0 0.0 copy-start.1
  1.0 5.1 %collective-permute-start.2 = (f32[104,1024]{1,0:T(8,128)S(1)}, f32[104,1024]{1,0:T(8,128)S(1)}, u32[]{:S(2)}, u32[]{:S(2)}) collective-permute-start(f32[104,1024]{1,0:T(8,128)S(1)} %shard_map.38.refs_2_), channel_id=1, source_target_pairs={{0,12},{4,8},{8,4},{12,0},{1,13},{5,9},{9,5},{13,1},{2,14},{6,10},... | collective-permute-start | bytes 1277960 | tf_op jit(solution)/shard_map/ppermute | solution.py:19
  6.1 0.0 copy-done.1
  6.2 1.2 %shard_map.39 = (f32[104,1024]{1,0:T(8,128)S(1)}, f32[104,1024]{1,0:T(8,128)S(1)}, f32[64,1024]{1,0:T(8,128)S(1)}) custom-call(f32[104,2048]{1,0:T(8,128)} %refs_0_.3, f32[128,2048]{1,0:T(8,128)} %refs_1_.1, f32[104,1024]{1,0:T(8,128)} %copy-done.1), custom_call_target="tpu_custom_call" | custom-call | tf_op jit(solution)/shard_map/pallas_call | solution.py:116
  7.4 0.1 collective-permute-start
  7.5 1.2 %collective-permute-start.4 = (f32[104,1024]{1,0:T(8,128)S(1)}, f32[104,1024]{1,0:T(8,128)S(1)}, u32[]{:S(2)}, u32[]{:S(2)}) collective-permute-start(f32[104,1024]{1,0:T(8,128)S(1)} %get-tuple-element.37), channel_id=1, source_target_pairs={{0,8},{1,4},{2,10},{3,6},{4,13},{5,1},{6,15},{7,3},{8,12},{9,0},{1... | collective-permute-start | bytes 1277960 | tf_op jit(solution)/shard_map/ppermute | solution.py:317
  8.7 0.8 %collective-permute-start.5 = (f32[104,1024]{1,0:T(8,128)S(1)}, f32[104,1024]{1,0:T(8,128)S(1)}, u32[]{:S(2)}, u32[]{:S(2)}) collective-permute-start(f32[104,1024]{1,0:T(8,128)S(1)} %get-tuple-element.38), channel_id=1, source_target_pairs={{0,4},{1,8},{2,6},{3,10},{4,1},{5,13},{6,3},{7,15},{8,0},{9,12},{1... | collective-permute-start | bytes 1277960 | tf_op jit(solution)/shard_map/ppermute | solution.py:317
  9.5 0.0 copy-start
  9.5 1.2 %copy-done = f32[104,2048]{1,0:T(8,128)S(1)} copy-done((f32[104,2048]{1,0:T(8,128)S(1)}, f32[104,2048]{1,0:T(8,128)}, u32[]{:S(2)}) %copy-start) | copy-done | bytes 851992
  10.7 0.0 copy-start.2
  10.7 1.2 %copy-done.2 = f32[128,2048]{1,0:T(8,128)S(1)} copy-done((f32[128,2048]{1,0:T(8,128)S(1)}, f32[128,2048]{1,0:T(8,128)}, u32[]{:S(2)}) %copy-start.2) | copy-done | bytes 1048600
  11.9 0.0 copy-start.3
  11.9 2.2 %copy-done.3 = f32[4,512,512]{2,1,0:T(8,128)S(1)} copy-done((f32[4,512,512]{2,1,0:T(8,128)S(1)}, f32[4,512,512]{2,1,0:T(8,128)}, u32[]{:S(2)}) %copy-start.3) | copy-done | bytes 4194328
  14.1 1.0 %shard_map.37 = (bf16[128,1024]{1,0:T(8,128)(2,1)S(1)}, bf16[128,1024]{1,0:T(8,128)(2,1)S(1)}, bf16[2,512,512]{2,1,0:T(8,128)(2,1)S(1)}, bf16[2,512,512]{2,1,0:T(8,128)(2,1)S(1)}, f32[104,1024]{1,0:T(8,128)S(1)}) custom-call(f32[128,2048]{1,0:T(8,128)S(1)} %copy-done.2, f32[4,512,512]{2,1,0:T(8,128)S(1)} %copy-done.3, f32[104,2048]{1,0:T(8,128)S(1)} %copy-done), custom_call_target="tpu_custom_call" | custom-call | flops 2147483648 | bytes 8388608 | tf_op jit(solution)/shard_map/pallas_call | solution.py:165
  15.0 7.0 %collective-permute-done.straight_ref = f32[64,1024]{1,0:T(8,128)S(1)} collective-permute-done((f32[64,1024]{1,0:T(8,128)S(1)}, f32[64,1024]{1,0:T(8,128)S(1)}, u32[]{:S(2)}, u32[]{:S(2)}) %collective-permute-start) | collective-permute-done | bytes 262176 | tf_op jit(solution)/shard_map/ppermute | solution.py:19
  22.0 1.5 %collective-permute-start.1 = (f32[64,1024]{1,0:T(8,128)S(1)}, f32[64,1024]{1,0:T(8,128)S(1)}, u32[]{:S(2)}, u32[]{:S(2)}) collective-permute-start(f32[64,1024]{1,0:T(8,128)S(1)} %collective-permute-done.straight_ref), channel_id=1, source_target_pairs={{0,16},{16,0},{1,17},{17,1},{2,18},{18,2},{3,19},{19,3},{4,20},{20... | collective-permute-start | bytes 786440 | tf_op jit(solution)/shard_map/ppermute | solution.py:19
  23.6 0.0 collective-permute-done.2.given_ref
  23.6 0.1 shard_map.40
  23.6 6.3 %collective-permute-done.1.swapped_ref = f32[64,1024]{1,0:T(8,128)S(1)} collective-permute-done((f32[64,1024]{1,0:T(8,128)S(1)}, f32[64,1024]{1,0:T(8,128)S(1)}, u32[]{:S(2)}, u32[]{:S(2)}) %collective-permute-start.1) | collective-permute-done | bytes 262176 | tf_op jit(solution)/shard_map/ppermute | solution.py:19
  29.9 0.7 %shard_map.41 = (bf16[256,1024]{1,0:T(8,128)(2,1)S(1)}, bf16[256,1024]{1,0:T(8,128)(2,1)S(1)}, f32[256,1024]{1,0:T(8,128)S(1)}) custom-call(bf16[128,1024]{1,0:T(8,128)(2,1)S(1)} %get-tuple-element.26.own_high, bf16[128,1024]{1,0:T(8,128)(2,1)S(1)} %get-tuple-element.27.own_low, bf16[2,512,512]{2,1,0:T(8,128)(2,1)S(1)} %get-tuple-element.28.g_high, ...), custom_call_target="tpu_custom_call" | custom-call | tf_op jit(solution)/shard_map/pallas_call | solution.py:195
  30.6 0.1 collective-permute-start.3
  30.7 0.5 shard_map.45
  31.2 0.5 shard_map.44
  31.6 0.6 %collective-permute-start.6 = (f32[104,256]{1,0:T(8,128)S(1)}, f32[104,256]{1,0:T(8,128)S(1)}, u32[]{:S(2)}, u32[]{:S(2)}) collective-permute-start(f32[104,256]{1,0:T(8,128)S(1)} %broadcast_select_fusion), channel_id=1, source_target_pairs={{0,1},{1,0},{2,3},{3,2},{4,5},{5,4},{6,7},{7,6},{8,9},{9,8},{10,11... | collective-permute-start | bytes 319496 | tf_op jit(solution)/shard_map/ppermute | solution.py:19
  32.2 10.3 %collective-permute-done.5.given_ref = f32[104,1024]{1,0:T(8,128)S(1)} collective-permute-done((f32[104,1024]{1,0:T(8,128)S(1)}, f32[104,1024]{1,0:T(8,128)S(1)}, u32[]{:S(2)}, u32[]{:S(2)}) %collective-permute-start.5) | collective-permute-done | bytes 426016 | tf_op jit(solution)/shard_map/ppermute | solution.py:317
  42.5 0.1 shard_map.43
  42.6 0.0 collective-permute-done.6
  42.7 0.0 collective-permute-done.3.given_ref
  42.7 0.1 shard_map.42
  42.8 0.0 collective-permute-done.4.refs_4_
  42.8 0.8 %shard_map.46 = (f32[104,128]{1,0:T(8,128)S(1)}, f32[104,128]{1,0:T(8,128)S(1)}, f32[104,128]{1,0:T(8,128)S(1)}, f32[104,128]{1,0:T(8,128)S(1)}) custom-call(bf16[256,1024]{1,0:T(8,128)(2,1)S(1)} %get-tuple-element.32.high_ref.refs_0_, bf16[256,1024]{1,0:T(8,128)(2,1)S(1)} %get-tuple-element.33.low_ref.refs_1_, ...), custom_call_target="tpu_custom_call" | custom-call | tf_op jit(solution)/shard_map/pallas_call | solution.py:266
  43.7 1.6 %collective-permute-start.9 = (f32[104,128]{1,0:T(8,128)S(1)}, f32[104,128]{1,0:T(8,128)S(1)}, u32[]{:S(2)}, u32[]{:S(2)}) collective-permute-start(f32[104,128]{1,0:T(8,128)S(1)} %get-tuple-element.46), channel_id=1, source_target_pairs={{0,2},{1,3},{2,0},{3,1},{4,6},{5,7},{6,4},{7,5},{8,10},{9,11},{10,... | collective-permute-start | bytes 159752 | tf_op jit(solution)/shard_map/ppermute | solution.py:317
  45.2 0.0 collective-permute-start.8
  45.2 2.0 %collective-permute-start.7 = (f32[104,128]{1,0:T(8,128)S(1)}, f32[104,128]{1,0:T(8,128)S(1)}, u32[]{:S(2)}, u32[]{:S(2)}) collective-permute-start(f32[104,128]{1,0:T(8,128)S(1)} %get-tuple-element.44), channel_id=1, source_target_pairs={{0,4},{1,5},{2,6},{3,7},{4,0},{5,1},{6,2},{7,3},{8,12},{9,13},{10,... | collective-permute-start | bytes 159752 | tf_op jit(solution)/shard_map/ppermute | solution.py:317
  47.2 0.6 %collective-permute-done.9 = f32[104,128]{1,0:T(8,128)S(1)} collective-permute-done((f32[104,128]{1,0:T(8,128)S(1)}, f32[104,128]{1,0:T(8,128)S(1)}, u32[]{:S(2)}, u32[]{:S(2)}) %collective-permute-start.9) | collective-permute-done | bytes 53280 | tf_op jit(solution)/shard_map/ppermute | solution.py:317
  47.9 2.4 %collective-permute-done.8 = f32[104,128]{1,0:T(8,128)S(1)} collective-permute-done((f32[104,128]{1,0:T(8,128)S(1)}, f32[104,128]{1,0:T(8,128)S(1)}, u32[]{:S(2)}, u32[]{:S(2)}) %collective-permute-start.8) | collective-permute-done | bytes 53280 | tf_op jit(solution)/shard_map/ppermute | solution.py:317
  50.3 0.0 collective-permute-done.7
  50.3 0.6 %add_bitcast_fusion = f32[128,104]{0,1:T(8,128)} fusion(f32[104,128]{1,0:T(8,128)S(1)} %collective-permute-done.9, f32[104,128]{1,0:T(8,128)S(1)} %collective-permute-done.8, f32[104,128]{1,0:T(8,128)S(1)} %get-tuple-element.43, f32[104,128]{1,0:T(8,128)S(1)} %collective-permute-done.7), kind=kLoop, calls=%fused_computation.1 | loop fusion | flops 39936 | bytes 266240 | tf_op jit(solution)/shard_map/transpose | solution.py:348
  (2 shorter events, 0.0 us)
Async XLA Ops:
  1.0 5.1 %copy-start.1 = (f32[104,1024]{1,0:T(8,128)}, f32[104,1024]{1,0:T(8,128)S(1)}, u32[]{:S(2)}) copy-start(f32[104,1024]{1,0:T(8,128)S(1)} %shard_map.38.refs_2_) | copy-start | bytes 1277956
  1.0 22.5 %collective-permute-start.2 = (f32[104,1024]{1,0:T(8,128)S(1)}, f32[104,1024]{1,0:T(8,128)S(1)}, u32[]{:S(2)}, u32[]{:S(2)}) collective-permute-start(f32[104,1024]{1,0:T(8,128)S(1)} %shard_map.38.refs_2_), channel_id=1, source_target_pairs={{0,12},{4,8},{8,4},{12,0},{1,13},{5,9},{9,5},{13,1},{2,14},{6,10},... | collective-permute-start | bytes 1277960 | tf_op jit(solution)/shard_map/ppermute | solution.py:19
  7.4 14.6 %collective-permute-start = (f32[64,1024]{1,0:T(8,128)S(1)}, f32[64,1024]{1,0:T(8,128)S(1)}, u32[]{:S(2)}, u32[]{:S(2)}) collective-permute-start(f32[64,1024]{1,0:T(8,128)S(1)} %get-tuple-element.30), channel_id=1, source_target_pairs={{0,4},{4,0},{8,12},{12,8},{1,5},{5,1},{9,13},{13,9},{2,6},{6,2},{1... | collective-permute-start | bytes 786440 | tf_op jit(solution)/shard_map/ppermute | solution.py:19
  7.5 35.4 %collective-permute-start.4 = (f32[104,1024]{1,0:T(8,128)S(1)}, f32[104,1024]{1,0:T(8,128)S(1)}, u32[]{:S(2)}, u32[]{:S(2)}) collective-permute-start(f32[104,1024]{1,0:T(8,128)S(1)} %get-tuple-element.37), channel_id=1, source_target_pairs={{0,8},{1,4},{2,10},{3,6},{4,13},{5,1},{6,15},{7,3},{8,12},{9,0},{1... | collective-permute-start | bytes 1277960 | tf_op jit(solution)/shard_map/ppermute | solution.py:317
  8.7 33.8 %collective-permute-start.5 = (f32[104,1024]{1,0:T(8,128)S(1)}, f32[104,1024]{1,0:T(8,128)S(1)}, u32[]{:S(2)}, u32[]{:S(2)}) collective-permute-start(f32[104,1024]{1,0:T(8,128)S(1)} %get-tuple-element.38), channel_id=1, source_target_pairs={{0,4},{1,8},{2,6},{3,10},{4,1},{5,13},{6,3},{7,15},{8,0},{9,12},{1... | collective-permute-start | bytes 1277960 | tf_op jit(solution)/shard_map/ppermute | solution.py:317
  9.5 1.2 %copy-start = (f32[104,2048]{1,0:T(8,128)S(1)}, f32[104,2048]{1,0:T(8,128)}, u32[]{:S(2)}) copy-start(f32[104,2048]{1,0:T(8,128)} %refs_0_.3) | copy-start | bytes 2555908
  10.7 1.2 %copy-start.2 = (f32[128,2048]{1,0:T(8,128)S(1)}, f32[128,2048]{1,0:T(8,128)}, u32[]{:S(2)}) copy-start(f32[128,2048]{1,0:T(8,128)} %refs_1_.1) | copy-start | bytes 3145732
  11.9 2.2 %copy-start.3 = (f32[4,512,512]{2,1,0:T(8,128)S(1)}, f32[4,512,512]{2,1,0:T(8,128)}, u32[]{:S(2)}) copy-start(f32[4,512,512]{2,1,0:T(8,128)} %gram_hbm.1) | copy-start | bytes 12582916
  22.0 7.9 %collective-permute-start.1 = (f32[64,1024]{1,0:T(8,128)S(1)}, f32[64,1024]{1,0:T(8,128)S(1)}, u32[]{:S(2)}, u32[]{:S(2)}) collective-permute-start(f32[64,1024]{1,0:T(8,128)S(1)} %collective-permute-done.straight_ref), channel_id=1, source_target_pairs={{0,16},{16,0},{1,17},{17,1},{2,18},{18,2},{3,19},{19,3},{4,20},{20... | collective-permute-start | bytes 786440 | tf_op jit(solution)/shard_map/ppermute | solution.py:19
  30.6 12.0 %collective-permute-start.3 = (f32[256,1024]{1,0:T(8,128)S(1)}, f32[256,1024]{1,0:T(8,128)S(1)}, u32[]{:S(2)}, u32[]{:S(2)}) collective-permute-start(f32[256,1024]{1,0:T(8,128)S(1)} %get-tuple-element.34), channel_id=1, source_target_pairs={{0,1},{1,0},{2,3},{3,2},{4,5},{5,4},{6,7},{7,6},{8,9},{9,8},{10,11... | collective-permute-start | bytes 3145736 | tf_op jit(solution)/shard_map/ppermute | solution.py:19
  31.6 11.0 %collective-permute-start.6 = (f32[104,256]{1,0:T(8,128)S(1)}, f32[104,256]{1,0:T(8,128)S(1)}, u32[]{:S(2)}, u32[]{:S(2)}) collective-permute-start(f32[104,256]{1,0:T(8,128)S(1)} %broadcast_select_fusion), channel_id=1, source_target_pairs={{0,1},{1,0},{2,3},{3,2},{4,5},{5,4},{6,7},{7,6},{8,9},{9,8},{10,11... | collective-permute-start | bytes 319496 | tf_op jit(solution)/shard_map/ppermute | solution.py:19
  43.7 4.2 %collective-permute-start.9 = (f32[104,128]{1,0:T(8,128)S(1)}, f32[104,128]{1,0:T(8,128)S(1)}, u32[]{:S(2)}, u32[]{:S(2)}) collective-permute-start(f32[104,128]{1,0:T(8,128)S(1)} %get-tuple-element.46), channel_id=1, source_target_pairs={{0,2},{1,3},{2,0},{3,1},{4,6},{5,7},{6,4},{7,5},{8,10},{9,11},{10,... | collective-permute-start | bytes 159752 | tf_op jit(solution)/shard_map/ppermute | solution.py:317
  45.2 5.0 %collective-permute-start.8 = (f32[104,128]{1,0:T(8,128)S(1)}, f32[104,128]{1,0:T(8,128)S(1)}, u32[]{:S(2)}, u32[]{:S(2)}) collective-permute-start(f32[104,128]{1,0:T(8,128)S(1)} %get-tuple-element.45), channel_id=1, source_target_pairs={{0,6},{1,7},{2,4},{3,5},{4,2},{5,3},{6,0},{7,1},{8,14},{9,15},{10,... | collective-permute-start | bytes 159752 | tf_op jit(solution)/shard_map/ppermute | solution.py:317
  45.2 5.0 %collective-permute-start.7 = (f32[104,128]{1,0:T(8,128)S(1)}, f32[104,128]{1,0:T(8,128)S(1)}, u32[]{:S(2)}, u32[]{:S(2)}) collective-permute-start(f32[104,128]{1,0:T(8,128)S(1)} %get-tuple-element.44), channel_id=1, source_target_pairs={{0,4},{1,5},{2,6},{3,7},{4,0},{5,1},{6,2},{7,3},{8,12},{9,13},{10,... | collective-permute-start | bytes 159752 | tf_op jit(solution)/shard_map/ppermute | solution.py:317

commit v8 on v7

--- a/solution.py
+++ b/solution.py
@@ -10,7 +10,7 @@
 HIGHEST = lax.Precision.HIGHEST
 ANYWHERE = pl.BlockSpec(memory_space=pl.ANY)
 VMEM = pl.BlockSpec(memory_space=pltpu.VMEM)
-TURNS = ((3, 2, 1, 0), (2, 0, 3, 1), (1, 3, 0, 2))
+TURNS = ((3, 2, 1, 0), (1, 0, 3, 2), (2, 3, 0, 1))
 FREE = pl.CostEstimate(flops=0, bytes_accessed=0, transcendentals=0)
 
 
@@ -237,7 +237,7 @@
     mine, other, second_ref, third = refs[:2], refs[2:4], refs[4], refs[5:7]
     early_ref, late_ref = refs[7], refs[12]
     row, feat = lax.axis_index("row"), lax.axis_index("feat")
-    here = feat % 2 == row // 2
+    here = feat % 2 == row % 2
 
     def scores(left, right):
         left, right = [ref[...] for ref in left], [ref[...] for ref in right]

time: 51.2 us -> 51.2 us (level)
  no operation moved by 1% of the time
where the time goes in v8:
time: 51.2 us; the launch traced here: 50.9 us
  waiting for transfers between devices  26.6 us (52%)
  starting transfers between devices  12.9 us (25%)
  Pallas kernels  5.95 us (12%)
  local copies, waits for them, and re-layouts  4.57 us (9%)
  other arithmetic  0.68 us (1%)
    ppermute x5, waiting for transfers between devices, permute(): return lax.ppermute(array, ('row', 'feat'), pairs)  13.3 us
    ppermute x5, waiting for transfers between devices, send(): return lax.ppermute(array, axis, [(i, to(i)) for i in range(devices)])  13.3 us
    ppermute x5, starting transfers between devices, send(): return lax.ppermute(array, axis, [(i, to(i)) for i in range(devices)])  7.34 us
    ppermute x5, starting transfers between devices, permute(): return lax.ppermute(array, ('row', 'feat'), pairs)  5.57 us
    unnamed x8, local copies, waits for them, and re-layouts  4.57 us
    pallas_call x2, Pallas kernels, pack(): pl.pallas_call(functools.partial(pack_kernel, turns=turns, queries=len(re...  2.25 us
  transfers between devices with their start and end apart: 10, of which 5 were waited for; matrix products, arithmetic and copies ran while one was open for 0% of the time, Pallas kernels for 8%

profile of v8, /device:TPU:0, one launch (start us, length us, event | category | flops | bytes accessed | tf_op | source)
XLA Modules:
  0.0 50.9 jit_solution(18319751417965921475)
XLA Ops:
  0.0 1.0 %shard_map.38.refs_2_ = f32[104,1024]{1,0:T(8,128)S(1)} custom-call(f32[104,2048]{1,0:T(8,128)} %refs_0_.3), custom_call_target="tpu_custom_call" | custom-call | tf_op jit(solution)/shard_map/pallas_call | solution.py:116
  1.0 0.0 copy-start.1
  1.0 5.1 %collective-permute-start.2 = (f32[104,1024]{1,0:T(8,128)S(1)}, f32[104,1024]{1,0:T(8,128)S(1)}, u32[]{:S(2)}, u32[]{:S(2)}) collective-permute-start(f32[104,1024]{1,0:T(8,128)S(1)} %shard_map.38.refs_2_), channel_id=1, source_target_pairs={{0,12},{4,8},{8,4},{12,0},{1,13},{5,9},{9,5},{13,1},{2,14},{6,10},... | collective-permute-start | bytes 1277960 | tf_op jit(solution)/shard_map/ppermute | solution.py:19
  6.1 0.0 copy-done.1
  6.2 1.2 %shard_map.39 = (f32[104,1024]{1,0:T(8,128)S(1)}, f32[104,1024]{1,0:T(8,128)S(1)}, f32[64,1024]{1,0:T(8,128)S(1)}) custom-call(f32[104,2048]{1,0:T(8,128)} %refs_0_.3, f32[128,2048]{1,0:T(8,128)} %refs_1_.1, f32[104,1024]{1,0:T(8,128)} %copy-done.1), custom_call_target="tpu_custom_call" | custom-call | tf_op jit(solution)/shard_map/pallas_call | solution.py:116
  7.4 0.1 collective-permute-start
  7.5 2.0 %collective-permute-start.4 = (f32[104,1024]{1,0:T(8,128)S(1)}, f32[104,1024]{1,0:T(8,128)S(1)}, u32[]{:S(2)}, u32[]{:S(2)}) collective-permute-start(f32[104,1024]{1,0:T(8,128)S(1)} %get-tuple-element.37), channel_id=1, source_target_pairs={{0,4},{1,8},{2,6},{3,10},{4,13},{5,1},{6,15},{7,3},{8,12},{9,0},{1... | collective-permute-start | bytes 1277960 | tf_op jit(solution)/shard_map/ppermute | solution.py:317
  9.5 0.0 collective-permute-start.5
  9.5 0.0 copy-start
  9.5 1.2 %copy-done = f32[104,2048]{1,0:T(8,128)S(1)} copy-done((f32[104,2048]{1,0:T(8,128)S(1)}, f32[104,2048]{1,0:T(8,128)}, u32[]{:S(2)}) %copy-start) | copy-done | bytes 851992
  10.6 0.0 copy-start.2
  10.6 1.2 %copy-done.2 = f32[128,2048]{1,0:T(8,128)S(1)} copy-done((f32[128,2048]{1,0:T(8,128)S(1)}, f32[128,2048]{1,0:T(8,128)}, u32[]{:S(2)}) %copy-start.2) | copy-done | bytes 1048600
  11.9 0.0 copy-start.3
  11.9 2.2 %copy-done.3 = f32[4,512,512]{2,1,0:T(8,128)S(1)} copy-done((f32[4,512,512]{2,1,0:T(8,128)S(1)}, f32[4,512,512]{2,1,0:T(8,128)}, u32[]{:S(2)}) %copy-start.3) | copy-done | bytes 4194328
  14.1 1.0 %shard_map.37 = (bf16[128,1024]{1,0:T(8,128)(2,1)S(1)}, bf16[128,1024]{1,0:T(8,128)(2,1)S(1)}, bf16[2,512,512]{2,1,0:T(8,128)(2,1)S(1)}, bf16[2,512,512]{2,1,0:T(8,128)(2,1)S(1)}, f32[104,1024]{1,0:T(8,128)S(1)}) custom-call(f32[128,2048]{1,0:T(8,128)S(1)} %copy-done.2, f32[4,512,512]{2,1,0:T(8,128)S(1)} %copy-done.3, f32[104,2048]{1,0:T(8,128)S(1)} %copy-done), custom_call_target="tpu_custom_call" | custom-call | flops 2147483648 | bytes 8388608 | tf_op jit(solution)/shard_map/pallas_call | solution.py:165
  15.0 7.0 %collective-permute-done.straight_ref = f32[64,1024]{1,0:T(8,128)S(1)} collective-permute-done((f32[64,1024]{1,0:T(8,128)S(1)}, f32[64,1024]{1,0:T(8,128)S(1)}, u32[]{:S(2)}, u32[]{:S(2)}) %collective-permute-start) | collective-permute-done | bytes 262176 | tf_op jit(solution)/shard_map/ppermute | solution.py:19
  22.0 1.5 %collective-permute-start.1 = (f32[64,1024]{1,0:T(8,128)S(1)}, f32[64,1024]{1,0:T(8,128)S(1)}, u32[]{:S(2)}, u32[]{:S(2)}) collective-permute-start(f32[64,1024]{1,0:T(8,128)S(1)} %collective-permute-done.straight_ref), channel_id=1, source_target_pairs={{0,16},{16,0},{1,17},{17,1},{2,18},{18,2},{3,19},{19,3},{4,20},{20... | collective-permute-start | bytes 786440 | tf_op jit(solution)/shard_map/ppermute | solution.py:19
  23.6 0.0 collective-permute-done.2.given_ref
  23.6 0.1 shard_map.40
  23.6 6.3 %collective-permute-done.1.swapped_ref = f32[64,1024]{1,0:T(8,128)S(1)} collective-permute-done((f32[64,1024]{1,0:T(8,128)S(1)}, f32[64,1024]{1,0:T(8,128)S(1)}, u32[]{:S(2)}, u32[]{:S(2)}) %collective-permute-start.1) | collective-permute-done | bytes 262176 | tf_op jit(solution)/shard_map/ppermute | solution.py:19
  29.9 0.7 %shard_map.41 = (bf16[256,1024]{1,0:T(8,128)(2,1)S(1)}, bf16[256,1024]{1,0:T(8,128)(2,1)S(1)}, f32[256,1024]{1,0:T(8,128)S(1)}) custom-call(bf16[128,1024]{1,0:T(8,128)(2,1)S(1)} %get-tuple-element.26.own_high, bf16[128,1024]{1,0:T(8,128)(2,1)S(1)} %get-tuple-element.27.own_low, bf16[2,512,512]{2,1,0:T(8,128)(2,1)S(1)} %get-tuple-element.28.g_high, ...), custom_call_target="tpu_custom_call" | custom-call | tf_op jit(solution)/shard_map/pallas_call | solution.py:195
  30.6 0.1 collective-permute-start.3
  30.7 0.5 shard_map.45
  31.2 0.5 shard_map.44
  31.6 0.6 %collective-permute-start.6 = (f32[104,256]{1,0:T(8,128)S(1)}, f32[104,256]{1,0:T(8,128)S(1)}, u32[]{:S(2)}, u32[]{:S(2)}) collective-permute-start(f32[104,256]{1,0:T(8,128)S(1)} %broadcast_select_fusion), channel_id=1, source_target_pairs={{0,1},{1,0},{2,3},{3,2},{4,5},{5,4},{6,7},{7,6},{8,9},{9,8},{10,11... | collective-permute-start | bytes 319496 | tf_op jit(solution)/shard_map/ppermute | solution.py:19
  32.2 10.3 %collective-permute-done.5.given_ref = f32[104,1024]{1,0:T(8,128)S(1)} collective-permute-done((f32[104,1024]{1,0:T(8,128)S(1)}, f32[104,1024]{1,0:T(8,128)S(1)}, u32[]{:S(2)}, u32[]{:S(2)}) %collective-permute-start.5) | collective-permute-done | bytes 426016 | tf_op jit(solution)/shard_map/ppermute | solution.py:317
  42.5 0.1 shard_map.43
  42.6 0.0 collective-permute-done.6
  42.6 0.0 collective-permute-done.3.given_ref
  42.6 0.1 shard_map.42
  42.8 0.0 collective-permute-done.4.refs_4_
  42.8 0.8 %shard_map.46 = (f32[104,128]{1,0:T(8,128)S(1)}, f32[104,128]{1,0:T(8,128)S(1)}, f32[104,128]{1,0:T(8,128)S(1)}, f32[104,128]{1,0:T(8,128)S(1)}) custom-call(bf16[256,1024]{1,0:T(8,128)(2,1)S(1)} %get-tuple-element.32.high_ref.refs_0_, bf16[256,1024]{1,0:T(8,128)(2,1)S(1)} %get-tuple-element.33.low_ref.refs_1_, ...), custom_call_target="tpu_custom_call" | custom-call | tf_op jit(solution)/shard_map/pallas_call | solution.py:266
  43.6 1.6 %collective-permute-start.9 = (f32[104,128]{1,0:T(8,128)S(1)}, f32[104,128]{1,0:T(8,128)S(1)}, u32[]{:S(2)}, u32[]{:S(2)}) collective-permute-start(f32[104,128]{1,0:T(8,128)S(1)} %get-tuple-element.46), channel_id=1, source_target_pairs={{0,2},{1,3},{2,0},{3,1},{4,6},{5,7},{6,4},{7,5},{8,10},{9,11},{10,... | collective-permute-start | bytes 159752 | tf_op jit(solution)/shard_map/ppermute | solution.py:317
  45.2 0.0 collective-permute-start.8
  45.2 2.0 %collective-permute-start.7 = (f32[104,128]{1,0:T(8,128)S(1)}, f32[104,128]{1,0:T(8,128)S(1)}, u32[]{:S(2)}, u32[]{:S(2)}) collective-permute-start(f32[104,128]{1,0:T(8,128)S(1)} %get-tuple-element.44), channel_id=1, source_target_pairs={{0,4},{1,5},{2,6},{3,7},{4,0},{5,1},{6,2},{7,3},{8,12},{9,13},{10,... | collective-permute-start | bytes 159752 | tf_op jit(solution)/shard_map/ppermute | solution.py:317
  47.2 0.6 %collective-permute-done.9 = f32[104,128]{1,0:T(8,128)S(1)} collective-permute-done((f32[104,128]{1,0:T(8,128)S(1)}, f32[104,128]{1,0:T(8,128)S(1)}, u32[]{:S(2)}, u32[]{:S(2)}) %collective-permute-start.9) | collective-permute-done | bytes 53280 | tf_op jit(solution)/shard_map/ppermute | solution.py:317
  47.8 2.4 %collective-permute-done.8 = f32[104,128]{1,0:T(8,128)S(1)} collective-permute-done((f32[104,128]{1,0:T(8,128)S(1)}, f32[104,128]{1,0:T(8,128)S(1)}, u32[]{:S(2)}, u32[]{:S(2)}) %collective-permute-start.8) | collective-permute-done | bytes 53280 | tf_op jit(solution)/shard_map/ppermute | solution.py:317
  50.2 0.0 collective-permute-done.7
  50.2 0.6 %add_bitcast_fusion = f32[128,104]{0,1:T(8,128)} fusion(f32[104,128]{1,0:T(8,128)S(1)} %collective-permute-done.9, f32[104,128]{1,0:T(8,128)S(1)} %collective-permute-done.8, f32[104,128]{1,0:T(8,128)S(1)} %get-tuple-element.43, f32[104,128]{1,0:T(8,128)S(1)} %collective-permute-done.7), kind=kLoop, calls=%fused_computation.1 | loop fusion | flops 39936 | bytes 266240 | tf_op jit(solution)/shard_map/transpose | solution.py:348
  (2 shorter events, 0.0 us)
Async XLA Ops:
  1.0 5.1 %copy-start.1 = (f32[104,1024]{1,0:T(8,128)}, f32[104,1024]{1,0:T(8,128)S(1)}, u32[]{:S(2)}) copy-start(f32[104,1024]{1,0:T(8,128)S(1)} %shard_map.38.refs_2_) | copy-start | bytes 1277956
  1.0 22.5 %collective-permute-start.2 = (f32[104,1024]{1,0:T(8,128)S(1)}, f32[104,1024]{1,0:T(8,128)S(1)}, u32[]{:S(2)}, u32[]{:S(2)}) collective-permute-start(f32[104,1024]{1,0:T(8,128)S(1)} %shard_map.38.refs_2_), channel_id=1, source_target_pairs={{0,12},{4,8},{8,4},{12,0},{1,13},{5,9},{9,5},{13,1},{2,14},{6,10},... | collective-permute-start | bytes 1277960 | tf_op jit(solution)/shard_map/ppermute | solution.py:19
  7.4 14.6 %collective-permute-start = (f32[64,1024]{1,0:T(8,128)S(1)}, f32[64,1024]{1,0:T(8,128)S(1)}, u32[]{:S(2)}, u32[]{:S(2)}) collective-permute-start(f32[64,1024]{1,0:T(8,128)S(1)} %get-tuple-element.30), channel_id=1, source_target_pairs={{0,4},{4,0},{8,12},{12,8},{1,5},{5,1},{9,13},{13,9},{2,6},{6,2},{1... | collective-permute-start | bytes 786440 | tf_op jit(solution)/shard_map/ppermute | solution.py:19
  7.5 35.3 %collective-permute-start.4 = (f32[104,1024]{1,0:T(8,128)S(1)}, f32[104,1024]{1,0:T(8,128)S(1)}, u32[]{:S(2)}, u32[]{:S(2)}) collective-permute-start(f32[104,1024]{1,0:T(8,128)S(1)} %get-tuple-element.37), channel_id=1, source_target_pairs={{0,4},{1,8},{2,6},{3,10},{4,13},{5,1},{6,15},{7,3},{8,12},{9,0},{1... | collective-permute-start | bytes 1277960 | tf_op jit(solution)/shard_map/ppermute | solution.py:317
  9.5 33.0 %collective-permute-start.5 = (f32[104,1024]{1,0:T(8,128)S(1)}, f32[104,1024]{1,0:T(8,128)S(1)}, u32[]{:S(2)}, u32[]{:S(2)}) collective-permute-start(f32[104,1024]{1,0:T(8,128)S(1)} %get-tuple-element.38), channel_id=1, source_target_pairs={{0,8},{1,4},{2,10},{3,6},{4,1},{5,13},{6,3},{7,15},{8,0},{9,12},{1... | collective-permute-start | bytes 1277960 | tf_op jit(solution)/shard_map/ppermute | solution.py:317
  9.5 1.2 %copy-start = (f32[104,2048]{1,0:T(8,128)S(1)}, f32[104,2048]{1,0:T(8,128)}, u32[]{:S(2)}) copy-start(f32[104,2048]{1,0:T(8,128)} %refs_0_.3) | copy-start | bytes 2555908
  10.6 1.2 %copy-start.2 = (f32[128,2048]{1,0:T(8,128)S(1)}, f32[128,2048]{1,0:T(8,128)}, u32[]{:S(2)}) copy-start(f32[128,2048]{1,0:T(8,128)} %refs_1_.1) | copy-start | bytes 3145732
  11.9 2.2 %copy-start.3 = (f32[4,512,512]{2,1,0:T(8,128)S(1)}, f32[4,512,512]{2,1,0:T(8,128)}, u32[]{:S(2)}) copy-start(f32[4,512,512]{2,1,0:T(8,128)} %gram_hbm.1) | copy-start | bytes 12582916
  22.0 7.9 %collective-permute-start.1 = (f32[64,1024]{1,0:T(8,128)S(1)}, f32[64,1024]{1,0:T(8,128)S(1)}, u32[]{:S(2)}, u32[]{:S(2)}) collective-permute-start(f32[64,1024]{1,0:T(8,128)S(1)} %collective-permute-done.straight_ref), channel_id=1, source_target_pairs={{0,16},{16,0},{1,17},{17,1},{2,18},{18,2},{3,19},{19,3},{4,20},{20... | collective-permute-start | bytes 786440 | tf_op jit(solution)/shard_map/ppermute | solution.py:19
  30.6 12.0 %collective-permute-start.3 = (f32[256,1024]{1,0:T(8,128)S(1)}, f32[256,1024]{1,0:T(8,128)S(1)}, u32[]{:S(2)}, u32[]{:S(2)}) collective-permute-start(f32[256,1024]{1,0:T(8,128)S(1)} %get-tuple-element.34), channel_id=1, source_target_pairs={{0,1},{1,0},{2,3},{3,2},{4,5},{5,4},{6,7},{7,6},{8,9},{9,8},{10,11... | collective-permute-start | bytes 3145736 | tf_op jit(solution)/shard_map/ppermute | solution.py:19
  31.6 10.9 %collective-permute-start.6 = (f32[104,256]{1,0:T(8,128)S(1)}, f32[104,256]{1,0:T(8,128)S(1)}, u32[]{:S(2)}, u32[]{:S(2)}) collective-permute-start(f32[104,256]{1,0:T(8,128)S(1)} %broadcast_select_fusion), channel_id=1, source_target_pairs={{0,1},{1,0},{2,3},{3,2},{4,5},{5,4},{6,7},{7,6},{8,9},{9,8},{10,11... | collective-permute-start | bytes 319496 | tf_op jit(solution)/shard_map/ppermute | solution.py:19
  43.6 4.2 %collective-permute-start.9 = (f32[104,128]{1,0:T(8,128)S(1)}, f32[104,128]{1,0:T(8,128)S(1)}, u32[]{:S(2)}, u32[]{:S(2)}) collective-permute-start(f32[104,128]{1,0:T(8,128)S(1)} %get-tuple-element.46), channel_id=1, source_target_pairs={{0,2},{1,3},{2,0},{3,1},{4,6},{5,7},{6,4},{7,5},{8,10},{9,11},{10,... | collective-permute-start | bytes 159752 | tf_op jit(solution)/shard_map/ppermute | solution.py:317
  45.2 5.0 %collective-permute-start.8 = (f32[104,128]{1,0:T(8,128)S(1)}, f32[104,128]{1,0:T(8,128)S(1)}, u32[]{:S(2)}, u32[]{:S(2)}) collective-permute-start(f32[104,128]{1,0:T(8,128)S(1)} %get-tuple-element.45), channel_id=1, source_target_pairs={{0,6},{1,7},{2,4},{3,5},{4,2},{5,3},{6,0},{7,1},{8,14},{9,15},{10,... | collective-permute-start | bytes 159752 | tf_op jit(solution)/shard_map/ppermute | solution.py:317
  45.2 5.0 %collective-permute-start.7 = (f32[104,128]{1,0:T(8,128)S(1)}, f32[104,128]{1,0:T(8,128)S(1)}, u32[]{:S(2)}, u32[]{:S(2)}) collective-permute-start(f32[104,128]{1,0:T(8,128)S(1)} %get-tuple-element.44), channel_id=1, source_target_pairs={{0,4},{1,5},{2,6},{3,7},{4,0},{5,1},{6,2},{7,3},{8,12},{9,13},{10,... | collective-permute-start | bytes 159752 | tf_op jit(solution)/shard_map/ppermute | solution.py:317

commit v9 on v8

--- a/solution.py
+++ b/solution.py
@@ -342,10 +342,10 @@
     early = jnp.where(own_core, own, cross) + swap(jnp.where(own_core, cross, own), "feat", 1)
     third = split_block(third, SPLIT_COST)
     keep, keep_pair, give, give_pair = last_scores(conditioned, other, second, third, early)
-    there = permute(keep_pair, lambda r, f: (r ^ 1, f))
     across = permute(give_pair, lambda r, f: (r ^ 1, f ^ 2))
     beside = permute(give, lambda r, f: (r, f ^ 2))
-    return (keep + there + across + beside).T
+    there = permute(keep_pair, lambda r, f: (r ^ 1, f))
+    return (keep + across + beside + there).T
 
 
 def solution(mesh):

time: 51.2 us -> 51.3 us (level)
  transfers between devices with their start and end apart: 10 -> 10, of which waited for: 5 -> 6; matrix products, arithmetic and copies ran while one was open for 0% -> 0% of each run, Pallas kernels for 8% -> 8%
where the time goes in v9:
time: 51.3 us; the launch traced here: 51 us
  waiting for transfers between devices  26.8 us (52%)
  starting transfers between devices  12.9 us (25%)
  Pallas kernels  5.94 us (12%)
  local copies, waits for them, and re-layouts  4.57 us (9%)
  other arithmetic  0.68 us (1%)
    ppermute x5, waiting for transfers between devices, permute(): return lax.ppermute(array, ('row', 'feat'), pairs)  13.5 us
    ppermute x5, waiting for transfers between devices, send(): return lax.ppermute(array, axis, [(i, to(i)) for i in range(devices)])  13.3 us
    ppermute x5, starting transfers between devices, send(): return lax.ppermute(array, axis, [(i, to(i)) for i in range(devices)])  7.34 us
    ppermute x5, starting transfers between devices, permute(): return lax.ppermute(array, ('row', 'feat'), pairs)  5.56 us
    unnamed x8, local copies, waits for them, and re-layouts  4.57 us
    pallas_call x2, Pallas kernels, pack(): pl.pallas_call(functools.partial(pack_kernel, turns=turns, queries=len(re...  2.25 us
  transfers between devices with their start and end apart: 10, of which 6 were waited for; matrix products, arithmetic and copies ran while one was open for 0% of the time, Pallas kernels for 8%

profile of v9, /device:TPU:0, one launch (start us, length us, event | category | flops | bytes accessed | tf_op | source)
XLA Modules:
  0.0 51.0 jit_solution(3505846658069342957)
XLA Ops:
  0.0 1.0 %shard_map.38.refs_2_ = f32[104,1024]{1,0:T(8,128)S(1)} custom-call(f32[104,2048]{1,0:T(8,128)} %refs_0_.3), custom_call_target="tpu_custom_call" | custom-call | tf_op jit(solution)/shard_map/pallas_call | solution.py:116
  1.0 0.0 copy-start.1
  1.0 5.1 %collective-permute-start.2 = (f32[104,1024]{1,0:T(8,128)S(1)}, f32[104,1024]{1,0:T(8,128)S(1)}, u32[]{:S(2)}, u32[]{:S(2)}) collective-permute-start(f32[104,1024]{1,0:T(8,128)S(1)} %shard_map.38.refs_2_), channel_id=1, source_target_pairs={{0,12},{4,8},{8,4},{12,0},{1,13},{5,9},{9,5},{13,1},{2,14},{6,10},... | collective-permute-start | bytes 1277960 | tf_op jit(solution)/shard_map/ppermute | solution.py:19
  6.1 0.0 copy-done.1
  6.2 1.2 %shard_map.39 = (f32[104,1024]{1,0:T(8,128)S(1)}, f32[104,1024]{1,0:T(8,128)S(1)}, f32[64,1024]{1,0:T(8,128)S(1)}) custom-call(f32[104,2048]{1,0:T(8,128)} %refs_0_.3, f32[128,2048]{1,0:T(8,128)} %refs_1_.1, f32[104,1024]{1,0:T(8,128)} %copy-done.1), custom_call_target="tpu_custom_call" | custom-call | tf_op jit(solution)/shard_map/pallas_call | solution.py:116
  7.4 0.1 collective-permute-start
  7.5 2.0 %collective-permute-start.4 = (f32[104,1024]{1,0:T(8,128)S(1)}, f32[104,1024]{1,0:T(8,128)S(1)}, u32[]{:S(2)}, u32[]{:S(2)}) collective-permute-start(f32[104,1024]{1,0:T(8,128)S(1)} %get-tuple-element.37), channel_id=1, source_target_pairs={{0,4},{1,8},{2,6},{3,10},{4,13},{5,1},{6,15},{7,3},{8,12},{9,0},{1... | collective-permute-start | bytes 1277960 | tf_op jit(solution)/shard_map/ppermute | solution.py:317
  9.5 0.0 collective-permute-start.5
  9.5 0.0 copy-start
  9.5 1.2 %copy-done = f32[104,2048]{1,0:T(8,128)S(1)} copy-done((f32[104,2048]{1,0:T(8,128)S(1)}, f32[104,2048]{1,0:T(8,128)}, u32[]{:S(2)}) %copy-start) | copy-done | bytes 851992
  10.6 0.0 copy-start.2
  10.6 1.2 %copy-done.2 = f32[128,2048]{1,0:T(8,128)S(1)} copy-done((f32[128,2048]{1,0:T(8,128)S(1)}, f32[128,2048]{1,0:T(8,128)}, u32[]{:S(2)}) %copy-start.2) | copy-done | bytes 1048600
  11.9 0.0 copy-start.3
  11.9 2.2 %copy-done.3 = f32[4,512,512]{2,1,0:T(8,128)S(1)} copy-done((f32[4,512,512]{2,1,0:T(8,128)S(1)}, f32[4,512,512]{2,1,0:T(8,128)}, u32[]{:S(2)}) %copy-start.3) | copy-done | bytes 4194328
  14.1 1.0 %shard_map.37 = (bf16[128,1024]{1,0:T(8,128)(2,1)S(1)}, bf16[128,1024]{1,0:T(8,128)(2,1)S(1)}, bf16[2,512,512]{2,1,0:T(8,128)(2,1)S(1)}, bf16[2,512,512]{2,1,0:T(8,128)(2,1)S(1)}, f32[104,1024]{1,0:T(8,128)S(1)}) custom-call(f32[128,2048]{1,0:T(8,128)S(1)} %copy-done.2, f32[4,512,512]{2,1,0:T(8,128)S(1)} %copy-done.3, f32[104,2048]{1,0:T(8,128)S(1)} %copy-done), custom_call_target="tpu_custom_call" | custom-call | flops 2147483648 | bytes 8388608 | tf_op jit(solution)/shard_map/pallas_call | solution.py:165
  15.0 7.0 %collective-permute-done.straight_ref = f32[64,1024]{1,0:T(8,128)S(1)} collective-permute-done((f32[64,1024]{1,0:T(8,128)S(1)}, f32[64,1024]{1,0:T(8,128)S(1)}, u32[]{:S(2)}, u32[]{:S(2)}) %collective-permute-start) | collective-permute-done | bytes 262176 | tf_op jit(solution)/shard_map/ppermute | solution.py:19
  22.0 1.5 %collective-permute-start.1 = (f32[64,1024]{1,0:T(8,128)S(1)}, f32[64,1024]{1,0:T(8,128)S(1)}, u32[]{:S(2)}, u32[]{:S(2)}) collective-permute-start(f32[64,1024]{1,0:T(8,128)S(1)} %collective-permute-done.straight_ref), channel_id=1, source_target_pairs={{0,16},{16,0},{1,17},{17,1},{2,18},{18,2},{3,19},{19,3},{4,20},{20... | collective-permute-start | bytes 786440 | tf_op jit(solution)/shard_map/ppermute | solution.py:19
  23.6 0.0 collective-permute-done.2.given_ref
  23.6 0.1 shard_map.40
  23.6 6.3 %collective-permute-done.1.swapped_ref = f32[64,1024]{1,0:T(8,128)S(1)} collective-permute-done((f32[64,1024]{1,0:T(8,128)S(1)}, f32[64,1024]{1,0:T(8,128)S(1)}, u32[]{:S(2)}, u32[]{:S(2)}) %collective-permute-start.1) | collective-permute-done | bytes 262176 | tf_op jit(solution)/shard_map/ppermute | solution.py:19
  29.9 0.7 %shard_map.41 = (bf16[256,1024]{1,0:T(8,128)(2,1)S(1)}, bf16[256,1024]{1,0:T(8,128)(2,1)S(1)}, f32[256,1024]{1,0:T(8,128)S(1)}) custom-call(bf16[128,1024]{1,0:T(8,128)(2,1)S(1)} %get-tuple-element.26.own_high, bf16[128,1024]{1,0:T(8,128)(2,1)S(1)} %get-tuple-element.27.own_low, bf16[2,512,512]{2,1,0:T(8,128)(2,1)S(1)} %get-tuple-element.28.g_high, ...), custom_call_target="tpu_custom_call" | custom-call | tf_op jit(solution)/shard_map/pallas_call | solution.py:195
  30.6 0.1 collective-permute-start.3
  30.7 0.5 shard_map.45
  31.2 0.5 shard_map.44
  31.6 0.6 %collective-permute-start.6 = (f32[104,256]{1,0:T(8,128)S(1)}, f32[104,256]{1,0:T(8,128)S(1)}, u32[]{:S(2)}, u32[]{:S(2)}) collective-permute-start(f32[104,256]{1,0:T(8,128)S(1)} %broadcast_select_fusion), channel_id=1, source_target_pairs={{0,1},{1,0},{2,3},{3,2},{4,5},{5,4},{6,7},{7,6},{8,9},{9,8},{10,11... | collective-permute-start | bytes 319496 | tf_op jit(solution)/shard_map/ppermute | solution.py:19
  32.2 10.3 %collective-permute-done.5.given_ref = f32[104,1024]{1,0:T(8,128)S(1)} collective-permute-done((f32[104,1024]{1,0:T(8,128)S(1)}, f32[104,1024]{1,0:T(8,128)S(1)}, u32[]{:S(2)}, u32[]{:S(2)}) %collective-permute-start.5) | collective-permute-done | bytes 426016 | tf_op jit(solution)/shard_map/ppermute | solution.py:317
  42.6 0.1 shard_map.43
  42.6 0.0 collective-permute-done.6
  42.7 0.0 collective-permute-done.3.given_ref
  42.7 0.1 shard_map.42
  42.8 0.0 collective-permute-done.4.refs_4_
  42.8 0.8 %shard_map.46 = (f32[104,128]{1,0:T(8,128)S(1)}, f32[104,128]{1,0:T(8,128)S(1)}, f32[104,128]{1,0:T(8,128)S(1)}, f32[104,128]{1,0:T(8,128)S(1)}) custom-call(bf16[256,1024]{1,0:T(8,128)(2,1)S(1)} %get-tuple-element.32.high_ref.refs_0_, bf16[256,1024]{1,0:T(8,128)(2,1)S(1)} %get-tuple-element.33.low_ref.refs_1_, ...), custom_call_target="tpu_custom_call" | custom-call | tf_op jit(solution)/shard_map/pallas_call | solution.py:266
  43.7 0.1 collective-permute-start.9
  43.8 1.6 %collective-permute-start.8 = (f32[104,128]{1,0:T(8,128)S(1)}, f32[104,128]{1,0:T(8,128)S(1)}, u32[]{:S(2)}, u32[]{:S(2)}) collective-permute-start(f32[104,128]{1,0:T(8,128)S(1)} %get-tuple-element.45), channel_id=1, source_target_pairs={{0,2},{1,3},{2,0},{3,1},{4,6},{5,7},{6,4},{7,5},{8,10},{9,11},{10,... | collective-permute-start | bytes 159752 | tf_op jit(solution)/shard_map/ppermute | solution.py:317
  45.3 1.9 %collective-permute-start.7 = (f32[104,128]{1,0:T(8,128)S(1)}, f32[104,128]{1,0:T(8,128)S(1)}, u32[]{:S(2)}, u32[]{:S(2)}) collective-permute-start(f32[104,128]{1,0:T(8,128)S(1)} %get-tuple-element.44), channel_id=1, source_target_pairs={{0,6},{1,7},{2,4},{3,5},{4,2},{5,3},{6,0},{7,1},{8,14},{9,15},{10,... | collective-permute-start | bytes 159752 | tf_op jit(solution)/shard_map/ppermute | solution.py:317
  47.2 0.6 %collective-permute-done.9 = f32[104,128]{1,0:T(8,128)S(1)} collective-permute-done((f32[104,128]{1,0:T(8,128)S(1)}, f32[104,128]{1,0:T(8,128)S(1)}, u32[]{:S(2)}, u32[]{:S(2)}) %collective-permute-start.9) | collective-permute-done | bytes 53280 | tf_op jit(solution)/shard_map/ppermute | solution.py:317
  47.9 0.1 collective-permute-done.8
  48.0 2.4 %collective-permute-done.7 = f32[104,128]{1,0:T(8,128)S(1)} collective-permute-done((f32[104,128]{1,0:T(8,128)S(1)}, f32[104,128]{1,0:T(8,128)S(1)}, u32[]{:S(2)}, u32[]{:S(2)}) %collective-permute-start.7) | collective-permute-done | bytes 53280 | tf_op jit(solution)/shard_map/ppermute | solution.py:317
  50.4 0.6 %add_bitcast_fusion = f32[128,104]{0,1:T(8,128)} fusion(f32[104,128]{1,0:T(8,128)S(1)} %collective-permute-done.9, f32[104,128]{1,0:T(8,128)S(1)} %collective-permute-done.8, f32[104,128]{1,0:T(8,128)S(1)} %get-tuple-element.43, f32[104,128]{1,0:T(8,128)S(1)} %collective-permute-done.7), kind=kLoop, calls=%fused_computation.1 | loop fusion | flops 39936 | bytes 266240 | tf_op jit(solution)/shard_map/transpose | solution.py:348
  (2 shorter events, 0.0 us)
Async XLA Ops:
  1.0 5.1 %copy-start.1 = (f32[104,1024]{1,0:T(8,128)}, f32[104,1024]{1,0:T(8,128)S(1)}, u32[]{:S(2)}) copy-start(f32[104,1024]{1,0:T(8,128)S(1)} %shard_map.38.refs_2_) | copy-start | bytes 1277956
  1.0 22.5 %collective-permute-start.2 = (f32[104,1024]{1,0:T(8,128)S(1)}, f32[104,1024]{1,0:T(8,128)S(1)}, u32[]{:S(2)}, u32[]{:S(2)}) collective-permute-start(f32[104,1024]{1,0:T(8,128)S(1)} %shard_map.38.refs_2_), channel_id=1, source_target_pairs={{0,12},{4,8},{8,4},{12,0},{1,13},{5,9},{9,5},{13,1},{2,14},{6,10},... | collective-permute-start | bytes 1277960 | tf_op jit(solution)/shard_map/ppermute | solution.py:19
  7.4 14.6 %collective-permute-start = (f32[64,1024]{1,0:T(8,128)S(1)}, f32[64,1024]{1,0:T(8,128)S(1)}, u32[]{:S(2)}, u32[]{:S(2)}) collective-permute-start(f32[64,1024]{1,0:T(8,128)S(1)} %get-tuple-element.30), channel_id=1, source_target_pairs={{0,4},{4,0},{8,12},{12,8},{1,5},{5,1},{9,13},{13,9},{2,6},{6,2},{1... | collective-permute-start | bytes 786440 | tf_op jit(solution)/shard_map/ppermute | solution.py:19
  7.5 35.4 %collective-permute-start.4 = (f32[104,1024]{1,0:T(8,128)S(1)}, f32[104,1024]{1,0:T(8,128)S(1)}, u32[]{:S(2)}, u32[]{:S(2)}) collective-permute-start(f32[104,1024]{1,0:T(8,128)S(1)} %get-tuple-element.37), channel_id=1, source_target_pairs={{0,4},{1,8},{2,6},{3,10},{4,13},{5,1},{6,15},{7,3},{8,12},{9,0},{1... | collective-permute-start | bytes 1277960 | tf_op jit(solution)/shard_map/ppermute | solution.py:317
  9.5 33.1 %collective-permute-start.5 = (f32[104,1024]{1,0:T(8,128)S(1)}, f32[104,1024]{1,0:T(8,128)S(1)}, u32[]{:S(2)}, u32[]{:S(2)}) collective-permute-start(f32[104,1024]{1,0:T(8,128)S(1)} %get-tuple-element.38), channel_id=1, source_target_pairs={{0,8},{1,4},{2,10},{3,6},{4,1},{5,13},{6,3},{7,15},{8,0},{9,12},{1... | collective-permute-start | bytes 1277960 | tf_op jit(solution)/shard_map/ppermute | solution.py:317
  9.5 1.2 %copy-start = (f32[104,2048]{1,0:T(8,128)S(1)}, f32[104,2048]{1,0:T(8,128)}, u32[]{:S(2)}) copy-start(f32[104,2048]{1,0:T(8,128)} %refs_0_.3) | copy-start | bytes 2555908
  10.6 1.2 %copy-start.2 = (f32[128,2048]{1,0:T(8,128)S(1)}, f32[128,2048]{1,0:T(8,128)}, u32[]{:S(2)}) copy-start(f32[128,2048]{1,0:T(8,128)} %refs_1_.1) | copy-start | bytes 3145732
  11.9 2.2 %copy-start.3 = (f32[4,512,512]{2,1,0:T(8,128)S(1)}, f32[4,512,512]{2,1,0:T(8,128)}, u32[]{:S(2)}) copy-start(f32[4,512,512]{2,1,0:T(8,128)} %gram_hbm.1) | copy-start | bytes 12582916
  22.0 7.9 %collective-permute-start.1 = (f32[64,1024]{1,0:T(8,128)S(1)}, f32[64,1024]{1,0:T(8,128)S(1)}, u32[]{:S(2)}, u32[]{:S(2)}) collective-permute-start(f32[64,1024]{1,0:T(8,128)S(1)} %collective-permute-done.straight_ref), channel_id=1, source_target_pairs={{0,16},{16,0},{1,17},{17,1},{2,18},{18,2},{3,19},{19,3},{4,20},{20... | collective-permute-start | bytes 786440 | tf_op jit(solution)/shard_map/ppermute | solution.py:19
  30.6 12.1 %collective-permute-start.3 = (f32[256,1024]{1,0:T(8,128)S(1)}, f32[256,1024]{1,0:T(8,128)S(1)}, u32[]{:S(2)}, u32[]{:S(2)}) collective-permute-start(f32[256,1024]{1,0:T(8,128)S(1)} %get-tuple-element.34), channel_id=1, source_target_pairs={{0,1},{1,0},{2,3},{3,2},{4,5},{5,4},{6,7},{7,6},{8,9},{9,8},{10,11... | collective-permute-start | bytes 3145736 | tf_op jit(solution)/shard_map/ppermute | solution.py:19
  31.6 11.0 %collective-permute-start.6 = (f32[104,256]{1,0:T(8,128)S(1)}, f32[104,256]{1,0:T(8,128)S(1)}, u32[]{:S(2)}, u32[]{:S(2)}) collective-permute-start(f32[104,256]{1,0:T(8,128)S(1)} %broadcast_select_fusion), channel_id=1, source_target_pairs={{0,1},{1,0},{2,3},{3,2},{4,5},{5,4},{6,7},{7,6},{8,9},{9,8},{10,11... | collective-permute-start | bytes 319496 | tf_op jit(solution)/shard_map/ppermute | solution.py:19
  43.7 4.2 %collective-permute-start.9 = (f32[104,128]{1,0:T(8,128)S(1)}, f32[104,128]{1,0:T(8,128)S(1)}, u32[]{:S(2)}, u32[]{:S(2)}) collective-permute-start(f32[104,128]{1,0:T(8,128)S(1)} %get-tuple-element.46), channel_id=1, source_target_pairs={{0,4},{1,5},{2,6},{3,7},{4,0},{5,1},{6,2},{7,3},{8,12},{9,13},{10,... | collective-permute-start | bytes 159752 | tf_op jit(solution)/shard_map/ppermute | solution.py:317
  43.8 4.2 %collective-permute-start.8 = (f32[104,128]{1,0:T(8,128)S(1)}, f32[104,128]{1,0:T(8,128)S(1)}, u32[]{:S(2)}, u32[]{:S(2)}) collective-permute-start(f32[104,128]{1,0:T(8,128)S(1)} %get-tuple-element.45), channel_id=1, source_target_pairs={{0,2},{1,3},{2,0},{3,1},{4,6},{5,7},{6,4},{7,5},{8,10},{9,11},{10,... | collective-permute-start | bytes 159752 | tf_op jit(solution)/shard_map/ppermute | solution.py:317
  45.3 5.0 %collective-permute-start.7 = (f32[104,128]{1,0:T(8,128)S(1)}, f32[104,128]{1,0:T(8,128)S(1)}, u32[]{:S(2)}, u32[]{:S(2)}) collective-permute-start(f32[104,128]{1,0:T(8,128)S(1)} %get-tuple-element.44), channel_id=1, source_target_pairs={{0,6},{1,7},{2,4},{3,5},{4,2},{5,3},{6,0},{7,1},{8,14},{9,15},{10,... | collective-permute-start | bytes 159752 | tf_op jit(solution)/shard_map/ppermute | solution.py:317
